TPU v7x, 32 devices: a whole 2x2x4 slice. The times are simulated.
32 devices in a mesh: grow: 2 (over x), cy: 4 (over y, core), cz: 4 (over z).
Axes of the slice: x: 2, y: 2, z: 4, core: 2. Of those that a mesh axis runs over, the one named last changes fastest.
Arguments:
- labels: int32 [8, 512, 512], P('grow', 'cy', 'cz'), may hold values 0 or 1
- roughness: float32 [8, 512, 512], P('grow', 'cy', 'cz'), may hold values from 0 to 1
- potential: float32 [8, 512, 512], P('grow', 'cy', 'cz'), may hold values from 0 to 1
- displacement: float32 [3, 8, 512, 512], P(None, 'grow', 'cy', 'cz'), may hold values from -1.8 to 1.8
Outputs:
- phase_out: float32 [8, 512, 512], P('grow', 'cy', 'cz')
- potential_out: float32 [8, 512, 512], P('grow', 'cy', 'cz')
- displacement_out: float32 [3, 8, 512, 512], P(None, 'grow', 'cy', 'cz')
All inputs are finite; a program needn't handle non-finite values. No bound on the sum of `labels` on one device may be relied on, other than what follows from the above.
Results may differ from a plain program's by a relative error of at most 0.00002.
Values sent between devices are 32-bit elements; how exact they have to be, the bound alone decides.
No kernel may reach another device: no remote copies, remote signals or barrier semaphores. Data moves between devices by JAX's collectives and lax.ppermute only.
A program may use at most 64 MiB of HBM per device.

v0:
```python
import jax
import jax.numpy as jnp
from jax import lax
from jax.sharding import PartitionSpec as P

STEPS = 2
SWEEPS = 3


TAU_P = 0.15
TAU_U = 0.08
SHEAR = 1.0
LAME_FIRST = 1.5
STIFF = 6.5
EIGEN = 0.1
COND_EL = 0.1
COND_LI = 0.9
V_HIGH = 1.0
TIME_STEP = 0.05
REST = 0.5
OMEGA_THIRD = 0.1
RATE = 0.5


def extended(cells, sides, width, closed):
    for axis, dim in sides:
        count = lax.axis_size(axis)
        ends = count if closed else count - 1
        head = lax.slice_in_dim(cells, 0, width, axis=dim)
        tail = lax.slice_in_dim(cells, cells.shape[dim] - width, cells.shape[dim], axis=dim)
        cells = jnp.concatenate(
            [
                lax.ppermute(tail, axis, [(i, (i + 1) % count) for i in range(ends)]),
                cells,
                lax.ppermute(head, axis, [((i + 1) % count, i) for i in range(ends)]),
            ],
            axis=dim,
        )
    return cells


def from_behind(block, axis, distance):
    devices = range(lax.axis_size(axis))
    route = [(i - distance, i) for i in devices if i - distance in devices]
    return lax.ppermute(block, axis, route)


def unit(direction, sign):
    offsets = [0, 0, 0]
    offsets[direction] = sign
    return offsets


def offset(field, offsets):
    lead_dims = field.ndim - 3
    slices = [slice(None)] * lead_dims
    for direction in range(3):
        extent = field.shape[lead_dims + direction]
        slices.append(slice(1 + offsets[direction], extent - 1 + offsets[direction]))
    return field[tuple(slices)]


def centre(field):
    return offset(field, (0, 0, 0))


def laplace(field):
    total = -6.0 * centre(field)
    for direction in range(3):
        total = total + offset(field, unit(direction, 1)) + offset(field, unit(direction, -1))
    return total


def interp(phase):
    return phase * phase * (3.0 - 2.0 * phase)


def interp_slope(phase):
    return 6.0 * phase * (1.0 - phase)


def potential_sweep(potential_pad, conduct_pad):
    here = centre(potential_pad)
    conduct_here = centre(conduct_pad)
    flux = jnp.zeros_like(here)
    for direction in range(3):
        for sign in (1, -1):
            moved = unit(direction, sign)
            flux = flux + 0.5 * (offset(conduct_pad, moved) + conduct_here) * (
                offset(potential_pad, moved) - here
            )
    return here + TAU_P * flux


def cross_term(field, first, second):
    total = jnp.zeros_like(centre(field))
    for sign_first in (1, -1):
        for sign_second in (1, -1):
            offsets = [0, 0, 0]
            offsets[first] = sign_first
            offsets[second] = sign_second
            total = total + sign_first * sign_second * offset(field, offsets)
    return 0.25 * total


def elastic_sweep(disp_pad, interp_pad):
    updated = []
    for component in range(3):
        own = disp_pad[component]
        grad_div = (
            offset(own, unit(component, 1)) - 2.0 * centre(own) + offset(own, unit(component, -1))
        )
        for other in range(3):
            if other != component:
                grad_div = grad_div + cross_term(disp_pad[other], component, other)
        slope = 0.5 * (
            offset(interp_pad, unit(component, 1)) - offset(interp_pad, unit(component, -1))
        )
        force = SHEAR * laplace(own) + (LAME_FIRST + SHEAR) * grad_div - STIFF * EIGEN * slope
        updated.append(centre(own) + TAU_U * force)
    return jnp.stack(updated)


def divergence(disp_pad):
    total = jnp.zeros_like(centre(disp_pad[0]))
    for component in range(3):
        total = total + 0.5 * (
            offset(disp_pad[component], unit(component, 1))
            - offset(disp_pad[component], unit(component, -1))
        )
    return total


def phase_update(phase_pad, potential, div_disp):
    phase = centre(phase_pad)
    trace = STIFF * (div_disp - 3.0 * EIGEN * interp(phase))
    over = potential - REST + OMEGA_THIRD * trace
    drive = jnp.exp(over) - jnp.exp(-over)
    change = (
        laplace(phase_pad)
        - 2.0 * phase * (1.0 - phase) * (1.0 - 2.0 * phase)
        - RATE * interp_slope(phase) * drive
    )
    return phase + TIME_STEP * change


def pin_ends(field, width, slab, low, high):
    if width == 0:
        return field
    lead_dims = field.ndim - 3
    planes = field.shape[lead_dims]
    first = lax.axis_index("grow") * slab - width
    position = first + lax.broadcasted_iota(jnp.int32, (planes, 1, 1), 0)
    limit = slab * lax.axis_size("grow")
    result = jnp.where(position < 0, low, field)
    return jnp.where(position >= limit, high, result)


def column_values(values):
    return jnp.array(values, jnp.float32).reshape(len(values), 1, 1, 1)


def strip(field, count):
    for repeat in range(count):
        field = centre(field)
    return field


def shards(labels, roughness, potential, displacement):
    slab = labels.shape[0]
    rim = SWEEPS + 1
    mark = labels.astype(jnp.float32)
    phase = mark * (1.0 - 0.3 * roughness) + (1.0 - mark) * (0.3 * roughness)
    low_five = column_values([1.0, 0.0, 0.0, 0.0, 0.0])
    high_five = column_values([0.0, V_HIGH, 0.0, 0.0, 0.0])
    for step_index in range(STEPS):
        packed = jnp.concatenate([phase[None], potential[None], displacement], axis=0)
        packed = extended(packed, (("grow", 1),), SWEEPS + 1, False)
        packed = pin_ends(packed, SWEEPS + 1, slab, low_five, high_five)
        packed = extended(packed, (("cy", 2), ("cz", 3)), SWEEPS + 1, True)
        phase_pad = packed[0]
        interp_pad = interp(phase_pad)
        conduct_pad = COND_EL + COND_LI * interp_pad
        pot_pad = strip(packed[1], 1)
        conduct_now = centre(conduct_pad)
        for repeat in range(SWEEPS):
            pot_pad = pin_ends(
                potential_sweep(pot_pad, conduct_now), SWEEPS - 1 - repeat, slab, 0.0, V_HIGH
            )
            if repeat + 1 < SWEEPS:
                conduct_now = centre(conduct_now)
        potential = pot_pad
        disp_pad = packed[2:]
        interp_now = interp_pad
        for repeat in range(SWEEPS):
            disp_pad = pin_ends(
                elastic_sweep(disp_pad, interp_now), SWEEPS - repeat, slab, 0.0, 0.0
            )
            if repeat + 1 < SWEEPS:
                interp_now = centre(interp_now)
        div_disp = divergence(disp_pad)
        displacement = centre(disp_pad)
        phase = phase_update(strip(phase_pad, rim - 1), potential, div_disp)
    stacked = jnp.concatenate([phase[None], potential[None], displacement], axis=0)
    arrived = from_behind(stacked, "grow", -1)
    fresh = jnp.array([0.0, V_HIGH, 0.0, 0.0, 0.0], jnp.float32).reshape(5, 1, 1, 1)
    is_last = lax.axis_index("grow") == lax.axis_size("grow") - 1
    arrived = jnp.where(is_last, fresh, arrived)
    return (arrived[0], arrived[1], arrived[2:])


def solution(mesh):
    placed = (
        P("grow", "cy", "cz"),
        P("grow", "cy", "cz"),
        P("grow", "cy", "cz"),
        P(None, "grow", "cy", "cz"),
    )
    return jax.shard_map(
        shards,
        mesh=mesh,
        in_specs=placed,
        out_specs=(P("grow", "cy", "cz"), P("grow", "cy", "cz"), P(None, "grow", "cy", "cz")),
        check_vma=False,
    )
```

profile of v0, /device:TPU:0, one launch (start us, length us, event | category | flops | bytes accessed | tf_op | source)
XLA Modules:
  0.0 300.5 jit_solution(10371739561224224435)
XLA Ops:
  3.1 5.9 %collective-permute-start = (f32[5,4,128,128]{3,2,1,0:T(8,128)S(1)}, f32[5,4,128,128]{3,2,1,0:T(8,128)}, u32[]{:S(2)}, u32[]{:S(2)}) collective-permute-start(f32[5,4,128,128]{3,2,1,0:T(8,128)S(1)} %pad_maximum_fusion.4), channel_id=1, source_target_pairs={{0,16},{1,17},{2,18},{3,19},{4,20},{5,21},{6,22},{7,23},{8,24},{9,... | collective-permute-start | bytes 3932168 | tf_op jit(solution)/shard_map/ppermute | solution.py:33
  10.4 25.6 %collective-permute-done = f32[5,4,128,128]{3,2,1,0:T(8,128)} collective-permute-done((f32[5,4,128,128]{3,2,1,0:T(8,128)S(1)}, f32[5,4,128,128]{3,2,1,0:T(8,128)}, u32[]{:S(2)}, u32[]{:S(2)}) %collective-permute-start) | collective-permute-done | bytes 1310752 | tf_op jit(solution)/shard_map/ppermute | solution.py:33
  36.0 5.3 %collective-permute-done.1 = f32[5,4,128,128]{3,2,1,0:T(8,128)} collective-permute-done((f32[5,4,128,128]{3,2,1,0:T(8,128)S(1)}, f32[5,4,128,128]{3,2,1,0:T(8,128)}, u32[]{:S(2)}, u32[]{:S(2)}) %collective-permute-start.1) | collective-permute-done | bytes 1310752 | tf_op jit(solution)/shard_map/ppermute | solution.py:35
  52.5 4.6 %fusion.457 = (f32[5,12,136,4]{3,2,1,0:T(8,128)}, f32[5,12,136,4]{3,2,1,0:T(8,128)}) fusion(f32[5,12,136,128]{3,2,1,0:T(8,128)S(1)} %pad_maximum_fusion.2), kind=kLoop, calls=%fused_computation.800 | loop fusion | bytes 522240 | tf_op jit(solution)/shard_map/slice | solution.py:30
  79.8 8.0 %pad_maximum_fusion = f32[5,12,136,136]{3,2,1,0:T(8,128)S(1)} fusion(f32[5,12,136,4]{3,2,1,0:T(8,128)} %copy.20, f32[5,12,4,128]{3,2,1,0:T(4,128)S(1)} %collective-permute-done.3, f32[5,12,128,128]{3,2,1,0:T(8,128)} %copy-done, f32[5,12,4,128]{3,2,1,0:T(4,128)S(1)} %collective-permute-done.2, f32[5,12,136,4]{3,2,1,0:T(8,128)} %copy.19), kind=kLoop, calls=%fused_computation | loop fusion | flops 4439040 | bytes 8878080 | tf_op jit(solution)/shard_map/concatenate | solution.py:31
  89.0 5.7 %fusion.95 = f32[1,10,134,134]{3,2,1,0:T(8,128)S(1)} fusion(f32[12,136,136]{2,1,0:T(8,128)S(1)} %get-tuple-element.18, f32[12,136,136]{2,1,0:T(8,128)S(1)} %get-tuple-element.20, f32[12,136,136]{2,1,0:T(8,128)S(1)} %get-tuple-element.21, f32[12,136,136]{2,1,0:T(8,128)S(1)} %get-tuple-element.22), kind=kLoop, calls=%fused_computation.183 | loop fusion | flops 5566360 | bytes 12928320 | tf_op jit(solution)/shard_map/stack | solution.py:121
  94.7 5.5 %fusion.78 = f32[1,10,134,134]{3,2,1,0:T(8,128)S(1)} fusion(f32[12,136,136]{2,1,0:T(8,128)S(1)} %get-tuple-element.18, f32[12,136,136]{2,1,0:T(8,128)S(1)} %get-tuple-element.20, f32[12,136,136]{2,1,0:T(8,128)S(1)} %get-tuple-element.22, f32[12,136,136]{2,1,0:T(8,128)S(1)} %get-tuple-element.21), kind=kLoop, calls=%fused_computation.155 | loop fusion | flops 5566360 | bytes 12928320 | tf_op jit(solution)/shard_map/stack | solution.py:121
  100.3 5.2 %fusion.61 = f32[1,10,134,134]{3,2,1,0:T(8,128)S(1)} fusion(f32[12,136,136]{2,1,0:T(8,128)S(1)} %get-tuple-element.18, f32[12,136,136]{2,1,0:T(8,128)S(1)} %get-tuple-element.21, f32[12,136,136]{2,1,0:T(8,128)S(1)} %get-tuple-element.22, f32[12,136,136]{2,1,0:T(8,128)S(1)} %get-tuple-element.20), kind=kLoop, calls=%fused_computation.127 | loop fusion | flops 5566360 | bytes 12928320 | tf_op jit(solution)/shard_map/stack | solution.py:121
  106.3 4.6 %fusion.214 = f32[1,8,132,132]{3,2,1,0:T(8,128)S(1)} fusion(f32[12,136,136]{2,1,0:T(8,128)S(1)} %get-tuple-element.18, f32[10,134,134]{2,1,0:T(8,128)S(1)} %get-tuple-element.29, f32[10,134,134]{2,1,0:T(8,128)S(1)} %get-tuple-element.30, f32[10,134,134]{2,1,0:T(8,128)S(1)} %get-tuple-element.31), kind=kLoop, calls=%fused_computation.389 | loop fusion | flops 4321152 | bytes 10036224 | tf_op jit(solution)/shard_map/stack | solution.py:121
  110.9 4.4 %fusion.197 = f32[1,8,132,132]{3,2,1,0:T(8,128)S(1)} fusion(f32[12,136,136]{2,1,0:T(8,128)S(1)} %get-tuple-element.18, f32[10,134,134]{2,1,0:T(8,128)S(1)} %get-tuple-element.29, f32[10,134,134]{2,1,0:T(8,128)S(1)} %get-tuple-element.31, f32[10,134,134]{2,1,0:T(8,128)S(1)} %get-tuple-element.30), kind=kLoop, calls=%fused_computation.361 | loop fusion | flops 4321152 | bytes 10036224 | tf_op jit(solution)/shard_map/stack | solution.py:121
  115.3 4.0 %fusion.180 = f32[1,8,132,132]{3,2,1,0:T(8,128)S(1)} fusion(f32[12,136,136]{2,1,0:T(8,128)S(1)} %get-tuple-element.18, f32[10,134,134]{2,1,0:T(8,128)S(1)} %get-tuple-element.30, f32[10,134,134]{2,1,0:T(8,128)S(1)} %get-tuple-element.31, f32[10,134,134]{2,1,0:T(8,128)S(1)} %get-tuple-element.29), kind=kLoop, calls=%fused_computation.333 | loop fusion | flops 4321152 | bytes 10036224 | tf_op jit(solution)/shard_map/stack | solution.py:121
  129.9 4.5 %fusion.230 = f32[8,132,132]{2,1,0:T(8,128)S(1)} fusion(f32[12,136,136]{2,1,0:T(8,128)S(1)} %get-tuple-element.19, f32[12,136,136]{2,1,0:T(8,128)S(1)} %get-tuple-element.17, pred[8]{0:T(512)(128)(4,1)S(1)} %get-tuple-element.56, pred[8]{0:T(512)(128)(4,1)S(1)} %get-tuple-element.57), kind=kLoop, calls=%fused_computation.416 | loop fusion | flops 4599936 | bytes 8363536 | tf_op jit(solution)/shard_map/jit(_where)/select_n | solution.py:156
  141.9 27.1 %collective-permute-done.6 = f32[5,4,128,128]{3,2,1,0:T(8,128)S(1)} collective-permute-done((f32[5,4,128,128]{3,2,1,0:T(8,128)S(1)}, f32[5,4,128,128]{3,2,1,0:T(8,128)S(1)}, u32[]{:S(2)}, u32[]{:S(2)}) %collective-permute-start.6) | collective-permute-done | bytes 1310752 | tf_op jit(solution)/shard_map/ppermute | solution.py:33
  169.1 4.2 %collective-permute-done.7 = f32[5,4,128,128]{3,2,1,0:T(8,128)S(1)} collective-permute-done((f32[5,4,128,128]{3,2,1,0:T(8,128)S(1)}, f32[5,4,128,128]{3,2,1,0:T(8,128)S(1)}, u32[]{:S(2)}, u32[]{:S(2)}) %collective-permute-start.7) | collective-permute-done | bytes 1310752 | tf_op jit(solution)/shard_map/ppermute | solution.py:35
  179.2 4.6 %fusion.456 = (f32[5,12,136,4]{3,2,1,0:T(8,128)}, f32[5,12,136,4]{3,2,1,0:T(8,128)}) fusion(f32[5,12,136,128]{3,2,1,0:T(8,128)S(1)} %pad_maximum_fusion.3), kind=kLoop, calls=%fused_computation.799 | loop fusion | bytes 522240 | tf_op jit(solution)/shard_map/slice | solution.py:30
  206.4 8.0 %pad_maximum_fusion.1 = f32[5,12,136,136]{3,2,1,0:T(8,128)S(1)} fusion(f32[5,12,136,4]{3,2,1,0:T(8,128)} %copy.24, f32[5,12,4,128]{3,2,1,0:T(4,128)S(1)} %collective-permute-done.9, f32[5,12,128,128]{3,2,1,0:T(8,128)} %copy-done.1, f32[5,12,4,128]{3,2,1,0:T(4,128)S(1)} %collective-permute-done.8, f32[5,12,136,4]{3,2,1,0:T(8,128)} %copy.23), kind=kLoop, calls=%fused_computation.1 | loop fusion | flops 4439040 | bytes 8878080 | tf_op jit(solution)/shard_map/concatenate | solution.py:31
  215.6 5.7 %fusion.46 = f32[1,10,134,134]{3,2,1,0:T(8,128)S(1)} fusion(f32[12,136,136]{2,1,0:T(8,128)S(1)} %get-tuple-element.11, f32[12,136,136]{2,1,0:T(8,128)S(1)} %get-tuple-element.13, f32[12,136,136]{2,1,0:T(8,128)S(1)} %get-tuple-element.14, f32[12,136,136]{2,1,0:T(8,128)S(1)} %get-tuple-element.15), kind=kLoop, calls=%fused_computation.98 | loop fusion | flops 5566360 | bytes 12928320 | tf_op jit(solution)/shard_map/stack | solution.py:121
  221.4 5.5 %fusion.29 = f32[1,10,134,134]{3,2,1,0:T(8,128)S(1)} fusion(f32[12,136,136]{2,1,0:T(8,128)S(1)} %get-tuple-element.11, f32[12,136,136]{2,1,0:T(8,128)S(1)} %get-tuple-element.13, f32[12,136,136]{2,1,0:T(8,128)S(1)} %get-tuple-element.15, f32[12,136,136]{2,1,0:T(8,128)S(1)} %get-tuple-element.14), kind=kLoop, calls=%fused_computation.70 | loop fusion | flops 5566360 | bytes 12928320 | tf_op jit(solution)/shard_map/stack | solution.py:121
  226.9 4.8 %fusion.12 = f32[1,10,134,134]{3,2,1,0:T(8,128)S(1)} fusion(f32[12,136,136]{2,1,0:T(8,128)S(1)} %get-tuple-element.11, f32[12,136,136]{2,1,0:T(8,128)S(1)} %get-tuple-element.14, f32[12,136,136]{2,1,0:T(8,128)S(1)} %get-tuple-element.15, f32[12,136,136]{2,1,0:T(8,128)S(1)} %get-tuple-element.13), kind=kLoop, calls=%fused_computation.42 | loop fusion | flops 5566360 | bytes 12928320 | tf_op jit(solution)/shard_map/stack | solution.py:121
  232.6 4.6 %fusion.144 = f32[1,8,132,132]{3,2,1,0:T(8,128)S(1)} fusion(f32[12,136,136]{2,1,0:T(8,128)S(1)} %get-tuple-element.11, f32[10,134,134]{2,1,0:T(8,128)S(1)} %get-tuple-element.24, f32[10,134,134]{2,1,0:T(8,128)S(1)} %get-tuple-element.25, f32[10,134,134]{2,1,0:T(8,128)S(1)} %get-tuple-element.26), kind=kLoop, calls=%fused_computation.271 | loop fusion | flops 4321152 | bytes 10036224 | tf_op jit(solution)/shard_map/stack | solution.py:121
  237.2 4.4 %fusion.127 = f32[1,8,132,132]{3,2,1,0:T(8,128)S(1)} fusion(f32[12,136,136]{2,1,0:T(8,128)S(1)} %get-tuple-element.11, f32[10,134,134]{2,1,0:T(8,128)S(1)} %get-tuple-element.24, f32[10,134,134]{2,1,0:T(8,128)S(1)} %get-tuple-element.26, f32[10,134,134]{2,1,0:T(8,128)S(1)} %get-tuple-element.25), kind=kLoop, calls=%fused_computation.243 | loop fusion | flops 4321152 | bytes 10036224 | tf_op jit(solution)/shard_map/stack | solution.py:121
  241.5 4.1 %fusion.110 = f32[1,8,132,132]{3,2,1,0:T(8,128)S(1)} fusion(f32[12,136,136]{2,1,0:T(8,128)S(1)} %get-tuple-element.11, f32[10,134,134]{2,1,0:T(8,128)S(1)} %get-tuple-element.25, f32[10,134,134]{2,1,0:T(8,128)S(1)} %get-tuple-element.26, f32[10,134,134]{2,1,0:T(8,128)S(1)} %get-tuple-element.24), kind=kLoop, calls=%fused_computation.215 | loop fusion | flops 4321152 | bytes 10036224 | tf_op jit(solution)/shard_map/stack | solution.py:121
  256.2 4.5 %fusion.160 = f32[8,132,132]{2,1,0:T(8,128)S(1)} fusion(f32[12,136,136]{2,1,0:T(8,128)S(1)} %get-tuple-element.12, f32[12,136,136]{2,1,0:T(8,128)S(1)} %get-tuple-element.10, pred[8]{0:T(512)(128)(4,1)S(1)} %get-tuple-element.56, pred[8]{0:T(512)(128)(4,1)S(1)} %get-tuple-element.57), kind=kLoop, calls=%fused_computation.298 | loop fusion | flops 4599936 | bytes 8363536 | tf_op jit(solution)/shard_map/jit(_where)/select_n | solution.py:156
  266.8 31.4 %collective-permute-done.12 = f32[5,4,128,128]{3,2,1,0:T(8,128)S(1)} collective-permute-done((f32[5,4,128,128]{3,2,1,0:T(8,128)S(1)}, f32[5,4,128,128]{3,2,1,0:T(8,128)S(1)}, u32[]{:S(2)}, u32[]{:S(2)}) %collective-permute-start.12) | collective-permute-done | bytes 1310752 | tf_op jit(solution)/shard_map/ppermute | solution.py:45
  (85 shorter events, 106.8 us)
Async XLA Ops:
  1.7 39.6 %copy-start.2 = (f32[3,4,128,128]{3,2,1,0:T(8,128)S(1)}, f32[3,4,128,128]{3,2,1,0:T(8,128)}, u32[]{:S(2)}) copy-start(f32[3,4,128,128]{3,2,1,0:T(8,128)} %param.10) | copy-start | bytes 2359300
  1.7 39.6 %copy-start.3 = (f32[4,128,128]{2,1,0:T(8,128)S(1)}, f32[4,128,128]{2,1,0:T(8,128)}, u32[]{:S(2)}) copy-start(f32[4,128,128]{2,1,0:T(8,128)} %param.9) | copy-start | bytes 786436
  1.8 39.6 %copy-start.4 = (f32[5]{0:T(128)S(1)}, f32[5]{0:T(128)}, u32[]{:S(2)}) copy-start(f32[5]{0:T(128)} %constant.119.clone) | copy-start | bytes 64
  1.8 39.5 %copy-start.5 = (f32[5]{0:T(128)S(1)}, f32[5]{0:T(128)}, u32[]{:S(2)}) copy-start(f32[5]{0:T(128)} %constant.118.clone) | copy-start | bytes 64
  3.1 32.9 %collective-permute-start = (f32[5,4,128,128]{3,2,1,0:T(8,128)S(1)}, f32[5,4,128,128]{3,2,1,0:T(8,128)}, u32[]{:S(2)}, u32[]{:S(2)}) collective-permute-start(f32[5,4,128,128]{3,2,1,0:T(8,128)S(1)} %pad_maximum_fusion.4), channel_id=1, source_target_pairs={{0,16},{1,17},{2,18},{3,19},{4,20},{5,21},{6,22},{7,23},{8,24},{9,... | collective-permute-start | bytes 3932168 | tf_op jit(solution)/shard_map/ppermute | solution.py:33
  9.1 32.2 %collective-permute-start.1 = (f32[5,4,128,128]{3,2,1,0:T(8,128)S(1)}, f32[5,4,128,128]{3,2,1,0:T(8,128)}, u32[]{:S(2)}, u32[]{:S(2)}) collective-permute-start(f32[5,4,128,128]{3,2,1,0:T(8,128)S(1)} %pad_maximum_fusion.4), channel_id=1, source_target_pairs={{16,0},{17,1},{18,2},{19,3},{20,4},{21,5},{22,6},{23,7},{24,8},{25... | collective-permute-start | bytes 3932168 | tf_op jit(solution)/shard_map/ppermute | solution.py:35
  43.4 1.9 copy-start
  45.3 4.4 %collective-permute-start.2 = (f32[5,12,4,128]{3,2,1,0:T(4,128)S(1)}, f32[5,12,4,128]{3,2,1,0:T(4,128)S(1)}, u32[]{:S(2)}, u32[]{:S(2)}) collective-permute-start(f32[5,12,4,128]{3,2,1,0:T(4,128)S(1)} %get-tuple-element.36), channel_id=1, source_target_pairs={{0,4},{4,8},{8,12},{12,0},{1,5},{5,9},{9,13},{13,1},{2,6},{6,10},{... | collective-permute-start | bytes 368648 | tf_op jit(solution)/shard_map/ppermute | solution.py:33
  45.4 4.6 %collective-permute-start.3 = (f32[5,12,4,128]{3,2,1,0:T(4,128)S(1)}, f32[5,12,4,128]{3,2,1,0:T(4,128)S(1)}, u32[]{:S(2)}, u32[]{:S(2)}) collective-permute-start(f32[5,12,4,128]{3,2,1,0:T(4,128)S(1)} %get-tuple-element.37), channel_id=1, source_target_pairs={{4,0},{8,4},{12,8},{0,12},{5,1},{9,5},{13,9},{1,13},{6,2},{10,6},{... | collective-permute-start | bytes 368648 | tf_op jit(solution)/shard_map/ppermute | solution.py:35
  61.0 10.5 %collective-permute-start.4 = (f32[5,12,136,4]{2,3,1,0:T(4,128)S(1)}, f32[5,12,136,4]{2,3,1,0:T(4,128)S(1)}, u32[]{:S(2)}, u32[]{:S(2)}) collective-permute-start(f32[5,12,136,4]{2,3,1,0:T(4,128)S(1)} %copy.17), channel_id=1, source_target_pairs={{0,1},{1,2},{2,3},{3,0},{4,5},{5,6},{6,7},{7,4},{8,9},{9,10},{10,1... | collective-permute-start | bytes 391688 | tf_op jit(solution)/shard_map/ppermute | solution.py:33
  66.5 10.5 %collective-permute-start.5 = (f32[5,12,136,4]{2,3,1,0:T(4,128)S(1)}, f32[5,12,136,4]{2,3,1,0:T(4,128)S(1)}, u32[]{:S(2)}, u32[]{:S(2)}) collective-permute-start(f32[5,12,136,4]{2,3,1,0:T(4,128)S(1)} %copy.18), channel_id=1, source_target_pairs={{1,0},{2,1},{3,2},{0,3},{5,4},{6,5},{7,6},{4,7},{9,8},{10,9},{11,1... | collective-permute-start | bytes 391688 | tf_op jit(solution)/shard_map/ppermute | solution.py:35
  139.2 29.9 %collective-permute-start.6 = (f32[5,4,128,128]{3,2,1,0:T(8,128)S(1)}, f32[5,4,128,128]{3,2,1,0:T(8,128)S(1)}, u32[]{:S(2)}, u32[]{:S(2)}) collective-permute-start(f32[5,4,128,128]{3,2,1,0:T(8,128)S(1)} %pad_maximum_fusion.5), channel_id=1, source_target_pairs={{0,16},{1,17},{2,18},{3,19},{4,20},{5,21},{6,22},{7,23},{8,24},{9,... | collective-permute-start | bytes 3932168 | tf_op jit(solution)/shard_map/ppermute | solution.py:33
  140.6 32.6 %collective-permute-start.7 = (f32[5,4,128,128]{3,2,1,0:T(8,128)S(1)}, f32[5,4,128,128]{3,2,1,0:T(8,128)S(1)}, u32[]{:S(2)}, u32[]{:S(2)}) collective-permute-start(f32[5,4,128,128]{3,2,1,0:T(8,128)S(1)} %pad_maximum_fusion.5), channel_id=1, source_target_pairs={{16,0},{17,1},{18,2},{19,3},{20,4},{21,5},{22,6},{23,7},{24,8},{25... | collective-permute-start | bytes 3932168 | tf_op jit(solution)/shard_map/ppermute | solution.py:35
  174.0 4.6 %copy-start.1 = (f32[5,12,128,128]{3,2,1,0:T(8,128)}, f32[5,12,128,128]{3,2,1,0:T(8,128)S(1)}, u32[]{:S(2)}) copy-start(f32[5,12,128,128]{3,2,1,0:T(8,128)S(1)} %fusion.3) | copy-start | bytes 11796484
  174.0 4.4 %collective-permute-start.8 = (f32[5,12,4,128]{3,2,1,0:T(4,128)S(1)}, f32[5,12,4,128]{3,2,1,0:T(4,128)S(1)}, u32[]{:S(2)}, u32[]{:S(2)}) collective-permute-start(f32[5,12,4,128]{3,2,1,0:T(4,128)S(1)} %get-tuple-element.34), channel_id=1, source_target_pairs={{0,4},{4,8},{8,12},{12,0},{1,5},{5,9},{9,13},{13,1},{2,6},{6,10},{... | collective-permute-start | bytes 368648 | tf_op jit(solution)/shard_map/ppermute | solution.py:33
  174.1 4.5 %collective-permute-start.9 = (f32[5,12,4,128]{3,2,1,0:T(4,128)S(1)}, f32[5,12,4,128]{3,2,1,0:T(4,128)S(1)}, u32[]{:S(2)}, u32[]{:S(2)}) collective-permute-start(f32[5,12,4,128]{3,2,1,0:T(4,128)S(1)} %get-tuple-element.35), channel_id=1, source_target_pairs={{4,0},{8,4},{12,8},{0,12},{5,1},{9,5},{13,9},{1,13},{6,2},{10,6},{... | collective-permute-start | bytes 368648 | tf_op jit(solution)/shard_map/ppermute | solution.py:35
  187.6 10.5 %collective-permute-start.10 = (f32[5,12,136,4]{2,3,1,0:T(4,128)S(1)}, f32[5,12,136,4]{2,3,1,0:T(4,128)S(1)}, u32[]{:S(2)}, u32[]{:S(2)}) collective-permute-start(f32[5,12,136,4]{2,3,1,0:T(4,128)S(1)} %copy.21), channel_id=1, source_target_pairs={{0,1},{1,2},{2,3},{3,0},{4,5},{5,6},{6,7},{7,4},{8,9},{9,10},{10,1... | collective-permute-start | bytes 391688 | tf_op jit(solution)/shard_map/ppermute | solution.py:33
  192.1 11.5 %collective-permute-start.11 = (f32[5,12,136,4]{2,3,1,0:T(4,128)S(1)}, f32[5,12,136,4]{2,3,1,0:T(4,128)S(1)}, u32[]{:S(2)}, u32[]{:S(2)}) collective-permute-start(f32[5,12,136,4]{2,3,1,0:T(4,128)S(1)} %copy.22), channel_id=1, source_target_pairs={{1,0},{2,1},{3,2},{0,3},{5,4},{6,5},{7,6},{4,7},{9,8},{10,9},{11,1... | collective-permute-start | bytes 391688 | tf_op jit(solution)/shard_map/ppermute | solution.py:35
  265.5 32.7 %collective-permute-start.12 = (f32[5,4,128,128]{3,2,1,0:T(8,128)S(1)}, f32[5,4,128,128]{3,2,1,0:T(8,128)S(1)}, u32[]{:S(2)}, u32[]{:S(2)}) collective-permute-start(f32[5,4,128,128]{3,2,1,0:T(8,128)S(1)} %pad_maximum_fusion.6), channel_id=1, source_target_pairs={{16,0},{17,1},{18,2},{19,3},{20,4},{21,5},{22,6},{23,7},{24,8},{25... | collective-permute-start | bytes 3932168 | tf_op jit(solution)/shard_map/ppermute | solution.py:45
where the time goes:
time: 304 us; the launch traced here: 300 us
  other arithmetic  123 us (40%)
  waiting for transfers between devices  109 us (36%)
  local copies, waits for them, and re-layouts  43.5 us (14%)
  starting transfers between devices  22.9 us (8%)
    another operation x18, other arithmetic, elastic_sweep(): return jnp.stack(updated)  76.9 us
    ppermute x6, waiting for transfers between devices, extended(): lax.ppermute(tail, axis, [(i, (i + 1) % count) for i in range(ends)])  63 us
    ppermute x1, waiting for transfers between devices, from_behind(): return lax.ppermute(block, axis, route)  31.4 us
    select_n x12, other arithmetic, pin_ends(): return jnp.where(position >= limit, high, result)  20.1 us
    concatenate x4, other arithmetic, extended(): jnp.concatenate([lax.ppermute(tail, axis, [(i, (i + 1) % count) for i in...  19.1 us
    slice x6, local copies, waits for them, and re-layouts, extended(): lax.slice_in_dim(cells, cells.shape[dim] - width, cells.shape[dim], axis=...  17 us
    ppermute x6, waiting for transfers between devices, extended(): lax.ppermute(head, axis, [((i + 1) % count, i) for i in range(ends)])  14.9 us
    ppermute x6, starting transfers between devices, extended(): lax.ppermute(head, axis, [((i + 1) % count, i) for i in range(ends)])  11.9 us
  transfers between devices with their start and end apart: 13, of which 13 were waited for; matrix products, arithmetic and copies ran while one was open for 5% of the time, Pallas kernels for 0%

commit v1 on v0

--- a/solution.py
+++ b/solution.py
@@ -1,6 +1,8 @@
 import jax
 import jax.numpy as jnp
 from jax import lax
+from jax.experimental import pallas as pl
+from jax.experimental.pallas import tpu as pltpu
 from jax.sharding import PartitionSpec as P
 
 STEPS = 2
@@ -209,6 +211,448 @@
     return (arrived[0], arrived[1], arrived[2:])
 
 
+REACH = STEPS * (SWEEPS + 1)
+TILE = 8
+LEAD = 2 * TILE
+FIELDS = 5
+
+
+def lanes(shape):
+    return lax.broadcasted_iota(jnp.int32, shape, 1)
+
+
+def from_lane(first):
+    lane = lanes((TILE, LANES))
+    return jnp.logical_and(lane >= first, lane < first + REACH)
+
+
+LANES = 128
+
+
+def turned(block, amount):
+    return pltpu.roll(block, lax.rem(amount + 2 * LANES, LANES), 1)
+
+
+def half_of(side):
+    low = lanes((TILE, LANES)) < LANES // 2
+    return jnp.logical_xor(low, side == 1)
+
+
+def field_reader(phase, potential, displacement):
+    def read(field, plane, row):
+        rows = pl.ds(row, TILE)
+        if field == 0:
+            return phase[plane, rows, :]
+        if field == 1:
+            return potential[plane, rows, :]
+        return displacement[field - 2, plane, rows, :]
+
+    return read
+
+
+def prepare_kernel(labels, roughness, potential, displacement, phase, halves, first, last):
+    slab, rows, _ = labels.shape
+    theirs = jnp.logical_not(half_of(lax.axis_index("grow")))
+    read = field_reader(phase, potential, displacement)
+    mid = rows // 2
+    for plane in range(slab):
+        for row in range(0, rows, TILE):
+            spot = (plane, pl.ds(row, TILE), slice(None))
+            mark = labels[spot].astype(jnp.float32)
+            rough = 0.3 * roughness[spot]
+            phase[spot] = mark * (1.0 - rough) + (1.0 - mark) * rough
+    for field in range(FIELDS):
+        for plane in range(slab):
+            which = field * slab + plane
+            for row in range(0, mid, TILE):
+                upper = read(field, plane, row)
+                lower = turned(read(field, plane, row + mid), LANES // 2)
+                halves[pl.ds(which * mid + row, TILE), :] = jnp.where(theirs, upper, lower)
+            first[pl.ds(which * TILE, TILE), :] = read(field, plane, 0)
+            last[pl.ds(which * TILE, TILE), :] = read(field, plane, rows - TILE)
+
+
+def strips(read, above, below, slab, rows, base, out, start):
+    count = FIELDS * slab
+    spare = []
+    for field in range(FIELDS):
+        for plane in range(slab):
+            which = field * slab + plane
+            packed = jnp.zeros((TILE, LANES), jnp.float32)
+            for group in range(rows // TILE):
+                block = turned(read(field, plane, group * TILE), group * REACH - base)
+                packed = jnp.where(from_lane(group * REACH), block, packed)
+            out[pl.ds(start + which * TILE, TILE), :] = packed
+            spot = pl.ds(which * TILE, TILE)
+            spare.append(above[spot, :])
+            spare.append(below[spot, :])
+    strips_of_rims(spare, base, out, start + count * TILE)
+
+
+def strips_of_rims(blocks, base, out, start):
+    per = LANES // REACH
+    for at in range(0, len(blocks), per):
+        packed = jnp.zeros((TILE, LANES), jnp.float32)
+        for group, block in enumerate(blocks[at : at + per]):
+            packed = jnp.where(
+                from_lane(group * REACH), turned(block, group * REACH - base), packed
+            )
+        out[pl.ds(start + at // per * TILE, TILE), :] = packed
+
+
+def rim_rows(slab):
+    count = FIELDS * slab
+    return (count + -(-2 * count * REACH // LANES)) * TILE
+
+
+def rims_kernel(phase, potential, displacement, above, below, across, same, other):
+    slab, rows, _ = phase.shape
+    side = lax.axis_index("grow")
+    theirs = jnp.logical_not(half_of(side))
+    read = field_reader(phase, potential, displacement)
+    count = FIELDS * slab
+    for which in range(count):
+        spot = pl.ds(which * TILE, TILE)
+        across[spot, :] = jnp.where(theirs, above[spot, :], turned(below[spot, :], LANES // 2))
+    inner = LANES // 2 - REACH + REACH * side
+    outer = LANES - REACH
+    strips(read, above, below, slab, rows, inner, across, count * TILE)
+    strips(read, above, below, slab, rows, outer * (1 - side), same, 0)
+    strips(read, above, below, slab, rows, outer * side, other, 0)
+
+
+def conduct_of(step):
+    return COND_EL + COND_LI * step
+
+
+def steps_kernel(
+    phase_in, potential_in, displacement_in, above, below, halves, across, same, other,
+    result, message, phase, pots, disps, slopes, cond_x, cond_y, cond_z,
+):
+    slab, rows, _ = phase_in.shape
+    planes = 2 * slab
+    side = lax.axis_index("grow")
+    mine = half_of(side)
+    mid = rows // 2
+    count = FIELDS * slab
+    read = field_reader(phase_in, potential_in, displacement_in)
+    groups = rows // TILE
+    per = LANES // REACH
+    inner = LANES // 2 - REACH * side
+    outer = (LANES - REACH) * (1 - side)
+    in_inner, in_outer = from_lane(inner), from_lane(outer)
+
+    def put(field, plane, row, value):
+        spot = (plane, pl.ds(LEAD + row, TILE), slice(None))
+        if field == 0:
+            phase[spot] = value
+        elif field == 1:
+            pots[(0,) + spot] = value
+        else:
+            disps[(0, field - 2) + spot] = value
+
+    for field in range(FIELDS):
+        for plane in range(slab):
+            which = field * slab + plane
+            own, far = side * slab + plane, (1 - side) * slab + plane
+            spot = pl.ds(which * TILE, TILE)
+            from_same, from_other = same[spot, :], other[spot, :]
+            strip = across[pl.ds((count + which) * TILE, TILE), :]
+            for group in range(groups):
+                row = group * TILE
+                near = read(field, plane, row)
+                back = outer - group * REACH
+                put(field, own, row, jnp.where(in_outer, turned(from_same, back), near))
+                block = halves[pl.ds(which * mid + row % mid, TILE), :]
+                if row >= mid:
+                    block = turned(block, LANES // 2)
+                block = jnp.where(in_inner, turned(strip, inner - group * REACH), block)
+                put(field, far, row, jnp.where(in_outer, turned(from_other, back), block))
+            rim = across[spot, :]
+            for end, row in ((0, -TILE), (1, rows)):
+                at, group = divmod(2 * which + end, per)
+                extra = pl.ds((count + at) * TILE, TILE)
+                back = outer - group * REACH
+                near = (below if end else above)[spot, :]
+                put(field, own, row, jnp.where(in_outer, turned(same[extra, :], back), near))
+                block = turned(rim, LANES // 2) if end else rim
+                strip = across[pl.ds((2 * count + at) * TILE, TILE), :]
+                block = jnp.where(in_inner, turned(strip, inner - group * REACH), block)
+                put(field, far, row, jnp.where(in_outer, turned(other[extra, :], back), block))
+
+    def over_rows(body, rim=1):
+        def one(block, carry):
+            body(pl.multiple_of(block * TILE, TILE))
+            return carry
+
+        lax.fori_loop(LEAD // TILE - rim, (LEAD + rows) // TILE + rim, one, 0)
+
+    def at(ref, row, shift, *lead):
+        return ref[lead + (pl.ds(row + shift, TILE), slice(None))]
+
+    def up(block):
+        return pltpu.roll(block, LANES - 1, 1)
+
+    def down(block):
+        return pltpu.roll(block, 1, 1)
+
+    def set_conduct(row):
+        face = 0.5 * TAU_P
+        before = conduct_of(1.0)
+        for plane in range(planes):
+            step = interp(at(phase, row, 0, plane))
+            here = conduct_of(step)
+            slopes[plane, pl.ds(row, TILE), :] = (0.5 * TAU_U * STIFF * EIGEN) * step
+            cond_x[plane, pl.ds(row, TILE), :] = face * (before + here)
+            cond_y[plane, pl.ds(row, TILE), :] = face * (
+                here + conduct_of(interp(at(phase, row, 1, plane)))
+            )
+            cond_z[plane, pl.ds(row, TILE), :] = face * (here + up(here))
+            before = here
+        cond_x[planes, pl.ds(row, TILE), :] = face * (before + conduct_of(0.0))
+
+    def potential_pass(old, new, low):
+        def body(row):
+            here = at(pots, row, 0, old, low)
+            before = at(pots, row, 0, old, low - 1) if low else 0.0
+            entering = at(cond_x, row, 0, low) * (here - before)
+            for plane in range(low, planes):
+                after = at(pots, row, 0, old, plane + 1) if plane + 1 < planes else V_HIGH
+                leaving = at(cond_x, row, 0, plane + 1) * (after - here)
+                along_y = at(cond_y, row, 0, plane) * (at(pots, row, 1, old, plane) - here)
+                along_y -= at(cond_y, row, -1, plane) * (here - at(pots, row, -1, old, plane))
+                along_z = at(cond_z, row, 0, plane) * (up(here) - here)
+                along_z -= down(along_z)
+                pots[new, plane, pl.ds(row, TILE), :] = here + (
+                    (leaving - entering) + along_y + along_z
+                )
+                here, entering = after, leaving
+
+        return body
+
+    grad = LAME_FIRST + SHEAR
+    cross = 0.25 * TAU_U * grad
+    side_on = TAU_U * SHEAR
+    head_on = TAU_U * (SHEAR + grad)
+    keep = 1.0 - TAU_U * (6.0 * SHEAR + 2.0 * grad)
+
+    def elastic_pass(old, new, low):
+        def body(row):
+            def load(plane):
+                if plane < 0 or plane >= planes:
+                    edge = 0.5 * TAU_U * STIFF * EIGEN if plane < 0 else 0.0
+                    return (0.0, 0.0, 0.0, 0.0, -edge)
+                a, b, c = (at(disps, row, 0, old, part, plane) for part in range(3))
+                diff = at(disps, row, 1, old, 0, plane) - at(disps, row, -1, old, 0, plane)
+                b_up, b_down = at(disps, row, 1, old, 1, plane), at(disps, row, -1, old, 1, plane)
+                slope = cross * (b_up - b_down) - at(slopes, row, 0, plane)
+                return (a, b, c, diff, slope)
+
+            before, here = load(low - 1), load(low)
+            for plane in range(low, planes):
+                after = load(plane + 1)
+                a, b, c, _, slope = here
+                sum_x = [after[part] + before[part] for part in range(3)]
+                ends = [
+                    [at(disps, row, shift, old, part, plane) for shift in (1, -1)]
+                    for part in range(3)
+                ]
+                sum_y = [pair[0] + pair[1] for pair in ends]
+                lift = cross * (after[2] - before[2])
+                mid_a = side_on * a
+                new_a = (
+                    keep * a
+                    + head_on * sum_x[0]
+                    + side_on * sum_y[0]
+                    + (up(mid_a + lift) + down(mid_a - lift))
+                    + (after[4] - before[4])
+                )
+                lift = cross * (ends[2][0] - ends[2][1])
+                mid_b = side_on * b
+                new_b = (
+                    keep * b
+                    + head_on * sum_y[1]
+                    + side_on * sum_x[1]
+                    + (up(mid_b + lift) + down(mid_b - lift))
+                    + cross * (after[3] - before[3])
+                    - (at(slopes, row, 1, plane) - at(slopes, row, -1, plane))
+                )
+                lift = cross * (after[0] - before[0]) + slope
+                mid_c = head_on * c
+                new_c = (
+                    keep * c
+                    + side_on * (sum_x[2] + sum_y[2])
+                    + (up(mid_c + lift) + down(mid_c - lift))
+                )
+                spot = (plane, pl.ds(row, TILE), slice(None))
+                disps[(new, 0) + spot] = new_a
+                disps[(new, 1) + spot] = new_b
+                disps[(new, 2) + spot] = new_c
+                before, here = here, after
+
+        return body
+
+    def phase_pass(pot_at, disp_at, low, store):
+        def body(row):
+            def load(plane):
+                if plane < 0 or plane >= planes:
+                    return (1.0 if plane < 0 else 0.0, 0.0)
+                return (at(phase, row, 0, plane), at(disps, row, 0, disp_at, 0, plane))
+
+            before, here = load(low - 1), load(low)
+            for plane in range(low, planes):
+                after = load(plane + 1)
+                p = here[0]
+                c = at(disps, row, 0, disp_at, 2, plane)
+                div = (
+                    (after[1] - before[1])
+                    + (at(disps, row, 1, disp_at, 1, plane) - at(disps, row, -1, disp_at, 1, plane))
+                    + (up(c) - down(c))
+                )
+                over = (
+                    (at(pots, row, 0, pot_at, plane) - REST)
+                    + (0.5 * OMEGA_THIRD * STIFF) * div
+                    - (OMEGA_THIRD * STIFF * 3.0 * EIGEN) * interp(p)
+                )
+                drive = jnp.exp(over) - jnp.exp(-over)
+                lap = (
+                    (before[0] + after[0])
+                    + (at(phase, row, 1, plane) + at(phase, row, -1, plane))
+                    + (up(p) + down(p))
+                    - 6.0 * p
+                )
+                well = p * (1.0 - p)
+                change = lap - well * (2.0 * (1.0 - 2.0 * p) + (6.0 * RATE) * drive)
+                store(plane, row, p + TIME_STEP * change)
+                before, here = here, after
+
+        return body
+
+    def store_new(plane, row, value):
+        pots[2, plane, pl.ds(row, TILE), :] = value
+
+    def store_result(plane, row, value):
+        to = (plane - slab, pl.ds(pl.multiple_of(row - LEAD, TILE), TILE), slice(None))
+        result[(0,) + to] = value
+        result[(1,) + to] = at(pots, row, 0, 0, plane)
+        for part in range(3):
+            result[(2 + part,) + to] = at(disps, row, 0, 0, part, plane)
+
+    now = 0
+    for step in range(STEPS):
+        last = step == STEPS - 1
+        over_rows(set_conduct)
+        for sweep in range(SWEEPS):
+            low = max(0, slab - (SWEEPS - 1 - sweep)) if last else 0
+            over_rows(potential_pass(now, 1 - now, low))
+            low = max(0, slab - (SWEEPS - sweep)) if last else 0
+            over_rows(elastic_pass(now, 1 - now, low))
+            now = 1 - now
+        if last:
+            over_rows(phase_pass(now, now, slab, store_result), 0)
+        else:
+            over_rows(phase_pass(now, now, 0, store_new))
+
+            def copy(row):
+                for plane in range(planes):
+                    phase[plane, pl.ds(row, TILE), :] = at(pots, row, 0, 2, plane)
+
+            over_rows(copy)
+    for field in range(FIELDS):
+        for plane in range(slab):
+            for row in range(0, mid, TILE):
+                upper = result[field, plane, pl.ds(row, TILE), :]
+                lower = turned(result[field, plane, pl.ds(row + mid, TILE), :], LANES // 2)
+                to = pl.ds((field * slab + plane) * mid + row, TILE)
+                message[to, :] = jnp.where(mine, upper, lower)
+
+
+def finish_kernel(result, message, phase, potential, displacement):
+    _, slab, rows, _ = result.shape
+    side = lax.axis_index("grow")
+    mine = half_of(side)
+    fresh = side == lax.axis_size("grow") - 1
+    mid = rows // 2
+    for field in range(FIELDS):
+        out = (phase, potential, displacement, displacement, displacement)[field]
+        for plane in range(slab):
+            for row in range(0, mid, TILE):
+                block = message[pl.ds((field * slab + plane) * mid + row, TILE), :]
+                for place, piece in ((row, block), (row + mid, turned(block, LANES // 2))):
+                    spot = (plane, pl.ds(place, TILE), slice(None))
+                    whole = jnp.where(mine, result[(field,) + spot], piece)
+                    whole = jnp.where(fresh, V_HIGH if field == 1 else 0.0, whole)
+                    out[spot if field < 2 else (field - 2,) + spot] = whole
+
+
+def call(kernel, outs, scratch=(), cost=0):
+    return pl.pallas_call(
+        kernel,
+        out_shape=[jax.ShapeDtypeStruct(shape, jnp.float32) for shape in outs],
+        scratch_shapes=[pltpu.VMEM(shape, jnp.float32) for shape in scratch],
+        cost_estimate=pl.CostEstimate(flops=cost, bytes_accessed=4 * cost, transcendentals=0)
+        if cost
+        else None,
+        compiler_params=pltpu.CompilerParams(vmem_limit_bytes=48 * 1024 * 1024),
+    )
+
+
+def pair_shards(labels, roughness, potential, displacement):
+    slab, rows, _ = labels.shape
+    count = FIELDS * slab
+    mid = rows // 2
+    sizes = {name: lax.axis_size(name) for name in ("grow", "cy", "cz")}
+
+    def index(grow, cy, cz):
+        cy, cz = cy % sizes["cy"], cz % sizes["cz"]
+        return (grow * sizes["cy"] + cy) * sizes["cz"] + cz
+
+    everyone = [
+        (grow, cy, cz)
+        for grow in range(sizes["grow"])
+        for cy in range(sizes["cy"])
+        for cz in range(sizes["cz"])
+    ]
+
+    def send(block, route):
+        pairs = [(index(*at), index(*route(*at))) for at in everyone]
+        return lax.ppermute(block, ("grow", "cy", "cz"), pairs)
+
+    phase, halves, first, last = call(
+        prepare_kernel,
+        [labels.shape, (count * mid, LANES), (count * TILE, LANES), (count * TILE, LANES)],
+    )(labels, roughness, potential, displacement)
+    halves = send(halves, lambda grow, cy, cz: (1 - grow, cy, cz))
+    above = send(last, lambda grow, cy, cz: (grow, cy + 1, cz))
+    below = send(first, lambda grow, cy, cz: (grow, cy - 1, cz))
+    extra = rim_rows(slab)
+    across, same, other = call(
+        rims_kernel, [(count * TILE + extra, LANES), (extra, LANES), (extra, LANES)]
+    )(phase, potential, displacement, above, below)
+    across = send(across, lambda grow, cy, cz: (1 - grow, cy, cz))
+    same = send(same, lambda grow, cy, cz: (grow, cy, cz - 1 if grow else cz + 1))
+    other = send(other, lambda grow, cy, cz: (1 - grow, cy, cz + 1 if grow else cz - 1))
+    deep = (2 * slab, rows + 2 * LEAD, LANES)
+    result, message = call(
+        steps_kernel,
+        [(FIELDS, slab, rows, LANES), (count * mid, LANES)],
+        [deep, (3,) + deep, (2, 3) + deep, deep, (2 * slab + 1,) + deep[1:], deep, deep],
+    )(phase, potential, displacement, above, below, halves, across, same, other)
+    message = from_behind(message, "grow", -1)
+    return call(finish_kernel, [labels.shape, labels.shape, displacement.shape])(result, message)
+
+
+def fits_pair(labels):
+    rows, columns = labels.shape[1:]
+    blocks = rows % (2 * TILE) == 0 and rows // TILE * REACH <= LANES
+    return lax.axis_size("grow") == 2 and columns == LANES and REACH == TILE and blocks
+
+
+def whole(labels, roughness, potential, displacement):
+    plan = pair_shards if fits_pair(labels) else shards
+    return tuple(plan(labels, roughness, potential, displacement))
+
+
 def solution(mesh):
     placed = (
         P("grow", "cy", "cz"),
@@ -217,7 +661,7 @@
         P(None, "grow", "cy", "cz"),
     )
     return jax.shard_map(
-        shards,
+        whole,
         mesh=mesh,
         in_specs=placed,
         out_specs=(P("grow", "cy", "cz"), P("grow", "cy", "cz"), P(None, "grow", "cy", "cz")),

time: 304 us -> 84.9 us (0.28); the launches traced: 300 us -> 84.7 us
  other arithmetic: 123 us -> 0 us
  waiting for transfers between devices: 109 us -> 28.5 us
  Pallas kernels: 0 us -> 39.9 us
  local copies, waits for them, and re-layouts: 43.5 us -> 3.98 us
  starting transfers between devices: 22.9 us -> 11.6 us
    another operation x18 -> x0, other arithmetic: 76.9 us -> none  [elastic_sweep(): return jnp.stack(updated)]
    ppermute x12 -> x6, waiting for transfers between devices: 78 us -> 12 us  [send(): return lax.ppermute(block, ('grow', 'cy', 'cz'), pairs)]
    pallas_call x0 -> x4, Pallas kernels: none -> 39.9 us  [the longest x1 37.2 us: pair_shards(): call(steps_kernel, [(FIELDS, slab, rows, LANES), (count * mid, LANES)], [...]
    slice x11 -> x0, local copies, waits for them, and re-layouts: 26.2 us -> none  [the longest x6 17 us: extended(): lax.slice_in_dim(cells, cells.shape[dim] - width, cells.shape[dim], axis=...]
    concatenate x7 -> x0, other arithmetic: 20.7 us -> none  [the longest x4 19.1 us: extended(): jnp.concatenate([lax.ppermute(tail, axis, [(i, (i + 1) % count) for i in...]
    select_n x13 -> x0, other arithmetic: 20.3 us -> none  [the longest x12 20.1 us: pin_ends(): return jnp.where(position >= limit, high, result)]
    ppermute x1, waiting for transfers between devices: 31.4 us -> 16.5 us  [from_behind(): return lax.ppermute(block, axis, route)]
    ppermute x4 -> x0, local copies, waits for them, and re-layouts: 11.6 us -> none  [the longest x2 5.95 us: extended(): lax.ppermute(tail, axis, [(i, (i + 1) % count) for i in range(ends)])]
  transfers between devices with their start and end apart: 13 -> 7, of which waited for: 13 -> 5; matrix products, arithmetic and copies ran while one was open for 5% -> 0% of each run, Pallas kernels for 0% -> 1%
where the time goes in v1:
time: 84.9 us; the launch traced here: 84.7 us
  Pallas kernels  39.9 us (47%)
  waiting for transfers between devices  28.5 us (34%)
  starting transfers between devices  11.6 us (14%)
  local copies, waits for them, and re-layouts  3.98 us (5%)
    pallas_call x1, Pallas kernels, pair_shards(): call(steps_kernel, [(FIELDS, slab, rows, LANES), (count * mid, LANES)], [...  37.2 us
    ppermute x1, waiting for transfers between devices, from_behind(): return lax.ppermute(block, axis, route)  16.5 us
    ppermute x6, waiting for transfers between devices, send(): return lax.ppermute(block, ('grow', 'cy', 'cz'), pairs)  12 us
    ppermute x6, starting transfers between devices, send(): return lax.ppermute(block, ('grow', 'cy', 'cz'), pairs)  10.3 us
    unnamed x10, local copies, waits for them, and re-layouts  3.98 us
  transfers between devices with their start and end apart: 7, of which 5 were waited for; matrix products, arithmetic and copies ran while one was open for 0% of the time, Pallas kernels for 1%

profile of v1, /device:TPU:0, one launch (start us, length us, event | category | flops | bytes accessed | tf_op | source)
XLA Modules:
  0.0 84.7 jit_solution(12881036000385877666)
XLA Ops:
  0.6 0.0 copy-start
  0.6 1.1 %copy-done = f32[3,4,128,128]{3,2,1,0:T(8,128)S(1)} copy-done((f32[3,4,128,128]{3,2,1,0:T(8,128)S(1)}, f32[3,4,128,128]{3,2,1,0:T(8,128)}, u32[]{:S(2)}) %copy-start) | copy-done | bytes 786456
  1.8 0.9 %copy-done.2 = f32[4,128,128]{2,1,0:T(8,128)S(1)} copy-done((f32[4,128,128]{2,1,0:T(8,128)S(1)}, f32[4,128,128]{2,1,0:T(8,128)}, u32[]{:S(2)}) %copy-start.2) | copy-done | bytes 262168
  2.7 0.9 %copy-done.3 = s32[4,128,128]{2,1,0:T(8,128)S(1)} copy-done((s32[4,128,128]{2,1,0:T(8,128)S(1)}, s32[4,128,128]{2,1,0:T(8,128)}, u32[]{:S(2)}) %copy-start.3) | copy-done | bytes 262168
  3.7 0.9 %copy-done.4 = f32[4,128,128]{2,1,0:T(8,128)S(1)} copy-done((f32[4,128,128]{2,1,0:T(8,128)S(1)}, f32[4,128,128]{2,1,0:T(8,128)}, u32[]{:S(2)}) %copy-start.4) | copy-done | bytes 262168
  4.6 0.2 shard_map.67
  4.9 3.0 %collective-permute-start.2 = (f32[1280,128]{1,0:T(8,128)S(1)}, f32[1280,128]{1,0:T(8,128)S(1)}, u32[]{:S(2)}, u32[]{:S(2)}) collective-permute-start(f32[1280,128]{1,0:T(8,128)S(1)} %get-tuple-element.15), channel_id=1, source_target_pairs={{0,16},{1,17},{2,18},{3,19},{4,20},{5,21},{6,22},{7,23},{8,24},{9,... | collective-permute-start | bytes 1966088 | tf_op jit(solution)/shard_map/ppermute | solution.py:619
  7.9 0.0 collective-permute-start
  7.9 1.7 %collective-permute-start.1 = (f32[160,128]{1,0:T(8,128)S(1)}, f32[160,128]{1,0:T(8,128)S(1)}, u32[]{:S(2)}, u32[]{:S(2)}) collective-permute-start(f32[160,128]{1,0:T(8,128)S(1)} %get-tuple-element.14), channel_id=1, source_target_pairs={{0,12},{1,13},{2,14},{3,15},{4,0},{5,1},{6,2},{7,3},{8,4},{9,5},{1... | collective-permute-start | bytes 245768 | tf_op jit(solution)/shard_map/ppermute | solution.py:619
  9.6 2.1 %collective-permute-done.above = f32[160,128]{1,0:T(8,128)S(1)} collective-permute-done((f32[160,128]{1,0:T(8,128)S(1)}, f32[160,128]{1,0:T(8,128)S(1)}, u32[]{:S(2)}, u32[]{:S(2)}) %collective-permute-start) | collective-permute-done | bytes 81952 | tf_op jit(solution)/shard_map/ppermute | solution.py:619
  11.7 0.0 collective-permute-done.1.below
  11.7 0.0 copy-done.1
  11.7 1.2 %shard_map.68 = (f32[344,128]{1,0:T(8,128)S(1)}, f32[184,128]{1,0:T(8,128)S(1)}, f32[184,128]{1,0:T(8,128)S(1)}) custom-call(f32[4,128,128]{2,1,0:T(8,128)S(1)} %get-tuple-element.12.phase.phase_in, f32[4,128,128]{2,1,0:T(8,128)S(1)} %copy-done.2, f32[3,4,128,128]{3,2,1,0:T(8,128)S(1)} %copy-done.1, f32[160,128]{1,0:T(8,128)S(1)} %collective-permute-done.above, ...), custom_call_target="tpu_custom_call" | custom-call | tf_op jit(solution)/shard_map/pallas_call | solution.py:629
  13.0 0.5 collective-permute-start.3
  13.5 1.7 %collective-permute-start.4 = (f32[184,128]{1,0:T(8,128)S(1)}, f32[184,128]{1,0:T(8,128)S(1)}, u32[]{:S(2)}, u32[]{:S(2)}) collective-permute-start(f32[184,128]{1,0:T(8,128)S(1)} %get-tuple-element.17), channel_id=1, source_target_pairs={{0,1},{1,2},{2,3},{3,0},{4,5},{5,6},{6,7},{7,4},{8,9},{9,10},{10,1... | collective-permute-start | bytes 282632 | tf_op jit(solution)/shard_map/ppermute | solution.py:619
  15.1 3.4 %collective-permute-start.5 = (f32[184,128]{1,0:T(8,128)S(1)}, f32[184,128]{1,0:T(8,128)S(1)}, u32[]{:S(2)}, u32[]{:S(2)}) collective-permute-start(f32[184,128]{1,0:T(8,128)S(1)} %get-tuple-element.18), channel_id=1, source_target_pairs={{0,19},{1,16},{2,17},{3,18},{4,23},{5,20},{6,21},{7,22},{8,27},{9,... | collective-permute-start | bytes 282632 | tf_op jit(solution)/shard_map/ppermute | solution.py:619
  18.5 1.6 %collective-permute-done.4.same = f32[184,128]{1,0:T(8,128)S(1)} collective-permute-done((f32[184,128]{1,0:T(8,128)S(1)}, f32[184,128]{1,0:T(8,128)S(1)}, u32[]{:S(2)}, u32[]{:S(2)}) %collective-permute-start.4) | collective-permute-done | bytes 94240 | tf_op jit(solution)/shard_map/ppermute | solution.py:619
  20.1 3.5 %collective-permute-done.5.other = f32[184,128]{1,0:T(8,128)S(1)} collective-permute-done((f32[184,128]{1,0:T(8,128)S(1)}, f32[184,128]{1,0:T(8,128)S(1)}, u32[]{:S(2)}, u32[]{:S(2)}) %collective-permute-start.5) | collective-permute-done | bytes 94240 | tf_op jit(solution)/shard_map/ppermute | solution.py:619
  23.6 4.8 %collective-permute-done.3.across = f32[344,128]{1,0:T(8,128)S(1)} collective-permute-done((f32[344,128]{1,0:T(8,128)S(1)}, f32[344,128]{1,0:T(8,128)S(1)}, u32[]{:S(2)}, u32[]{:S(2)}) %collective-permute-start.3) | collective-permute-done | bytes 176160 | tf_op jit(solution)/shard_map/ppermute | solution.py:619
  28.4 0.0 collective-permute-done.2.halves
  28.4 37.2 %shard_map.69 = (f32[5,4,128,128]{3,2,1,0:T(8,128)S(1)}, f32[1280,128]{1,0:T(8,128)S(1)}) custom-call(f32[4,128,128]{2,1,0:T(8,128)S(1)} %get-tuple-element.12.phase.phase_in, f32[4,128,128]{2,1,0:T(8,128)S(1)} %copy-done.2, f32[3,4,128,128]{3,2,1,0:T(8,128)S(1)} %copy-done.1, f32[160,128]{1,0:T(8,128)S(1)} %collective-permute-done.above, ...), custom_call_target="tpu_custom_call" | custom-call | tf_op jit(solution)/shard_map/pallas_call | solution.py:636
  65.6 1.3 %collective-permute-start.6 = (f32[1280,128]{1,0:T(8,128)S(1)}, f32[1280,128]{1,0:T(8,128)S(1)}, u32[]{:S(2)}, u32[]{:S(2)}) collective-permute-start(f32[1280,128]{1,0:T(8,128)S(1)} %get-tuple-element.20), channel_id=1, source_target_pairs={{16,0},{17,1},{18,2},{19,3},{20,4},{21,5},{22,6},{23,7},{24,8},{25... | collective-permute-start | bytes 1966088 | tf_op jit(solution)/shard_map/ppermute | solution.py:47
  66.9 16.5 %collective-permute-done.6.message = f32[1280,128]{1,0:T(8,128)S(1)} collective-permute-done((f32[1280,128]{1,0:T(8,128)S(1)}, f32[1280,128]{1,0:T(8,128)S(1)}, u32[]{:S(2)}, u32[]{:S(2)}) %collective-permute-start.6) | collective-permute-done | bytes 655392 | tf_op jit(solution)/shard_map/ppermute | solution.py:47
  83.4 1.2 %shard_map.70 = (f32[4,128,128]{2,1,0:T(8,128)}, f32[4,128,128]{2,1,0:T(8,128)}, f32[3,4,128,128]{3,2,1,0:T(8,128)}) custom-call(f32[5,4,128,128]{3,2,1,0:T(8,128)S(1)} %get-tuple-element.19.result, f32[1280,128]{1,0:T(8,128)S(1)} %collective-permute-done.6.message), custom_call_target="tpu_custom_call" | custom-call | tf_op jit(solution)/shard_map/pallas_call | solution.py:642
  (4 shorter events, 0.0 us)
Async XLA Ops:
  0.6 1.1 %copy-start = (f32[3,4,128,128]{3,2,1,0:T(8,128)S(1)}, f32[3,4,128,128]{3,2,1,0:T(8,128)}, u32[]{:S(2)}) copy-start(f32[3,4,128,128]{3,2,1,0:T(8,128)} %displacement_in.1) | copy-start | bytes 2359300
  1.8 0.9 %copy-start.2 = (f32[4,128,128]{2,1,0:T(8,128)S(1)}, f32[4,128,128]{2,1,0:T(8,128)}, u32[]{:S(2)}) copy-start(f32[4,128,128]{2,1,0:T(8,128)} %potential_in.1) | copy-start | bytes 786436
  2.7 0.9 %copy-start.3 = (s32[4,128,128]{2,1,0:T(8,128)S(1)}, s32[4,128,128]{2,1,0:T(8,128)}, u32[]{:S(2)}) copy-start(s32[4,128,128]{2,1,0:T(8,128)} %labels.1) | copy-start | bytes 786436
  3.7 0.9 %copy-start.4 = (f32[4,128,128]{2,1,0:T(8,128)S(1)}, f32[4,128,128]{2,1,0:T(8,128)}, u32[]{:S(2)}) copy-start(f32[4,128,128]{2,1,0:T(8,128)} %roughness.1) | copy-start | bytes 786436
  4.6 7.1 %copy-start.1 = (f32[3,4,128,128]{3,2,1,0:T(8,128)S(1)}, f32[3,4,128,128]{3,2,1,0:T(8,128)}, u32[]{:S(2)}) copy-start(f32[3,4,128,128]{3,2,1,0:T(8,128)} %displacement_in.1) | copy-start | bytes 2359300
  4.9 23.5 %collective-permute-start.2 = (f32[1280,128]{1,0:T(8,128)S(1)}, f32[1280,128]{1,0:T(8,128)S(1)}, u32[]{:S(2)}, u32[]{:S(2)}) collective-permute-start(f32[1280,128]{1,0:T(8,128)S(1)} %get-tuple-element.15), channel_id=1, source_target_pairs={{0,16},{1,17},{2,18},{3,19},{4,20},{5,21},{6,22},{7,23},{8,24},{9,... | collective-permute-start | bytes 1966088 | tf_op jit(solution)/shard_map/ppermute | solution.py:619
  7.9 3.9 %collective-permute-start = (f32[160,128]{1,0:T(8,128)S(1)}, f32[160,128]{1,0:T(8,128)S(1)}, u32[]{:S(2)}, u32[]{:S(2)}) collective-permute-start(f32[160,128]{1,0:T(8,128)S(1)} %get-tuple-element.13), channel_id=1, source_target_pairs={{0,4},{1,5},{2,6},{3,7},{4,8},{5,9},{6,10},{7,11},{8,12},{9,13},{1... | collective-permute-start | bytes 245768 | tf_op jit(solution)/shard_map/ppermute | solution.py:619
  7.9 3.9 %collective-permute-start.1 = (f32[160,128]{1,0:T(8,128)S(1)}, f32[160,128]{1,0:T(8,128)S(1)}, u32[]{:S(2)}, u32[]{:S(2)}) collective-permute-start(f32[160,128]{1,0:T(8,128)S(1)} %get-tuple-element.14), channel_id=1, source_target_pairs={{0,12},{1,13},{2,14},{3,15},{4,0},{5,1},{6,2},{7,3},{8,4},{9,5},{1... | collective-permute-start | bytes 245768 | tf_op jit(solution)/shard_map/ppermute | solution.py:619
  13.0 15.4 %collective-permute-start.3 = (f32[344,128]{1,0:T(8,128)S(1)}, f32[344,128]{1,0:T(8,128)S(1)}, u32[]{:S(2)}, u32[]{:S(2)}) collective-permute-start(f32[344,128]{1,0:T(8,128)S(1)} %get-tuple-element.16), channel_id=1, source_target_pairs={{0,16},{1,17},{2,18},{3,19},{4,20},{5,21},{6,22},{7,23},{8,24},{9,... | collective-permute-start | bytes 528392 | tf_op jit(solution)/shard_map/ppermute | solution.py:619
  13.5 6.6 %collective-permute-start.4 = (f32[184,128]{1,0:T(8,128)S(1)}, f32[184,128]{1,0:T(8,128)S(1)}, u32[]{:S(2)}, u32[]{:S(2)}) collective-permute-start(f32[184,128]{1,0:T(8,128)S(1)} %get-tuple-element.17), channel_id=1, source_target_pairs={{0,1},{1,2},{2,3},{3,0},{4,5},{5,6},{6,7},{7,4},{8,9},{9,10},{10,1... | collective-permute-start | bytes 282632 | tf_op jit(solution)/shard_map/ppermute | solution.py:619
  15.1 8.4 %collective-permute-start.5 = (f32[184,128]{1,0:T(8,128)S(1)}, f32[184,128]{1,0:T(8,128)S(1)}, u32[]{:S(2)}, u32[]{:S(2)}) collective-permute-start(f32[184,128]{1,0:T(8,128)S(1)} %get-tuple-element.18), channel_id=1, source_target_pairs={{0,19},{1,16},{2,17},{3,18},{4,23},{5,20},{6,21},{7,22},{8,27},{9,... | collective-permute-start | bytes 282632 | tf_op jit(solution)/shard_map/ppermute | solution.py:619
  65.6 17.8 %collective-permute-start.6 = (f32[1280,128]{1,0:T(8,128)S(1)}, f32[1280,128]{1,0:T(8,128)S(1)}, u32[]{:S(2)}, u32[]{:S(2)}) collective-permute-start(f32[1280,128]{1,0:T(8,128)S(1)} %get-tuple-element.20), channel_id=1, source_target_pairs={{16,0},{17,1},{18,2},{19,3},{20,4},{21,5},{22,6},{23,7},{24,8},{25... | collective-permute-start | bytes 1966088 | tf_op jit(solution)/shard_map/ppermute | solution.py:47

commit v2 on v1

--- a/solution.py
+++ b/solution.py
@@ -238,41 +238,48 @@
     return jnp.logical_xor(low, side == 1)
 
 
-def field_reader(phase, potential, displacement):
-    def read(field, plane, row):
-        rows = pl.ds(row, TILE)
-        if field == 0:
-            return phase[plane, rows, :]
-        if field == 1:
-            return potential[plane, rows, :]
-        return displacement[field - 2, plane, rows, :]
-
-    return read
-
-
-def prepare_kernel(labels, roughness, potential, displacement, phase, halves, first, last):
-    slab, rows, _ = labels.shape
+def prepare_kernel(
+    labels, roughness, potential, displacement, fields, halves, first, last, marks, rough, arrived
+):
+    _, slab, rows, _ = fields.shape
     theirs = jnp.logical_not(half_of(lax.axis_index("grow")))
-    read = field_reader(phase, potential, displacement)
     mid = rows // 2
+    copies = [
+        pltpu.make_async_copy(source, target, arrived.at[which])
+        for which, (source, target) in enumerate(
+            (
+                (labels, marks),
+                (roughness, rough),
+                (potential, fields.at[1]),
+                (displacement, fields.at[pl.ds(2, 3)]),
+            )
+        )
+    ]
+    for copy in copies:
+        copy.start()
+    for copy in copies[:2]:
+        copy.wait()
     for plane in range(slab):
         for row in range(0, rows, TILE):
             spot = (plane, pl.ds(row, TILE), slice(None))
-            mark = labels[spot].astype(jnp.float32)
-            rough = 0.3 * roughness[spot]
-            phase[spot] = mark * (1.0 - rough) + (1.0 - mark) * rough
+            mark = marks[spot].astype(jnp.float32)
+            part = 0.3 * rough[spot]
+            fields[(0,) + spot] = mark * (1.0 - part) + (1.0 - mark) * part
+    for copy in copies[2:]:
+        copy.wait()
     for field in range(FIELDS):
         for plane in range(slab):
             which = field * slab + plane
             for row in range(0, mid, TILE):
-                upper = read(field, plane, row)
-                lower = turned(read(field, plane, row + mid), LANES // 2)
+                upper = fields[field, plane, pl.ds(row, TILE), :]
+                lower = turned(fields[field, plane, pl.ds(row + mid, TILE), :], LANES // 2)
                 halves[pl.ds(which * mid + row, TILE), :] = jnp.where(theirs, upper, lower)
-            first[pl.ds(which * TILE, TILE), :] = read(field, plane, 0)
-            last[pl.ds(which * TILE, TILE), :] = read(field, plane, rows - TILE)
-
-
-def strips(read, above, below, slab, rows, base, out, start):
+            first[pl.ds(which * TILE, TILE), :] = fields[field, plane, pl.ds(0, TILE), :]
+            last[pl.ds(which * TILE, TILE), :] = fields[field, plane, pl.ds(rows - TILE, TILE), :]
+
+
+def strips(fields, above, below, base, out, start):
+    _, slab, rows, _ = fields.shape
     count = FIELDS * slab
     spare = []
     for field in range(FIELDS):
@@ -280,7 +287,8 @@
             which = field * slab + plane
             packed = jnp.zeros((TILE, LANES), jnp.float32)
             for group in range(rows // TILE):
-                block = turned(read(field, plane, group * TILE), group * REACH - base)
+                block = fields[field, plane, pl.ds(group * TILE, TILE), :]
+                block = turned(block, group * REACH - base)
                 packed = jnp.where(from_lane(group * REACH), block, packed)
             out[pl.ds(start + which * TILE, TILE), :] = packed
             spot = pl.ds(which * TILE, TILE)
@@ -305,20 +313,19 @@
     return (count + -(-2 * count * REACH // LANES)) * TILE
 
 
-def rims_kernel(phase, potential, displacement, above, below, across, same, other):
-    slab, rows, _ = phase.shape
+def rims_kernel(fields, above, below, across, same, other):
+    slab = fields.shape[1]
     side = lax.axis_index("grow")
     theirs = jnp.logical_not(half_of(side))
-    read = field_reader(phase, potential, displacement)
     count = FIELDS * slab
     for which in range(count):
         spot = pl.ds(which * TILE, TILE)
         across[spot, :] = jnp.where(theirs, above[spot, :], turned(below[spot, :], LANES // 2))
     inner = LANES // 2 - REACH + REACH * side
     outer = LANES - REACH
-    strips(read, above, below, slab, rows, inner, across, count * TILE)
-    strips(read, above, below, slab, rows, outer * (1 - side), same, 0)
-    strips(read, above, below, slab, rows, outer * side, other, 0)
+    strips(fields, above, below, inner, across, count * TILE)
+    strips(fields, above, below, outer * (1 - side), same, 0)
+    strips(fields, above, below, outer * side, other, 0)
 
 
 def conduct_of(step):
@@ -326,16 +333,16 @@
 
 
 def steps_kernel(
-    phase_in, potential_in, displacement_in, above, below, halves, across, same, other,
-    result, message, phase, pots, disps, slopes, cond_x, cond_y, cond_z,
+    fields, above, below, halves, across, same, other, result, message,
+    phase, phase_new, pot, pot_new, disp, disp_new,
+    slopes, slopes_y, cond_x, cond_y, cond_y_back, cond_z,
 ):
-    slab, rows, _ = phase_in.shape
+    _, slab, rows, _ = fields.shape
     planes = 2 * slab
     side = lax.axis_index("grow")
     mine = half_of(side)
     mid = rows // 2
     count = FIELDS * slab
-    read = field_reader(phase_in, potential_in, displacement_in)
     groups = rows // TILE
     per = LANES // REACH
     inner = LANES // 2 - REACH * side
@@ -347,9 +354,9 @@
         if field == 0:
             phase[spot] = value
         elif field == 1:
-            pots[(0,) + spot] = value
+            pot[spot] = value
         else:
-            disps[(0, field - 2) + spot] = value
+            disp[(field - 2,) + spot] = value
 
     for field in range(FIELDS):
         for plane in range(slab):
@@ -360,7 +367,7 @@
             strip = across[pl.ds((count + which) * TILE, TILE), :]
             for group in range(groups):
                 row = group * TILE
-                near = read(field, plane, row)
+                near = fields[field, plane, pl.ds(row, TILE), :]
                 back = outer - group * REACH
                 put(field, own, row, jnp.where(in_outer, turned(from_same, back), near))
                 block = halves[pl.ds(which * mid + row % mid, TILE), :]
@@ -382,7 +389,10 @@
 
     def over_rows(body, rim=1):
         def one(block, carry):
-            body(pl.multiple_of(block * TILE, TILE))
+            row = pl.multiple_of(block * TILE, TILE)
+            stores = body(row)
+            for ref, lead, value in stores:
+                ref[lead + (pl.ds(row, TILE), slice(None))] = value
             return carry
 
         lax.fori_loop(LEAD // TILE - rim, (LEAD + rows) // TILE + rim, one, 0)
@@ -396,37 +406,46 @@
     def down(block):
         return pltpu.roll(block, 1, 1)
 
-    def set_conduct(row):
-        face = 0.5 * TAU_P
-        before = conduct_of(1.0)
-        for plane in range(planes):
-            step = interp(at(phase, row, 0, plane))
-            here = conduct_of(step)
-            slopes[plane, pl.ds(row, TILE), :] = (0.5 * TAU_U * STIFF * EIGEN) * step
-            cond_x[plane, pl.ds(row, TILE), :] = face * (before + here)
-            cond_y[plane, pl.ds(row, TILE), :] = face * (
-                here + conduct_of(interp(at(phase, row, 1, plane)))
-            )
-            cond_z[plane, pl.ds(row, TILE), :] = face * (here + up(here))
-            before = here
-        cond_x[planes, pl.ds(row, TILE), :] = face * (before + conduct_of(0.0))
+    push = 0.5 * TAU_U * STIFF * EIGEN
+
+    def conduct_pass(source):
+        def body(row):
+            stores = []
+            face = 0.5 * TAU_P
+            before = conduct_of(1.0)
+            for plane in range(planes):
+                step, above, below = (interp(at(source, row, shift, plane)) for shift in (0, 1, -1))
+                here = conduct_of(step)
+                stores += [
+                    (slopes, (plane,), push * step),
+                    (slopes_y, (plane,), push * (above - below)),
+                    (cond_x, (plane,), face * (before + here)),
+                    (cond_y, (plane,), face * (here + conduct_of(above))),
+                    (cond_y_back, (plane,), face * (here + conduct_of(below))),
+                    (cond_z, (plane,), face * (here + up(here))),
+                ]
+                before = here
+            return stores + [(cond_x, (planes,), face * (before + conduct_of(0.0)))]
+
+        return body
 
     def potential_pass(old, new, low):
         def body(row):
-            here = at(pots, row, 0, old, low)
-            before = at(pots, row, 0, old, low - 1) if low else 0.0
+            stores = []
+            here = at(old, row, 0, low)
+            before = at(old, row, 0, low - 1) if low else 0.0
             entering = at(cond_x, row, 0, low) * (here - before)
             for plane in range(low, planes):
-                after = at(pots, row, 0, old, plane + 1) if plane + 1 < planes else V_HIGH
+                after = at(old, row, 0, plane + 1) if plane + 1 < planes else V_HIGH
                 leaving = at(cond_x, row, 0, plane + 1) * (after - here)
-                along_y = at(cond_y, row, 0, plane) * (at(pots, row, 1, old, plane) - here)
-                along_y -= at(cond_y, row, -1, plane) * (here - at(pots, row, -1, old, plane))
+                along_y = at(cond_y, row, 0, plane) * (at(old, row, 1, plane) - here)
+                along_y -= at(cond_y_back, row, 0, plane) * (here - at(old, row, -1, plane))
                 along_z = at(cond_z, row, 0, plane) * (up(here) - here)
                 along_z -= down(along_z)
-                pots[new, plane, pl.ds(row, TILE), :] = here + (
-                    (leaving - entering) + along_y + along_z
-                )
+                value = here + ((leaving - entering) + along_y + along_z)
+                stores.append((new, (plane,), value))
                 here, entering = after, leaving
+            return stores
 
         return body
 
@@ -440,131 +459,110 @@
         def body(row):
             def load(plane):
                 if plane < 0 or plane >= planes:
-                    edge = 0.5 * TAU_U * STIFF * EIGEN if plane < 0 else 0.0
-                    return (0.0, 0.0, 0.0, 0.0, -edge)
-                a, b, c = (at(disps, row, 0, old, part, plane) for part in range(3))
-                diff = at(disps, row, 1, old, 0, plane) - at(disps, row, -1, old, 0, plane)
-                b_up, b_down = at(disps, row, 1, old, 1, plane), at(disps, row, -1, old, 1, plane)
-                slope = cross * (b_up - b_down) - at(slopes, row, 0, plane)
-                return (a, b, c, diff, slope)
-
+                    return (0.0,) * 3, (0.0,) * 3, (0.0,) * 3, -push if plane < 0 else 0.0
+                parts = [at(old, row, 0, part, plane) for part in range(3)]
+                ahead = [at(old, row, 1, part, plane) for part in range(3)]
+                back = [at(old, row, -1, part, plane) for part in range(3)]
+                sums = [one + two for one, two in zip(ahead, back)]
+                diffs = [one - two for one, two in zip(ahead, back)]
+                return parts, sums, diffs, cross * diffs[1] - at(slopes, row, 0, plane)
+
+            stores = []
             before, here = load(low - 1), load(low)
             for plane in range(low, planes):
                 after = load(plane + 1)
-                a, b, c, _, slope = here
-                sum_x = [after[part] + before[part] for part in range(3)]
-                ends = [
-                    [at(disps, row, shift, old, part, plane) for shift in (1, -1)]
-                    for part in range(3)
-                ]
-                sum_y = [pair[0] + pair[1] for pair in ends]
-                lift = cross * (after[2] - before[2])
+                (a, b, c), sums, diffs, slope = here
+                sum_x = [one + two for one, two in zip(after[0], before[0])]
+                lift = cross * (after[0][2] - before[0][2])
                 mid_a = side_on * a
                 new_a = (
                     keep * a
                     + head_on * sum_x[0]
-                    + side_on * sum_y[0]
+                    + side_on * sums[0]
                     + (up(mid_a + lift) + down(mid_a - lift))
-                    + (after[4] - before[4])
+                    + (after[3] - before[3])
                 )
-                lift = cross * (ends[2][0] - ends[2][1])
+                lift = cross * diffs[2]
                 mid_b = side_on * b
                 new_b = (
                     keep * b
-                    + head_on * sum_y[1]
+                    + head_on * sums[1]
                     + side_on * sum_x[1]
                     + (up(mid_b + lift) + down(mid_b - lift))
-                    + cross * (after[3] - before[3])
-                    - (at(slopes, row, 1, plane) - at(slopes, row, -1, plane))
+                    + (cross * (after[2][0] - before[2][0]) - at(slopes_y, row, 0, plane))
                 )
-                lift = cross * (after[0] - before[0]) + slope
+                lift = cross * (after[0][0] - before[0][0]) + slope
                 mid_c = head_on * c
                 new_c = (
                     keep * c
-                    + side_on * (sum_x[2] + sum_y[2])
+                    + side_on * (sum_x[2] + sums[2])
                     + (up(mid_c + lift) + down(mid_c - lift))
                 )
-                spot = (plane, pl.ds(row, TILE), slice(None))
-                disps[(new, 0) + spot] = new_a
-                disps[(new, 1) + spot] = new_b
-                disps[(new, 2) + spot] = new_c
+                stores += [(new, (0, plane), new_a), (new, (1, plane), new_b), (new, (2, plane), new_c)]
                 before, here = here, after
+            return stores
 
         return body
 
-    def phase_pass(pot_at, disp_at, low, store):
+    def phase_pass(source, pot_now, disp_now, low, store):
         def body(row):
             def load(plane):
                 if plane < 0 or plane >= planes:
                     return (1.0 if plane < 0 else 0.0, 0.0)
-                return (at(phase, row, 0, plane), at(disps, row, 0, disp_at, 0, plane))
-
+                return (at(source, row, 0, plane), at(disp_now, row, 0, 0, plane))
+
+            stores = []
             before, here = load(low - 1), load(low)
             for plane in range(low, planes):
                 after = load(plane + 1)
                 p = here[0]
-                c = at(disps, row, 0, disp_at, 2, plane)
+                c = at(disp_now, row, 0, 2, plane)
                 div = (
                     (after[1] - before[1])
-                    + (at(disps, row, 1, disp_at, 1, plane) - at(disps, row, -1, disp_at, 1, plane))
+                    + (at(disp_now, row, 1, 1, plane) - at(disp_now, row, -1, 1, plane))
                     + (up(c) - down(c))
                 )
                 over = (
-                    (at(pots, row, 0, pot_at, plane) - REST)
+                    (at(pot_now, row, 0, plane) - REST)
                     + (0.5 * OMEGA_THIRD * STIFF) * div
                     - (OMEGA_THIRD * STIFF * 3.0 * EIGEN) * interp(p)
                 )
                 drive = jnp.exp(over) - jnp.exp(-over)
                 lap = (
                     (before[0] + after[0])
-                    + (at(phase, row, 1, plane) + at(phase, row, -1, plane))
+                    + (at(source, row, 1, plane) + at(source, row, -1, plane))
                     + (up(p) + down(p))
                     - 6.0 * p
                 )
                 well = p * (1.0 - p)
                 change = lap - well * (2.0 * (1.0 - 2.0 * p) + (6.0 * RATE) * drive)
-                store(plane, row, p + TIME_STEP * change)
+                stores.append((store, (plane,), p + TIME_STEP * change))
                 before, here = here, after
+            return stores
 
         return body
 
-    def store_new(plane, row, value):
-        pots[2, plane, pl.ds(row, TILE), :] = value
-
-    def store_result(plane, row, value):
-        to = (plane - slab, pl.ds(pl.multiple_of(row - LEAD, TILE), TILE), slice(None))
-        result[(0,) + to] = value
-        result[(1,) + to] = at(pots, row, 0, 0, plane)
-        for part in range(3):
-            result[(2 + part,) + to] = at(disps, row, 0, 0, part, plane)
-
-    now = 0
     for step in range(STEPS):
         last = step == STEPS - 1
-        over_rows(set_conduct)
+        over_rows(conduct_pass(phase))
         for sweep in range(SWEEPS):
             low = max(0, slab - (SWEEPS - 1 - sweep)) if last else 0
-            over_rows(potential_pass(now, 1 - now, low))
+            over_rows(potential_pass(pot, pot_new, low))
             low = max(0, slab - (SWEEPS - sweep)) if last else 0
-            over_rows(elastic_pass(now, 1 - now, low))
-            now = 1 - now
-        if last:
-            over_rows(phase_pass(now, now, slab, store_result), 0)
-        else:
-            over_rows(phase_pass(now, now, 0, store_new))
-
-            def copy(row):
-                for plane in range(planes):
-                    phase[plane, pl.ds(row, TILE), :] = at(pots, row, 0, 2, plane)
-
-            over_rows(copy)
+            over_rows(elastic_pass(disp, disp_new, low))
+            pot, pot_new, disp, disp_new = pot_new, pot, disp_new, disp
+        over_rows(phase_pass(phase, pot, disp, slab if last else 0, phase_new), 0 if last else 1)
+        phase, phase_new = phase_new, phase
     for field in range(FIELDS):
+        source = (phase, pot, disp.at[0], disp.at[1], disp.at[2])[field]
         for plane in range(slab):
             for row in range(0, mid, TILE):
-                upper = result[field, plane, pl.ds(row, TILE), :]
-                lower = turned(result[field, plane, pl.ds(row + mid, TILE), :], LANES // 2)
+                upper = source[slab + plane, pl.ds(LEAD + row, TILE), :]
+                lower = source[slab + plane, pl.ds(LEAD + row + mid, TILE), :]
+                result[field, plane, pl.ds(row, TILE), :] = upper
+                result[field, plane, pl.ds(row + mid, TILE), :] = lower
                 to = pl.ds((field * slab + plane) * mid + row, TILE)
-                message[to, :] = jnp.where(mine, upper, lower)
+                message[to, :] = jnp.where(mine, upper, turned(lower, LANES // 2))
 
 
 def finish_kernel(result, message, phase, potential, displacement):
@@ -585,14 +583,14 @@
                     out[spot if field < 2 else (field - 2,) + spot] = whole
 
 
-def call(kernel, outs, scratch=(), cost=0):
+def call(kernel, outs, scratch=(), **how):
     return pl.pallas_call(
         kernel,
         out_shape=[jax.ShapeDtypeStruct(shape, jnp.float32) for shape in outs],
-        scratch_shapes=[pltpu.VMEM(shape, jnp.float32) for shape in scratch],
-        cost_estimate=pl.CostEstimate(flops=cost, bytes_accessed=4 * cost, transcendentals=0)
-        if cost
-        else None,
+        scratch_shapes=[
+            pltpu.VMEM(one, jnp.float32) if isinstance(one, tuple) else one for one in scratch
+        ],
+        **how,
         compiler_params=pltpu.CompilerParams(vmem_limit_bytes=48 * 1024 * 1024),
     )
 
@@ -618,9 +616,11 @@
         pairs = [(index(*at), index(*route(*at))) for at in everyone]
         return lax.ppermute(block, ("grow", "cy", "cz"), pairs)
 
-    phase, halves, first, last = call(
+    fields, halves, first, last = call(
         prepare_kernel,
-        [labels.shape, (count * mid, LANES), (count * TILE, LANES), (count * TILE, LANES)],
+        [(FIELDS,) + labels.shape, (count * mid, LANES)] + [(count * TILE, LANES)] * 2,
+        [pltpu.VMEM(labels.shape, labels.dtype), labels.shape, pltpu.SemaphoreType.DMA((4,))],
+        in_specs=[pl.BlockSpec(memory_space=pltpu.HBM)] * 4,
     )(labels, roughness, potential, displacement)
     halves = send(halves, lambda grow, cy, cz: (1 - grow, cy, cz))
     above = send(last, lambda grow, cy, cz: (grow, cy + 1, cz))
@@ -628,7 +628,7 @@
     extra = rim_rows(slab)
     across, same, other = call(
         rims_kernel, [(count * TILE + extra, LANES), (extra, LANES), (extra, LANES)]
-    )(phase, potential, displacement, above, below)
+    )(fields, above, below)
     across = send(across, lambda grow, cy, cz: (1 - grow, cy, cz))
     same = send(same, lambda grow, cy, cz: (grow, cy, cz - 1 if grow else cz + 1))
     other = send(other, lambda grow, cy, cz: (1 - grow, cy, cz + 1 if grow else cz - 1))
@@ -636,8 +636,10 @@
     result, message = call(
         steps_kernel,
         [(FIELDS, slab, rows, LANES), (count * mid, LANES)],
-        [deep, (3,) + deep, (2, 3) + deep, deep, (2 * slab + 1,) + deep[1:], deep, deep],
-    )(phase, potential, displacement, above, below, halves, across, same, other)
+        [deep] * 4
+        + [(3,) + deep] * 2
+        + [deep, deep, (2 * slab + 1,) + deep[1:], deep, deep, deep],
+    )(fields, above, below, halves, across, same, other)
     message = from_behind(message, "grow", -1)
     return call(finish_kernel, [labels.shape, labels.shape, displacement.shape])(result, message)
 

time: 84.9 us -> 86.9 us (1.024)
  Pallas kernels: 39.9 us -> 41.9 us
    pallas_call x1, Pallas kernels: 37.2 us -> 39 us  [pair_shards(): call(steps_kernel, [(FIELDS, slab, rows, LANES), (count * mid, LANES)], [...]
    unnamed x10 -> x8, local copies, waits for them, and re-layouts: 3.98 us -> 3.97 us
where the time goes in v2:
time: 86.9 us; the launch traced here: 86.7 us
  Pallas kernels  41.9 us (48%)
  waiting for transfers between devices  28.5 us (33%)
  starting transfers between devices  11.6 us (13%)
  local copies, waits for them, and re-layouts  3.97 us (5%)
    pallas_call x1, Pallas kernels, pair_shards(): call(steps_kernel, [(FIELDS, slab, rows, LANES), (count * mid, LANES)], [...  39 us
    ppermute x1, waiting for transfers between devices, from_behind(): return lax.ppermute(block, axis, route)  16.5 us
    ppermute x6, waiting for transfers between devices, send(): return lax.ppermute(block, ('grow', 'cy', 'cz'), pairs)  12 us
    ppermute x6, starting transfers between devices, send(): return lax.ppermute(block, ('grow', 'cy', 'cz'), pairs)  10.3 us
    unnamed x8, local copies, waits for them, and re-layouts  3.97 us
  transfers between devices with their start and end apart: 7, of which 5 were waited for; matrix products, arithmetic and copies ran while one was open for 0% of the time, Pallas kernels for 1%

profile of v2, /device:TPU:0, one launch (start us, length us, event | category | flops | bytes accessed | tf_op | source)
XLA Modules:
  0.0 86.7 jit_solution(13566136159289433568)
XLA Ops:
  0.6 0.0 copy-start
  0.6 1.1 %copy-done = f32[3,4,128,128]{3,2,1,0:T(8,128)S(1)} copy-done((f32[3,4,128,128]{3,2,1,0:T(8,128)S(1)}, f32[3,4,128,128]{3,2,1,0:T(8,128)}, u32[]{:S(2)}) %copy-start) | copy-done | bytes 786456
  1.8 0.0 copy-start.1
  1.8 0.9 %copy-done.1 = s32[4,128,128]{2,1,0:T(8,128)S(1)} copy-done((s32[4,128,128]{2,1,0:T(8,128)S(1)}, s32[4,128,128]{2,1,0:T(8,128)}, u32[]{:S(2)}) %copy-start.1) | copy-done | bytes 262168
  2.7 0.9 %copy-done.2 = f32[4,128,128]{2,1,0:T(8,128)S(1)} copy-done((f32[4,128,128]{2,1,0:T(8,128)S(1)}, f32[4,128,128]{2,1,0:T(8,128)}, u32[]{:S(2)}) %copy-start.2) | copy-done | bytes 262168
  3.7 0.9 %copy-done.3 = f32[4,128,128]{2,1,0:T(8,128)S(1)} copy-done((f32[4,128,128]{2,1,0:T(8,128)S(1)}, f32[4,128,128]{2,1,0:T(8,128)}, u32[]{:S(2)}) %copy-start.3) | copy-done | bytes 262168
  4.6 0.5 shard_map.67
  5.1 3.0 %collective-permute-start.2 = (f32[1280,128]{1,0:T(8,128)S(1)}, f32[1280,128]{1,0:T(8,128)S(1)}, u32[]{:S(2)}, u32[]{:S(2)}) collective-permute-start(f32[1280,128]{1,0:T(8,128)S(1)} %get-tuple-element.15), channel_id=1, source_target_pairs={{0,16},{1,17},{2,18},{3,19},{4,20},{5,21},{6,22},{7,23},{8,24},{9,... | collective-permute-start | bytes 1966088 | tf_op jit(solution)/shard_map/ppermute | solution.py:617
  8.1 0.0 collective-permute-start
  8.1 1.7 %collective-permute-start.1 = (f32[160,128]{1,0:T(8,128)S(1)}, f32[160,128]{1,0:T(8,128)S(1)}, u32[]{:S(2)}, u32[]{:S(2)}) collective-permute-start(f32[160,128]{1,0:T(8,128)S(1)} %get-tuple-element.14), channel_id=1, source_target_pairs={{0,12},{1,13},{2,14},{3,15},{4,0},{5,1},{6,2},{7,3},{8,4},{9,5},{1... | collective-permute-start | bytes 245768 | tf_op jit(solution)/shard_map/ppermute | solution.py:617
  9.8 2.1 %collective-permute-done.above = f32[160,128]{1,0:T(8,128)S(1)} collective-permute-done((f32[160,128]{1,0:T(8,128)S(1)}, f32[160,128]{1,0:T(8,128)S(1)}, u32[]{:S(2)}, u32[]{:S(2)}) %collective-permute-start) | collective-permute-done | bytes 81952 | tf_op jit(solution)/shard_map/ppermute | solution.py:617
  12.0 0.0 collective-permute-done.1.below
  12.0 1.2 %shard_map.68 = (f32[344,128]{1,0:T(8,128)S(1)}, f32[184,128]{1,0:T(8,128)S(1)}, f32[184,128]{1,0:T(8,128)S(1)}) custom-call(f32[5,4,128,128]{3,2,1,0:T(8,128)S(1)} %get-tuple-element.12.fields, f32[160,128]{1,0:T(8,128)S(1)} %collective-permute-done.above, f32[160,128]{1,0:T(8,128)S(1)} %collective-permute-done.1.below), custom_call_target="tpu_custom_call" | custom-call | tf_op jit(solution)/shard_map/pallas_call | solution.py:629
  13.2 0.5 collective-permute-start.3
  13.7 1.7 %collective-permute-start.4 = (f32[184,128]{1,0:T(8,128)S(1)}, f32[184,128]{1,0:T(8,128)S(1)}, u32[]{:S(2)}, u32[]{:S(2)}) collective-permute-start(f32[184,128]{1,0:T(8,128)S(1)} %get-tuple-element.17), channel_id=1, source_target_pairs={{0,1},{1,2},{2,3},{3,0},{4,5},{5,6},{6,7},{7,4},{8,9},{9,10},{10,1... | collective-permute-start | bytes 282632 | tf_op jit(solution)/shard_map/ppermute | solution.py:617
  15.4 3.4 %collective-permute-start.5 = (f32[184,128]{1,0:T(8,128)S(1)}, f32[184,128]{1,0:T(8,128)S(1)}, u32[]{:S(2)}, u32[]{:S(2)}) collective-permute-start(f32[184,128]{1,0:T(8,128)S(1)} %get-tuple-element.18), channel_id=1, source_target_pairs={{0,19},{1,16},{2,17},{3,18},{4,23},{5,20},{6,21},{7,22},{8,27},{9,... | collective-permute-start | bytes 282632 | tf_op jit(solution)/shard_map/ppermute | solution.py:617
  18.8 1.6 %collective-permute-done.4.same = f32[184,128]{1,0:T(8,128)S(1)} collective-permute-done((f32[184,128]{1,0:T(8,128)S(1)}, f32[184,128]{1,0:T(8,128)S(1)}, u32[]{:S(2)}, u32[]{:S(2)}) %collective-permute-start.4) | collective-permute-done | bytes 94240 | tf_op jit(solution)/shard_map/ppermute | solution.py:617
  20.3 3.5 %collective-permute-done.5.other = f32[184,128]{1,0:T(8,128)S(1)} collective-permute-done((f32[184,128]{1,0:T(8,128)S(1)}, f32[184,128]{1,0:T(8,128)S(1)}, u32[]{:S(2)}, u32[]{:S(2)}) %collective-permute-start.5) | collective-permute-done | bytes 94240 | tf_op jit(solution)/shard_map/ppermute | solution.py:617
  23.8 4.8 %collective-permute-done.3.across = f32[344,128]{1,0:T(8,128)S(1)} collective-permute-done((f32[344,128]{1,0:T(8,128)S(1)}, f32[344,128]{1,0:T(8,128)S(1)}, u32[]{:S(2)}, u32[]{:S(2)}) %collective-permute-start.3) | collective-permute-done | bytes 176160 | tf_op jit(solution)/shard_map/ppermute | solution.py:617
  28.6 0.0 collective-permute-done.2.halves
  28.6 39.0 %shard_map.69 = (f32[5,4,128,128]{3,2,1,0:T(8,128)S(1)}, f32[1280,128]{1,0:T(8,128)S(1)}) custom-call(f32[5,4,128,128]{3,2,1,0:T(8,128)S(1)} %get-tuple-element.12.fields, f32[160,128]{1,0:T(8,128)S(1)} %collective-permute-done.above, f32[160,128]{1,0:T(8,128)S(1)} %collective-permute-done.1.below, f32[1280,128]{1,0:T(8,128)S(1)} %collective-permute-done.2.halves, ...), custom_call_target="tpu_custom_call" | custom-call | tf_op jit(solution)/shard_map/pallas_call | solution.py:636
  67.7 1.3 %collective-permute-start.6 = (f32[1280,128]{1,0:T(8,128)S(1)}, f32[1280,128]{1,0:T(8,128)S(1)}, u32[]{:S(2)}, u32[]{:S(2)}) collective-permute-start(f32[1280,128]{1,0:T(8,128)S(1)} %get-tuple-element.20), channel_id=1, source_target_pairs={{16,0},{17,1},{18,2},{19,3},{20,4},{21,5},{22,6},{23,7},{24,8},{25... | collective-permute-start | bytes 1966088 | tf_op jit(solution)/shard_map/ppermute | solution.py:47
  69.0 16.5 %collective-permute-done.6.message = f32[1280,128]{1,0:T(8,128)S(1)} collective-permute-done((f32[1280,128]{1,0:T(8,128)S(1)}, f32[1280,128]{1,0:T(8,128)S(1)}, u32[]{:S(2)}, u32[]{:S(2)}) %collective-permute-start.6) | collective-permute-done | bytes 655392 | tf_op jit(solution)/shard_map/ppermute | solution.py:47
  85.5 1.2 %shard_map.70 = (f32[4,128,128]{2,1,0:T(8,128)}, f32[4,128,128]{2,1,0:T(8,128)}, f32[3,4,128,128]{3,2,1,0:T(8,128)}) custom-call(f32[5,4,128,128]{3,2,1,0:T(8,128)S(1)} %get-tuple-element.19.result, f32[1280,128]{1,0:T(8,128)S(1)} %collective-permute-done.6.message), custom_call_target="tpu_custom_call" | custom-call | tf_op jit(solution)/shard_map/pallas_call | solution.py:644
  (2 shorter events, 0.0 us)
Async XLA Ops:
  0.6 1.1 %copy-start = (f32[3,4,128,128]{3,2,1,0:T(8,128)S(1)}, f32[3,4,128,128]{3,2,1,0:T(8,128)}, u32[]{:S(2)}) copy-start(f32[3,4,128,128]{3,2,1,0:T(8,128)} %displacement.1) | copy-start | bytes 2359300
  1.8 0.9 %copy-start.1 = (s32[4,128,128]{2,1,0:T(8,128)S(1)}, s32[4,128,128]{2,1,0:T(8,128)}, u32[]{:S(2)}) copy-start(s32[4,128,128]{2,1,0:T(8,128)} %labels.1) | copy-start | bytes 786436
  2.7 0.9 %copy-start.2 = (f32[4,128,128]{2,1,0:T(8,128)S(1)}, f32[4,128,128]{2,1,0:T(8,128)}, u32[]{:S(2)}) copy-start(f32[4,128,128]{2,1,0:T(8,128)} %roughness.1) | copy-start | bytes 786436
  3.7 0.9 %copy-start.3 = (f32[4,128,128]{2,1,0:T(8,128)S(1)}, f32[4,128,128]{2,1,0:T(8,128)}, u32[]{:S(2)}) copy-start(f32[4,128,128]{2,1,0:T(8,128)} %potential.1) | copy-start | bytes 786436
  5.1 23.5 %collective-permute-start.2 = (f32[1280,128]{1,0:T(8,128)S(1)}, f32[1280,128]{1,0:T(8,128)S(1)}, u32[]{:S(2)}, u32[]{:S(2)}) collective-permute-start(f32[1280,128]{1,0:T(8,128)S(1)} %get-tuple-element.15), channel_id=1, source_target_pairs={{0,16},{1,17},{2,18},{3,19},{4,20},{5,21},{6,22},{7,23},{8,24},{9,... | collective-permute-start | bytes 1966088 | tf_op jit(solution)/shard_map/ppermute | solution.py:617
  8.1 3.9 %collective-permute-start = (f32[160,128]{1,0:T(8,128)S(1)}, f32[160,128]{1,0:T(8,128)S(1)}, u32[]{:S(2)}, u32[]{:S(2)}) collective-permute-start(f32[160,128]{1,0:T(8,128)S(1)} %get-tuple-element.13), channel_id=1, source_target_pairs={{0,4},{1,5},{2,6},{3,7},{4,8},{5,9},{6,10},{7,11},{8,12},{9,13},{1... | collective-permute-start | bytes 245768 | tf_op jit(solution)/shard_map/ppermute | solution.py:617
  8.1 3.9 %collective-permute-start.1 = (f32[160,128]{1,0:T(8,128)S(1)}, f32[160,128]{1,0:T(8,128)S(1)}, u32[]{:S(2)}, u32[]{:S(2)}) collective-permute-start(f32[160,128]{1,0:T(8,128)S(1)} %get-tuple-element.14), channel_id=1, source_target_pairs={{0,12},{1,13},{2,14},{3,15},{4,0},{5,1},{6,2},{7,3},{8,4},{9,5},{1... | collective-permute-start | bytes 245768 | tf_op jit(solution)/shard_map/ppermute | solution.py:617
  13.2 15.4 %collective-permute-start.3 = (f32[344,128]{1,0:T(8,128)S(1)}, f32[344,128]{1,0:T(8,128)S(1)}, u32[]{:S(2)}, u32[]{:S(2)}) collective-permute-start(f32[344,128]{1,0:T(8,128)S(1)} %get-tuple-element.16), channel_id=1, source_target_pairs={{0,16},{1,17},{2,18},{3,19},{4,20},{5,21},{6,22},{7,23},{8,24},{9,... | collective-permute-start | bytes 528392 | tf_op jit(solution)/shard_map/ppermute | solution.py:617
  13.7 6.6 %collective-permute-start.4 = (f32[184,128]{1,0:T(8,128)S(1)}, f32[184,128]{1,0:T(8,128)S(1)}, u32[]{:S(2)}, u32[]{:S(2)}) collective-permute-start(f32[184,128]{1,0:T(8,128)S(1)} %get-tuple-element.17), channel_id=1, source_target_pairs={{0,1},{1,2},{2,3},{3,0},{4,5},{5,6},{6,7},{7,4},{8,9},{9,10},{10,1... | collective-permute-start | bytes 282632 | tf_op jit(solution)/shard_map/ppermute | solution.py:617
  15.4 8.4 %collective-permute-start.5 = (f32[184,128]{1,0:T(8,128)S(1)}, f32[184,128]{1,0:T(8,128)S(1)}, u32[]{:S(2)}, u32[]{:S(2)}) collective-permute-start(f32[184,128]{1,0:T(8,128)S(1)} %get-tuple-element.18), channel_id=1, source_target_pairs={{0,19},{1,16},{2,17},{3,18},{4,23},{5,20},{6,21},{7,22},{8,27},{9,... | collective-permute-start | bytes 282632 | tf_op jit(solution)/shard_map/ppermute | solution.py:617
  67.7 17.8 %collective-permute-start.6 = (f32[1280,128]{1,0:T(8,128)S(1)}, f32[1280,128]{1,0:T(8,128)S(1)}, u32[]{:S(2)}, u32[]{:S(2)}) collective-permute-start(f32[1280,128]{1,0:T(8,128)S(1)} %get-tuple-element.20), channel_id=1, source_target_pairs={{16,0},{17,1},{18,2},{19,3},{20,4},{21,5},{22,6},{23,7},{24,8},{25... | collective-permute-start | bytes 1966088 | tf_op jit(solution)/shard_map/ppermute | solution.py:47

commit v3 on v2

--- a/solution.py
+++ b/solution.py
@@ -213,8 +213,8 @@
 
 REACH = STEPS * (SWEEPS + 1)
 TILE = 8
-LEAD = 2 * TILE
 FIELDS = 5
+LAG = 2
 
 
 def lanes(shape):
@@ -334,7 +334,7 @@
 
 def steps_kernel(
     fields, above, below, halves, across, same, other, result, message,
-    phase, phase_new, pot, pot_new, disp, disp_new,
+    natural, phase, phase_new, pot, pot_new, disp, disp_new,
     slopes, slopes_y, cond_x, cond_y, cond_y_back, cond_z,
 ):
     _, slab, rows, _ = fields.shape
@@ -348,15 +348,7 @@
     inner = LANES // 2 - REACH * side
     outer = (LANES - REACH) * (1 - side)
     in_inner, in_outer = from_lane(inner), from_lane(outer)
-
-    def put(field, plane, row, value):
-        spot = (plane, pl.ds(LEAD + row, TILE), slice(None))
-        if field == 0:
-            phase[spot] = value
-        elif field == 1:
-            pot[spot] = value
-        else:
-            disp[(field - 2,) + spot] = value
+    segment = phase.shape[1] - 2
 
     for field in range(FIELDS):
         for plane in range(slab):
@@ -367,38 +359,60 @@
             strip = across[pl.ds((count + which) * TILE, TILE), :]
             for group in range(groups):
                 row = group * TILE
+                to = pl.ds(REACH + row, TILE)
                 near = fields[field, plane, pl.ds(row, TILE), :]
                 back = outer - group * REACH
-                put(field, own, row, jnp.where(in_outer, turned(from_same, back), near))
+                natural[field, own, to, :] = jnp.where(in_outer, turned(from_same, back), near)
                 block = halves[pl.ds(which * mid + row % mid, TILE), :]
                 if row >= mid:
                     block = turned(block, LANES // 2)
                 block = jnp.where(in_inner, turned(strip, inner - group * REACH), block)
-                put(field, far, row, jnp.where(in_outer, turned(from_other, back), block))
+                natural[field, far, to, :] = jnp.where(in_outer, turned(from_other, back), block)
             rim = across[spot, :]
-            for end, row in ((0, -TILE), (1, rows)):
+            for end, to in ((0, pl.ds(0, TILE)), (1, pl.ds(REACH + rows, TILE))):
                 at, group = divmod(2 * which + end, per)
                 extra = pl.ds((count + at) * TILE, TILE)
                 back = outer - group * REACH
                 near = (below if end else above)[spot, :]
-                put(field, own, row, jnp.where(in_outer, turned(same[extra, :], back), near))
+                block = jnp.where(in_outer, turned(same[extra, :], back), near)
+                natural[field, own, to, :] = block
                 block = turned(rim, LANES // 2) if end else rim
                 strip = across[pl.ds((2 * count + at) * TILE, TILE), :]
                 block = jnp.where(in_inner, turned(strip, inner - group * REACH), block)
-                put(field, far, row, jnp.where(in_outer, turned(other[extra, :], back), block))
-
-    def over_rows(body, rim=1):
-        def one(block, carry):
-            row = pl.multiple_of(block * TILE, TILE)
-            stores = body(row)
-            for ref, lead, value in stores:
-                ref[lead + (pl.ds(row, TILE), slice(None))] = value
+                block = jnp.where(in_outer, turned(other[extra, :], back), block)
+                natural[field, far, to, :] = block
+
+    def parts_of(phase, pot, disp):
+        return (phase, pot, disp.at[0], disp.at[1], disp.at[2])
+
+    def close(ref):
+        for plane in range(planes):
+            ref[plane, 0] = pltpu.roll(ref[plane, segment], 1, 0)
+            ref[plane, segment + 1] = pltpu.roll(ref[plane, 1], TILE - 1, 0)
+
+    for field, ref in enumerate(parts_of(phase, pot, disp)):
+        for plane in range(planes):
+            for row in range(segment):
+                ref[plane, 1 + row] = natural[field, plane, pl.ds(row, TILE, stride=segment), :]
+        close(ref)
+
+    def over_rows(*bodies):
+        def one(row, carry):
+            waiting = []
+            running = [body(row) for body in bodies]
+            while running:
+                for body in list(running):
+                    stores = next(body, None)
+                    if stores is None:
+                        running.remove(body)
+                    else:
+                        waiting.append(stores)
+                while len(waiting) > LAG * len(bodies) or (waiting and not running):
+                    for ref, lead, value in waiting.pop(0):
+                        ref[lead + (row,)] = value
             return carry
 
-        lax.fori_loop(LEAD // TILE - rim, (LEAD + rows) // TILE + rim, one, 0)
-
-    def at(ref, row, shift, *lead):
-        return ref[lead + (pl.ds(row + shift, TILE), slice(None))]
+        lax.fori_loop(1, segment + 1, one, 0)
 
     def up(block):
         return pltpu.roll(block, LANES - 1, 1)
@@ -410,42 +424,38 @@
 
     def conduct_pass(source):
         def body(row):
-            stores = []
             face = 0.5 * TAU_P
             before = conduct_of(1.0)
             for plane in range(planes):
-                step, above, below = (interp(at(source, row, shift, plane)) for shift in (0, 1, -1))
+                step, ahead, back = (interp(source[plane, row + shift]) for shift in (0, 1, -1))
                 here = conduct_of(step)
-                stores += [
+                yield [
                     (slopes, (plane,), push * step),
-                    (slopes_y, (plane,), push * (above - below)),
+                    (slopes_y, (plane,), push * (ahead - back)),
                     (cond_x, (plane,), face * (before + here)),
-                    (cond_y, (plane,), face * (here + conduct_of(above))),
-                    (cond_y_back, (plane,), face * (here + conduct_of(below))),
+                    (cond_y, (plane,), face * (here + conduct_of(ahead))),
+                    (cond_y_back, (plane,), face * (here + conduct_of(back))),
                     (cond_z, (plane,), face * (here + up(here))),
                 ]
                 before = here
-            return stores + [(cond_x, (planes,), face * (before + conduct_of(0.0)))]
+            yield [(cond_x, (planes,), face * (before + conduct_of(0.0)))]
 
         return body
 
     def potential_pass(old, new, low):
         def body(row):
-            stores = []
-            here = at(old, row, 0, low)
-            before = at(old, row, 0, low - 1) if low else 0.0
-            entering = at(cond_x, row, 0, low) * (here - before)
+            here = old[low, row]
+            before = old[low - 1, row] if low else 0.0
+            entering = cond_x[low, row] * (here - before)
             for plane in range(low, planes):
-                after = at(old, row, 0, plane + 1) if plane + 1 < planes else V_HIGH
-                leaving = at(cond_x, row, 0, plane + 1) * (after - here)
-                along_y = at(cond_y, row, 0, plane) * (at(old, row, 1, plane) - here)
-                along_y -= at(cond_y_back, row, 0, plane) * (here - at(old, row, -1, plane))
-                along_z = at(cond_z, row, 0, plane) * (up(here) - here)
+                after = old[plane + 1, row] if plane + 1 < planes else V_HIGH
+                leaving = cond_x[plane + 1, row] * (after - here)
+                along_y = cond_y[plane, row] * (old[plane, row + 1] - here)
+                along_y -= cond_y_back[plane, row] * (here - old[plane, row - 1])
+                along_z = cond_z[plane, row] * (up(here) - here)
                 along_z -= down(along_z)
-                value = here + ((leaving - entering) + along_y + along_z)
-                stores.append((new, (plane,), value))
+                yield [(new, (plane,), here + ((leaving - entering) + along_y + along_z))]
                 here, entering = after, leaving
-            return stores
 
         return body
 
@@ -460,14 +470,13 @@
             def load(plane):
                 if plane < 0 or plane >= planes:
                     return (0.0,) * 3, (0.0,) * 3, (0.0,) * 3, -push if plane < 0 else 0.0
-                parts = [at(old, row, 0, part, plane) for part in range(3)]
-                ahead = [at(old, row, 1, part, plane) for part in range(3)]
-                back = [at(old, row, -1, part, plane) for part in range(3)]
+                parts = [old[part, plane, row] for part in range(3)]
+                ahead = [old[part, plane, row + 1] for part in range(3)]
+                back = [old[part, plane, row - 1] for part in range(3)]
                 sums = [one + two for one, two in zip(ahead, back)]
                 diffs = [one - two for one, two in zip(ahead, back)]
-                return parts, sums, diffs, cross * diffs[1] - at(slopes, row, 0, plane)
-
-            stores = []
+                return parts, sums, diffs, cross * diffs[1] - slopes[plane, row]
+
             before, here = load(low - 1), load(low)
             for plane in range(low, planes):
                 after = load(plane + 1)
@@ -489,7 +498,7 @@
                     + head_on * sums[1]
                     + side_on * sum_x[1]
                     + (up(mid_b + lift) + down(mid_b - lift))
-                    + (cross * (after[2][0] - before[2][0]) - at(slopes_y, row, 0, plane))
+                    + (cross * (after[2][0] - before[2][0]) - slopes_y[plane, row])
                 )
                 lift = cross * (after[0][0] - before[0][0]) + slope
                 mid_c = head_on * c
@@ -498,47 +507,44 @@
                     + side_on * (sum_x[2] + sums[2])
                     + (up(mid_c + lift) + down(mid_c - lift))
                 )
-                stores += [(new, (0, plane), new_a), (new, (1, plane), new_b), (new, (2, plane), new_c)]
+                yield [(new, (part, plane), value) for part, value in enumerate((new_a, new_b, new_c))]
                 before, here = here, after
-            return stores
 
         return body
 
-    def phase_pass(source, pot_now, disp_now, low, store):
+    def phase_pass(source, pot_now, disp_now, low, new):
         def body(row):
             def load(plane):
                 if plane < 0 or plane >= planes:
                     return (1.0 if plane < 0 else 0.0, 0.0)
-                return (at(source, row, 0, plane), at(disp_now, row, 0, 0, plane))
-
-            stores = []
+                return (source[plane, row], disp_now[0, plane, row])
+
             before, here = load(low - 1), load(low)
             for plane in range(low, planes):
                 after = load(plane + 1)
                 p = here[0]
-                c = at(disp_now, row, 0, 2, plane)
+                c = disp_now[2, plane, row]
                 div = (
                     (after[1] - before[1])
-                    + (at(disp_now, row, 1, 1, plane) - at(disp_now, row, -1, 1, plane))
+                    + (disp_now[1, plane, row + 1] - disp_now[1, plane, row - 1])
                     + (up(c) - down(c))
                 )
                 over = (
-                    (at(pot_now, row, 0, plane) - REST)
+                    (pot_now[plane, row] - REST)
                     + (0.5 * OMEGA_THIRD * STIFF) * div
                     - (OMEGA_THIRD * STIFF * 3.0 * EIGEN) * interp(p)
                 )
                 drive = jnp.exp(over) - jnp.exp(-over)
                 lap = (
                     (before[0] + after[0])
-                    + (at(source, row, 1, plane) + at(source, row, -1, plane))
+                    + (source[plane, row + 1] + source[plane, row - 1])
                     + (up(p) + down(p))
                     - 6.0 * p
                 )
                 well = p * (1.0 - p)
                 change = lap - well * (2.0 * (1.0 - 2.0 * p) + (6.0 * RATE) * drive)
-                stores.append((store, (plane,), p + TIME_STEP * change))
+                yield [(new, (plane,), p + TIME_STEP * change)]
                 before, here = here, after
-            return stores
 
         return body
 
@@ -546,19 +552,26 @@
         last = step == STEPS - 1
         over_rows(conduct_pass(phase))
         for sweep in range(SWEEPS):
-            low = max(0, slab - (SWEEPS - 1 - sweep)) if last else 0
-            over_rows(potential_pass(pot, pot_new, low))
-            low = max(0, slab - (SWEEPS - sweep)) if last else 0
-            over_rows(elastic_pass(disp, disp_new, low))
+            ahead = SWEEPS - 1 - sweep
+            over_rows(
+                potential_pass(pot, pot_new, max(0, slab - ahead) if last else 0),
+                elastic_pass(disp, disp_new, max(0, slab - ahead - 1) if last else 0),
+            )
             pot, pot_new, disp, disp_new = pot_new, pot, disp_new, disp
-        over_rows(phase_pass(phase, pot, disp, slab if last else 0, phase_new), 0 if last else 1)
+            for ref in (pot, disp.at[0], disp.at[1], disp.at[2]):
+                close(ref)
+        over_rows(phase_pass(phase, pot, disp, slab if last else 0, phase_new))
         phase, phase_new = phase_new, phase
-    for field in range(FIELDS):
-        source = (phase, pot, disp.at[0], disp.at[1], disp.at[2])[field]
+        if not last:
+            close(phase)
+    for field, ref in enumerate(parts_of(phase, pot, disp)):
         for plane in range(slab):
+            for row in range(segment):
+                to = pl.ds(row, TILE, stride=segment)
+                natural[field, plane, to, :] = ref[slab + plane, 1 + row]
             for row in range(0, mid, TILE):
-                upper = source[slab + plane, pl.ds(LEAD + row, TILE), :]
-                lower = source[slab + plane, pl.ds(LEAD + row + mid, TILE), :]
+                upper = natural[field, plane, pl.ds(REACH + row, TILE), :]
+                lower = natural[field, plane, pl.ds(REACH + row + mid, TILE), :]
                 result[field, plane, pl.ds(row, TILE), :] = upper
                 result[field, plane, pl.ds(row + mid, TILE), :] = lower
                 to = pl.ds((field * slab + plane) * mid + row, TILE)
@@ -632,11 +645,13 @@
     across = send(across, lambda grow, cy, cz: (1 - grow, cy, cz))
     same = send(same, lambda grow, cy, cz: (grow, cy, cz - 1 if grow else cz + 1))
     other = send(other, lambda grow, cy, cz: (1 - grow, cy, cz + 1 if grow else cz - 1))
-    deep = (2 * slab, rows + 2 * LEAD, LANES)
+    span = rows + 2 * REACH
+    deep = (2 * slab, span // TILE + 2, TILE, LANES)
     result, message = call(
         steps_kernel,
         [(FIELDS, slab, rows, LANES), (count * mid, LANES)],
-        [deep] * 4
+        [(FIELDS, 2 * slab, span, LANES)]
+        + [deep] * 4
         + [(3,) + deep] * 2
         + [deep, deep, (2 * slab + 1,) + deep[1:], deep, deep, deep],
     )(fields, above, below, halves, across, same, other)

time: 86.9 us -> 73.2 us (0.84)
  Pallas kernels: 41.9 us -> 28.1 us
    pallas_call x1, Pallas kernels: 39 us -> 25.3 us  [pair_shards(): call(steps_kernel, [(FIELDS, slab, rows, LANES), (count * mid, LANES)], [...]
  transfers between devices with their start and end apart: 7 -> 7, of which waited for: 5 -> 5; matrix products, arithmetic and copies ran while one was open for 0% -> 0% of each run, Pallas kernels for 1% -> 2%
where the time goes in v3:
time: 73.2 us; the launch traced here: 72.9 us
  waiting for transfers between devices  28.5 us (39%)
  Pallas kernels  28.1 us (38%)
  starting transfers between devices  11.6 us (16%)
  local copies, waits for them, and re-layouts  3.97 us (5%)
    pallas_call x1, Pallas kernels, pair_shards(): call(steps_kernel, [(FIELDS, slab, rows, LANES), (count * mid, LANES)], [...  25.3 us
    ppermute x1, waiting for transfers between devices, from_behind(): return lax.ppermute(block, axis, route)  16.5 us
    ppermute x6, waiting for transfers between devices, send(): return lax.ppermute(block, ('grow', 'cy', 'cz'), pairs)  12 us
    ppermute x6, starting transfers between devices, send(): return lax.ppermute(block, ('grow', 'cy', 'cz'), pairs)  10.3 us
    unnamed x8, local copies, waits for them, and re-layouts  3.97 us
  transfers between devices with their start and end apart: 7, of which 5 were waited for; matrix products, arithmetic and copies ran while one was open for 0% of the time, Pallas kernels for 2%

profile of v3, /device:TPU:0, one launch (start us, length us, event | category | flops | bytes accessed | tf_op | source)
XLA Modules:
  0.0 72.9 jit_solution(7985442558644240482)
XLA Ops:
  0.6 0.0 copy-start
  0.6 1.1 %copy-done = f32[3,4,128,128]{3,2,1,0:T(8,128)S(1)} copy-done((f32[3,4,128,128]{3,2,1,0:T(8,128)S(1)}, f32[3,4,128,128]{3,2,1,0:T(8,128)}, u32[]{:S(2)}) %copy-start) | copy-done | bytes 786456
  1.8 0.0 copy-start.1
  1.8 0.9 %copy-done.1 = s32[4,128,128]{2,1,0:T(8,128)S(1)} copy-done((s32[4,128,128]{2,1,0:T(8,128)S(1)}, s32[4,128,128]{2,1,0:T(8,128)}, u32[]{:S(2)}) %copy-start.1) | copy-done | bytes 262168
  2.7 0.9 %copy-done.2 = f32[4,128,128]{2,1,0:T(8,128)S(1)} copy-done((f32[4,128,128]{2,1,0:T(8,128)S(1)}, f32[4,128,128]{2,1,0:T(8,128)}, u32[]{:S(2)}) %copy-start.2) | copy-done | bytes 262168
  3.7 0.9 %copy-done.3 = f32[4,128,128]{2,1,0:T(8,128)S(1)} copy-done((f32[4,128,128]{2,1,0:T(8,128)S(1)}, f32[4,128,128]{2,1,0:T(8,128)}, u32[]{:S(2)}) %copy-start.3) | copy-done | bytes 262168
  4.6 0.5 shard_map.67
  5.1 3.0 %collective-permute-start.2 = (f32[1280,128]{1,0:T(8,128)S(1)}, f32[1280,128]{1,0:T(8,128)S(1)}, u32[]{:S(2)}, u32[]{:S(2)}) collective-permute-start(f32[1280,128]{1,0:T(8,128)S(1)} %get-tuple-element.15), channel_id=1, source_target_pairs={{0,16},{1,17},{2,18},{3,19},{4,20},{5,21},{6,22},{7,23},{8,24},{9,... | collective-permute-start | bytes 1966088 | tf_op jit(solution)/shard_map/ppermute | solution.py:630
  8.1 0.0 collective-permute-start
  8.1 1.7 %collective-permute-start.1 = (f32[160,128]{1,0:T(8,128)S(1)}, f32[160,128]{1,0:T(8,128)S(1)}, u32[]{:S(2)}, u32[]{:S(2)}) collective-permute-start(f32[160,128]{1,0:T(8,128)S(1)} %get-tuple-element.14), channel_id=1, source_target_pairs={{0,12},{1,13},{2,14},{3,15},{4,0},{5,1},{6,2},{7,3},{8,4},{9,5},{1... | collective-permute-start | bytes 245768 | tf_op jit(solution)/shard_map/ppermute | solution.py:630
  9.8 2.1 %collective-permute-done.above = f32[160,128]{1,0:T(8,128)S(1)} collective-permute-done((f32[160,128]{1,0:T(8,128)S(1)}, f32[160,128]{1,0:T(8,128)S(1)}, u32[]{:S(2)}, u32[]{:S(2)}) %collective-permute-start) | collective-permute-done | bytes 81952 | tf_op jit(solution)/shard_map/ppermute | solution.py:630
  12.0 0.0 collective-permute-done.1.below
  12.0 1.2 %shard_map.68 = (f32[344,128]{1,0:T(8,128)S(1)}, f32[184,128]{1,0:T(8,128)S(1)}, f32[184,128]{1,0:T(8,128)S(1)}) custom-call(f32[5,4,128,128]{3,2,1,0:T(8,128)S(1)} %get-tuple-element.12.fields, f32[160,128]{1,0:T(8,128)S(1)} %collective-permute-done.above, f32[160,128]{1,0:T(8,128)S(1)} %collective-permute-done.1.below), custom_call_target="tpu_custom_call" | custom-call | tf_op jit(solution)/shard_map/pallas_call | solution.py:642
  13.2 0.5 collective-permute-start.3
  13.7 1.7 %collective-permute-start.4 = (f32[184,128]{1,0:T(8,128)S(1)}, f32[184,128]{1,0:T(8,128)S(1)}, u32[]{:S(2)}, u32[]{:S(2)}) collective-permute-start(f32[184,128]{1,0:T(8,128)S(1)} %get-tuple-element.17), channel_id=1, source_target_pairs={{0,1},{1,2},{2,3},{3,0},{4,5},{5,6},{6,7},{7,4},{8,9},{9,10},{10,1... | collective-permute-start | bytes 282632 | tf_op jit(solution)/shard_map/ppermute | solution.py:630
  15.4 3.4 %collective-permute-start.5 = (f32[184,128]{1,0:T(8,128)S(1)}, f32[184,128]{1,0:T(8,128)S(1)}, u32[]{:S(2)}, u32[]{:S(2)}) collective-permute-start(f32[184,128]{1,0:T(8,128)S(1)} %get-tuple-element.18), channel_id=1, source_target_pairs={{0,19},{1,16},{2,17},{3,18},{4,23},{5,20},{6,21},{7,22},{8,27},{9,... | collective-permute-start | bytes 282632 | tf_op jit(solution)/shard_map/ppermute | solution.py:630
  18.8 1.6 %collective-permute-done.4.same = f32[184,128]{1,0:T(8,128)S(1)} collective-permute-done((f32[184,128]{1,0:T(8,128)S(1)}, f32[184,128]{1,0:T(8,128)S(1)}, u32[]{:S(2)}, u32[]{:S(2)}) %collective-permute-start.4) | collective-permute-done | bytes 94240 | tf_op jit(solution)/shard_map/ppermute | solution.py:630
  20.3 3.5 %collective-permute-done.5.other = f32[184,128]{1,0:T(8,128)S(1)} collective-permute-done((f32[184,128]{1,0:T(8,128)S(1)}, f32[184,128]{1,0:T(8,128)S(1)}, u32[]{:S(2)}, u32[]{:S(2)}) %collective-permute-start.5) | collective-permute-done | bytes 94240 | tf_op jit(solution)/shard_map/ppermute | solution.py:630
  23.8 4.8 %collective-permute-done.3.across = f32[344,128]{1,0:T(8,128)S(1)} collective-permute-done((f32[344,128]{1,0:T(8,128)S(1)}, f32[344,128]{1,0:T(8,128)S(1)}, u32[]{:S(2)}, u32[]{:S(2)}) %collective-permute-start.3) | collective-permute-done | bytes 176160 | tf_op jit(solution)/shard_map/ppermute | solution.py:630
  28.6 0.0 collective-permute-done.2.halves
  28.6 25.3 %shard_map.69 = (f32[5,4,128,128]{3,2,1,0:T(8,128)S(1)}, f32[1280,128]{1,0:T(8,128)S(1)}) custom-call(f32[5,4,128,128]{3,2,1,0:T(8,128)S(1)} %get-tuple-element.12.fields, f32[160,128]{1,0:T(8,128)S(1)} %collective-permute-done.above, f32[160,128]{1,0:T(8,128)S(1)} %collective-permute-done.1.below, f32[1280,128]{1,0:T(8,128)S(1)} %collective-permute-done.2.halves, ...), custom_call_target="tpu_custom_call" | custom-call | tf_op jit(solution)/shard_map/pallas_call | solution.py:650
  53.9 1.3 %collective-permute-start.6 = (f32[1280,128]{1,0:T(8,128)S(1)}, f32[1280,128]{1,0:T(8,128)S(1)}, u32[]{:S(2)}, u32[]{:S(2)}) collective-permute-start(f32[1280,128]{1,0:T(8,128)S(1)} %get-tuple-element.20), channel_id=1, source_target_pairs={{16,0},{17,1},{18,2},{19,3},{20,4},{21,5},{22,6},{23,7},{24,8},{25... | collective-permute-start | bytes 1966088 | tf_op jit(solution)/shard_map/ppermute | solution.py:47
  55.2 16.5 %collective-permute-done.6.message = f32[1280,128]{1,0:T(8,128)S(1)} collective-permute-done((f32[1280,128]{1,0:T(8,128)S(1)}, f32[1280,128]{1,0:T(8,128)S(1)}, u32[]{:S(2)}, u32[]{:S(2)}) %collective-permute-start.6) | collective-permute-done | bytes 655392 | tf_op jit(solution)/shard_map/ppermute | solution.py:47
  71.7 1.2 %shard_map.70 = (f32[4,128,128]{2,1,0:T(8,128)}, f32[4,128,128]{2,1,0:T(8,128)}, f32[3,4,128,128]{3,2,1,0:T(8,128)}) custom-call(f32[5,4,128,128]{3,2,1,0:T(8,128)S(1)} %get-tuple-element.19.result, f32[1280,128]{1,0:T(8,128)S(1)} %collective-permute-done.6.message), custom_call_target="tpu_custom_call" | custom-call | tf_op jit(solution)/shard_map/pallas_call | solution.py:659
  (2 shorter events, 0.0 us)
Async XLA Ops:
  0.6 1.1 %copy-start = (f32[3,4,128,128]{3,2,1,0:T(8,128)S(1)}, f32[3,4,128,128]{3,2,1,0:T(8,128)}, u32[]{:S(2)}) copy-start(f32[3,4,128,128]{3,2,1,0:T(8,128)} %displacement.1) | copy-start | bytes 2359300
  1.8 0.9 %copy-start.1 = (s32[4,128,128]{2,1,0:T(8,128)S(1)}, s32[4,128,128]{2,1,0:T(8,128)}, u32[]{:S(2)}) copy-start(s32[4,128,128]{2,1,0:T(8,128)} %labels.1) | copy-start | bytes 786436
  2.7 0.9 %copy-start.2 = (f32[4,128,128]{2,1,0:T(8,128)S(1)}, f32[4,128,128]{2,1,0:T(8,128)}, u32[]{:S(2)}) copy-start(f32[4,128,128]{2,1,0:T(8,128)} %roughness.1) | copy-start | bytes 786436
  3.7 0.9 %copy-start.3 = (f32[4,128,128]{2,1,0:T(8,128)S(1)}, f32[4,128,128]{2,1,0:T(8,128)}, u32[]{:S(2)}) copy-start(f32[4,128,128]{2,1,0:T(8,128)} %potential.1) | copy-start | bytes 786436
  5.1 23.5 %collective-permute-start.2 = (f32[1280,128]{1,0:T(8,128)S(1)}, f32[1280,128]{1,0:T(8,128)S(1)}, u32[]{:S(2)}, u32[]{:S(2)}) collective-permute-start(f32[1280,128]{1,0:T(8,128)S(1)} %get-tuple-element.15), channel_id=1, source_target_pairs={{0,16},{1,17},{2,18},{3,19},{4,20},{5,21},{6,22},{7,23},{8,24},{9,... | collective-permute-start | bytes 1966088 | tf_op jit(solution)/shard_map/ppermute | solution.py:630
  8.1 3.9 %collective-permute-start = (f32[160,128]{1,0:T(8,128)S(1)}, f32[160,128]{1,0:T(8,128)S(1)}, u32[]{:S(2)}, u32[]{:S(2)}) collective-permute-start(f32[160,128]{1,0:T(8,128)S(1)} %get-tuple-element.13), channel_id=1, source_target_pairs={{0,4},{1,5},{2,6},{3,7},{4,8},{5,9},{6,10},{7,11},{8,12},{9,13},{1... | collective-permute-start | bytes 245768 | tf_op jit(solution)/shard_map/ppermute | solution.py:630
  8.1 3.9 %collective-permute-start.1 = (f32[160,128]{1,0:T(8,128)S(1)}, f32[160,128]{1,0:T(8,128)S(1)}, u32[]{:S(2)}, u32[]{:S(2)}) collective-permute-start(f32[160,128]{1,0:T(8,128)S(1)} %get-tuple-element.14), channel_id=1, source_target_pairs={{0,12},{1,13},{2,14},{3,15},{4,0},{5,1},{6,2},{7,3},{8,4},{9,5},{1... | collective-permute-start | bytes 245768 | tf_op jit(solution)/shard_map/ppermute | solution.py:630
  13.2 15.4 %collective-permute-start.3 = (f32[344,128]{1,0:T(8,128)S(1)}, f32[344,128]{1,0:T(8,128)S(1)}, u32[]{:S(2)}, u32[]{:S(2)}) collective-permute-start(f32[344,128]{1,0:T(8,128)S(1)} %get-tuple-element.16), channel_id=1, source_target_pairs={{0,16},{1,17},{2,18},{3,19},{4,20},{5,21},{6,22},{7,23},{8,24},{9,... | collective-permute-start | bytes 528392 | tf_op jit(solution)/shard_map/ppermute | solution.py:630
  13.7 6.6 %collective-permute-start.4 = (f32[184,128]{1,0:T(8,128)S(1)}, f32[184,128]{1,0:T(8,128)S(1)}, u32[]{:S(2)}, u32[]{:S(2)}) collective-permute-start(f32[184,128]{1,0:T(8,128)S(1)} %get-tuple-element.17), channel_id=1, source_target_pairs={{0,1},{1,2},{2,3},{3,0},{4,5},{5,6},{6,7},{7,4},{8,9},{9,10},{10,1... | collective-permute-start | bytes 282632 | tf_op jit(solution)/shard_map/ppermute | solution.py:630
  15.4 8.4 %collective-permute-start.5 = (f32[184,128]{1,0:T(8,128)S(1)}, f32[184,128]{1,0:T(8,128)S(1)}, u32[]{:S(2)}, u32[]{:S(2)}) collective-permute-start(f32[184,128]{1,0:T(8,128)S(1)} %get-tuple-element.18), channel_id=1, source_target_pairs={{0,19},{1,16},{2,17},{3,18},{4,23},{5,20},{6,21},{7,22},{8,27},{9,... | collective-permute-start | bytes 282632 | tf_op jit(solution)/shard_map/ppermute | solution.py:630
  53.9 17.8 %collective-permute-start.6 = (f32[1280,128]{1,0:T(8,128)S(1)}, f32[1280,128]{1,0:T(8,128)S(1)}, u32[]{:S(2)}, u32[]{:S(2)}) collective-permute-start(f32[1280,128]{1,0:T(8,128)S(1)} %get-tuple-element.20), channel_id=1, source_target_pairs={{16,0},{17,1},{18,2},{19,3},{20,4},{21,5},{22,6},{23,7},{24,8},{25... | collective-permute-start | bytes 1966088 | tf_op jit(solution)/shard_map/ppermute | solution.py:47

commit v4 on v3

--- a/solution.py
+++ b/solution.py
@@ -214,7 +214,7 @@
 REACH = STEPS * (SWEEPS + 1)
 TILE = 8
 FIELDS = 5
-LAG = 2
+LAG = 99
 
 
 def lanes(shape):
@@ -596,7 +596,7 @@
                     out[spot if field < 2 else (field - 2,) + spot] = whole
 
 
-def call(kernel, outs, scratch=(), **how):
+def call(kernel, outs, scratch=(), limit=48, **how):
     return pl.pallas_call(
         kernel,
         out_shape=[jax.ShapeDtypeStruct(shape, jnp.float32) for shape in outs],
@@ -604,7 +604,7 @@
             pltpu.VMEM(one, jnp.float32) if isinstance(one, tuple) else one for one in scratch
         ],
         **how,
-        compiler_params=pltpu.CompilerParams(vmem_limit_bytes=48 * 1024 * 1024),
+        compiler_params=pltpu.CompilerParams(vmem_limit_bytes=limit * 1024 * 1024),
     )
 
 
@@ -633,6 +633,7 @@
         prepare_kernel,
         [(FIELDS,) + labels.shape, (count * mid, LANES)] + [(count * TILE, LANES)] * 2,
         [pltpu.VMEM(labels.shape, labels.dtype), labels.shape, pltpu.SemaphoreType.DMA((4,))],
+        limit=54,
         in_specs=[pl.BlockSpec(memory_space=pltpu.HBM)] * 4,
     )(labels, roughness, potential, displacement)
     halves = send(halves, lambda grow, cy, cz: (1 - grow, cy, cz))

time: 73.2 us -> 71.6 us (0.978)
  local copies, waits for them, and re-layouts: 3.97 us -> 1.32 us
  Pallas kernels: 28.1 us -> 30.4 us
  waiting for transfers between devices: 28.5 us -> 27.4 us
    unnamed x8 -> x2, local copies, waits for them, and re-layouts: 3.97 us -> 1.32 us
    pallas_call x1, Pallas kernels: 0.46 us -> 2.73 us  [pair_shards(): call(prepare_kernel, [(FIELDS,) + labels.shape, (count * mid, LANES)] + [...]
    ppermute x6, waiting for transfers between devices: 12 us -> 10.9 us  [send(): return lax.ppermute(block, ('grow', 'cy', 'cz'), pairs)]
where the time goes in v4:
time: 71.6 us; the launch traced here: 71.4 us
  Pallas kernels  30.4 us (42%)
  waiting for transfers between devices  27.4 us (38%)
  starting transfers between devices  11.6 us (16%)
  local copies, waits for them, and re-layouts  1.32 us (2%)
    pallas_call x1, Pallas kernels, pair_shards(): call(steps_kernel, [(FIELDS, slab, rows, LANES), (count * mid, LANES)], [...  25.3 us
    ppermute x1, waiting for transfers between devices, from_behind(): return lax.ppermute(block, axis, route)  16.5 us
    ppermute x6, waiting for transfers between devices, send(): return lax.ppermute(block, ('grow', 'cy', 'cz'), pairs)  10.9 us
    ppermute x6, starting transfers between devices, send(): return lax.ppermute(block, ('grow', 'cy', 'cz'), pairs)  10.3 us
    pallas_call x1, Pallas kernels, pair_shards(): call(prepare_kernel, [(FIELDS,) + labels.shape, (count * mid, LANES)] + [...  2.73 us
  transfers between devices with their start and end apart: 7, of which 5 were waited for; matrix products, arithmetic and copies ran while one was open for 0% of the time, Pallas kernels for 2%

profile of v4, /device:TPU:0, one launch (start us, length us, event | category | flops | bytes accessed | tf_op | source)
XLA Modules:
  0.0 71.4 jit_solution(15051977674415686907)
XLA Ops:
  0.6 2.7 %shard_map.67 = (f32[5,4,128,128]{3,2,1,0:T(8,128)}, f32[1280,128]{1,0:T(8,128)}, f32[160,128]{1,0:T(8,128)}, f32[160,128]{1,0:T(8,128)}) custom-call(s32[4,128,128]{2,1,0:T(8,128)} %labels.1, f32[4,128,128]{2,1,0:T(8,128)} %roughness.1, f32[4,128,128]{2,1,0:T(8,128)} %potential.1, f32[3,4,128,128]{3,2,1,0:T(8,128)} %displacement.1), custom_call_target="tpu_custom_call" | custom-call | tf_op jit(solution)/shard_map/pallas_call | solution.py:632
  3.4 3.0 %collective-permute-start.2 = (f32[1280,128]{1,0:T(8,128)}, f32[1280,128]{1,0:T(8,128)S(1)}, u32[]{:S(2)}, u32[]{:S(2)}) collective-permute-start(f32[1280,128]{1,0:T(8,128)} %get-tuple-element.15), channel_id=1, source_target_pairs={{0,16},{1,17},{2,18},{3,19},{4,20},{5,21},{6,22},{7,23},{8,24},{9,... | collective-permute-start | bytes 1966088 | tf_op jit(solution)/shard_map/ppermute | solution.py:630
  6.4 0.0 collective-permute-start
  6.4 1.7 %collective-permute-start.1 = (f32[160,128]{1,0:T(8,128)}, f32[160,128]{1,0:T(8,128)S(1)}, u32[]{:S(2)}, u32[]{:S(2)}) collective-permute-start(f32[160,128]{1,0:T(8,128)} %get-tuple-element.14), channel_id=1, source_target_pairs={{0,12},{1,13},{2,14},{3,15},{4,0},{5,1},{6,2},{7,3},{8,4},{9,5},{1... | collective-permute-start | bytes 245768 | tf_op jit(solution)/shard_map/ppermute | solution.py:630
  8.1 2.3 %collective-permute-done.above = f32[160,128]{1,0:T(8,128)S(1)} collective-permute-done((f32[160,128]{1,0:T(8,128)}, f32[160,128]{1,0:T(8,128)S(1)}, u32[]{:S(2)}, u32[]{:S(2)}) %collective-permute-start) | collective-permute-done | bytes 81952 | tf_op jit(solution)/shard_map/ppermute | solution.py:630
  10.4 0.0 collective-permute-done.1.below
  10.5 0.0 copy-start
  10.5 1.3 %copy-done = f32[5,4,128,128]{3,2,1,0:T(8,128)S(1)} copy-done((f32[5,4,128,128]{3,2,1,0:T(8,128)S(1)}, f32[5,4,128,128]{3,2,1,0:T(8,128)}, u32[]{:S(2)}) %copy-start) | copy-done | bytes 1310744
  11.8 1.2 %shard_map.68 = (f32[344,128]{1,0:T(8,128)S(1)}, f32[184,128]{1,0:T(8,128)S(1)}, f32[184,128]{1,0:T(8,128)S(1)}) custom-call(f32[5,4,128,128]{3,2,1,0:T(8,128)S(1)} %copy-done, f32[160,128]{1,0:T(8,128)S(1)} %collective-permute-done.above, f32[160,128]{1,0:T(8,128)S(1)} %collective-permute-done.1.below), custom_call_target="tpu_custom_call" | custom-call | tf_op jit(solution)/shard_map/pallas_call | solution.py:643
  13.0 0.6 collective-permute-start.3
  13.6 1.6 %collective-permute-start.4 = (f32[184,128]{1,0:T(8,128)S(1)}, f32[184,128]{1,0:T(8,128)S(1)}, u32[]{:S(2)}, u32[]{:S(2)}) collective-permute-start(f32[184,128]{1,0:T(8,128)S(1)} %get-tuple-element.17), channel_id=1, source_target_pairs={{0,1},{1,2},{2,3},{3,0},{4,5},{5,6},{6,7},{7,4},{8,9},{9,10},{10,1... | collective-permute-start | bytes 282632 | tf_op jit(solution)/shard_map/ppermute | solution.py:630
  15.2 3.4 %collective-permute-start.5 = (f32[184,128]{1,0:T(8,128)S(1)}, f32[184,128]{1,0:T(8,128)S(1)}, u32[]{:S(2)}, u32[]{:S(2)}) collective-permute-start(f32[184,128]{1,0:T(8,128)S(1)} %get-tuple-element.18), channel_id=1, source_target_pairs={{0,19},{1,16},{2,17},{3,18},{4,23},{5,20},{6,21},{7,22},{8,27},{9,... | collective-permute-start | bytes 282632 | tf_op jit(solution)/shard_map/ppermute | solution.py:630
  18.6 1.8 %collective-permute-done.4.same = f32[184,128]{1,0:T(8,128)S(1)} collective-permute-done((f32[184,128]{1,0:T(8,128)S(1)}, f32[184,128]{1,0:T(8,128)S(1)}, u32[]{:S(2)}, u32[]{:S(2)}) %collective-permute-start.4) | collective-permute-done | bytes 94240 | tf_op jit(solution)/shard_map/ppermute | solution.py:630
  20.4 3.3 %collective-permute-done.5.other = f32[184,128]{1,0:T(8,128)S(1)} collective-permute-done((f32[184,128]{1,0:T(8,128)S(1)}, f32[184,128]{1,0:T(8,128)S(1)}, u32[]{:S(2)}, u32[]{:S(2)}) %collective-permute-start.5) | collective-permute-done | bytes 94240 | tf_op jit(solution)/shard_map/ppermute | solution.py:630
  23.7 3.4 %collective-permute-done.3.across = f32[344,128]{1,0:T(8,128)S(1)} collective-permute-done((f32[344,128]{1,0:T(8,128)S(1)}, f32[344,128]{1,0:T(8,128)S(1)}, u32[]{:S(2)}, u32[]{:S(2)}) %collective-permute-start.3) | collective-permute-done | bytes 176160 | tf_op jit(solution)/shard_map/ppermute | solution.py:630
  27.1 0.0 collective-permute-done.2.halves
  27.1 25.3 %shard_map.69 = (f32[5,4,128,128]{3,2,1,0:T(8,128)S(1)}, f32[1280,128]{1,0:T(8,128)S(1)}) custom-call(f32[5,4,128,128]{3,2,1,0:T(8,128)S(1)} %copy-done, f32[160,128]{1,0:T(8,128)S(1)} %collective-permute-done.above, f32[160,128]{1,0:T(8,128)S(1)} %collective-permute-done.1.below, f32[1280,128]{1,0:T(8,128)S(1)} %collective-permute-done.2.halves, ...), custom_call_target="tpu_custom_call" | custom-call | tf_op jit(solution)/shard_map/pallas_call | solution.py:651
  52.4 1.3 %collective-permute-start.6 = (f32[1280,128]{1,0:T(8,128)S(1)}, f32[1280,128]{1,0:T(8,128)S(1)}, u32[]{:S(2)}, u32[]{:S(2)}) collective-permute-start(f32[1280,128]{1,0:T(8,128)S(1)} %get-tuple-element.20), channel_id=1, source_target_pairs={{16,0},{17,1},{18,2},{19,3},{20,4},{21,5},{22,6},{23,7},{24,8},{25... | collective-permute-start | bytes 1966088 | tf_op jit(solution)/shard_map/ppermute | solution.py:47
  53.7 16.5 %collective-permute-done.6.message = f32[1280,128]{1,0:T(8,128)S(1)} collective-permute-done((f32[1280,128]{1,0:T(8,128)S(1)}, f32[1280,128]{1,0:T(8,128)S(1)}, u32[]{:S(2)}, u32[]{:S(2)}) %collective-permute-start.6) | collective-permute-done | bytes 655392 | tf_op jit(solution)/shard_map/ppermute | solution.py:47
  70.2 1.2 %shard_map.70 = (f32[4,128,128]{2,1,0:T(8,128)}, f32[4,128,128]{2,1,0:T(8,128)}, f32[3,4,128,128]{3,2,1,0:T(8,128)}) custom-call(f32[5,4,128,128]{3,2,1,0:T(8,128)S(1)} %get-tuple-element.19.result, f32[1280,128]{1,0:T(8,128)S(1)} %collective-permute-done.6.message), custom_call_target="tpu_custom_call" | custom-call | tf_op jit(solution)/shard_map/pallas_call | solution.py:660
Async XLA Ops:
  3.4 23.7 %collective-permute-start.2 = (f32[1280,128]{1,0:T(8,128)}, f32[1280,128]{1,0:T(8,128)S(1)}, u32[]{:S(2)}, u32[]{:S(2)}) collective-permute-start(f32[1280,128]{1,0:T(8,128)} %get-tuple-element.15), channel_id=1, source_target_pairs={{0,16},{1,17},{2,18},{3,19},{4,20},{5,21},{6,22},{7,23},{8,24},{9,... | collective-permute-start | bytes 1966088 | tf_op jit(solution)/shard_map/ppermute | solution.py:630
  6.4 4.1 %collective-permute-start = (f32[160,128]{1,0:T(8,128)}, f32[160,128]{1,0:T(8,128)S(1)}, u32[]{:S(2)}, u32[]{:S(2)}) collective-permute-start(f32[160,128]{1,0:T(8,128)} %get-tuple-element.13), channel_id=1, source_target_pairs={{0,4},{1,5},{2,6},{3,7},{4,8},{5,9},{6,10},{7,11},{8,12},{9,13},{1... | collective-permute-start | bytes 245768 | tf_op jit(solution)/shard_map/ppermute | solution.py:630
  6.4 4.1 %collective-permute-start.1 = (f32[160,128]{1,0:T(8,128)}, f32[160,128]{1,0:T(8,128)S(1)}, u32[]{:S(2)}, u32[]{:S(2)}) collective-permute-start(f32[160,128]{1,0:T(8,128)} %get-tuple-element.14), channel_id=1, source_target_pairs={{0,12},{1,13},{2,14},{3,15},{4,0},{5,1},{6,2},{7,3},{8,4},{9,5},{1... | collective-permute-start | bytes 245768 | tf_op jit(solution)/shard_map/ppermute | solution.py:630
  10.5 1.3 %copy-start = (f32[5,4,128,128]{3,2,1,0:T(8,128)S(1)}, f32[5,4,128,128]{3,2,1,0:T(8,128)}, u32[]{:S(2)}) copy-start(f32[5,4,128,128]{3,2,1,0:T(8,128)} %get-tuple-element.12.fields) | copy-start | bytes 3932164
  13.0 14.1 %collective-permute-start.3 = (f32[344,128]{1,0:T(8,128)S(1)}, f32[344,128]{1,0:T(8,128)S(1)}, u32[]{:S(2)}, u32[]{:S(2)}) collective-permute-start(f32[344,128]{1,0:T(8,128)S(1)} %get-tuple-element.16), channel_id=1, source_target_pairs={{0,16},{1,17},{2,18},{3,19},{4,20},{5,21},{6,22},{7,23},{8,24},{9,... | collective-permute-start | bytes 528392 | tf_op jit(solution)/shard_map/ppermute | solution.py:630
  13.6 6.8 %collective-permute-start.4 = (f32[184,128]{1,0:T(8,128)S(1)}, f32[184,128]{1,0:T(8,128)S(1)}, u32[]{:S(2)}, u32[]{:S(2)}) collective-permute-start(f32[184,128]{1,0:T(8,128)S(1)} %get-tuple-element.17), channel_id=1, source_target_pairs={{0,1},{1,2},{2,3},{3,0},{4,5},{5,6},{6,7},{7,4},{8,9},{9,10},{10,1... | collective-permute-start | bytes 282632 | tf_op jit(solution)/shard_map/ppermute | solution.py:630
  15.2 8.5 %collective-permute-start.5 = (f32[184,128]{1,0:T(8,128)S(1)}, f32[184,128]{1,0:T(8,128)S(1)}, u32[]{:S(2)}, u32[]{:S(2)}) collective-permute-start(f32[184,128]{1,0:T(8,128)S(1)} %get-tuple-element.18), channel_id=1, source_target_pairs={{0,19},{1,16},{2,17},{3,18},{4,23},{5,20},{6,21},{7,22},{8,27},{9,... | collective-permute-start | bytes 282632 | tf_op jit(solution)/shard_map/ppermute | solution.py:630
  52.4 17.8 %collective-permute-start.6 = (f32[1280,128]{1,0:T(8,128)S(1)}, f32[1280,128]{1,0:T(8,128)S(1)}, u32[]{:S(2)}, u32[]{:S(2)}) collective-permute-start(f32[1280,128]{1,0:T(8,128)S(1)} %get-tuple-element.20), channel_id=1, source_target_pairs={{16,0},{17,1},{18,2},{19,3},{20,4},{21,5},{22,6},{23,7},{24,8},{25... | collective-permute-start | bytes 1966088 | tf_op jit(solution)/shard_map/ppermute | solution.py:47

commit v5 on v4

--- a/solution.py
+++ b/solution.py
@@ -214,7 +214,8 @@
 REACH = STEPS * (SWEEPS + 1)
 TILE = 8
 FIELDS = 5
-LAG = 99
+LAG = 2
+TOGETHER = 6
 
 
 def lanes(shape):
@@ -396,23 +397,29 @@
                 ref[plane, 1 + row] = natural[field, plane, pl.ds(row, TILE, stride=segment), :]
         close(ref)
 
+    def one_row(row, bodies):
+        waiting = []
+        running = [body(row) for body in bodies]
+        while running:
+            for body in list(running):
+                stores = next(body, None)
+                if stores is None:
+                    running.remove(body)
+                else:
+                    waiting.append(stores)
+            while len(waiting) > LAG * len(bodies) or (waiting and not running):
+                for ref, lead, value in waiting.pop(0):
+                    ref[lead + (row,)] = value
+
     def over_rows(*bodies):
-        def one(row, carry):
-            waiting = []
-            running = [body(row) for body in bodies]
-            while running:
-                for body in list(running):
-                    stores = next(body, None)
-                    if stores is None:
-                        running.remove(body)
-                    else:
-                        waiting.append(stores)
-                while len(waiting) > LAG * len(bodies) or (waiting and not running):
-                    for ref, lead, value in waiting.pop(0):
-                        ref[lead + (row,)] = value
+        together = max(n for n in range(1, TOGETHER + 1) if segment % n == 0)
+
+        def some(turn, carry):
+            for more in range(together):
+                one_row(1 + turn * together + more, bodies)
             return carry
 
-        lax.fori_loop(1, segment + 1, one, 0)
+        lax.fori_loop(0, segment // together, some, 0)
 
     def up(block):
         return pltpu.roll(block, LANES - 1, 1)

time: 71.6 us -> 60.9 us (0.85)
  Pallas kernels: 30.4 us -> 19.7 us
    pallas_call x1, Pallas kernels: 25.3 us -> 14.5 us  [pair_shards(): call(steps_kernel, [(FIELDS, slab, rows, LANES), (count * mid, LANES)], [...]
where the time goes in v5:
time: 60.9 us; the launch traced here: 60.7 us
  waiting for transfers between devices  27.4 us (45%)
  Pallas kernels  19.7 us (32%)
  starting transfers between devices  11.6 us (19%)
  local copies, waits for them, and re-layouts  1.32 us (2%)
  between operations  0.66 us (1%)
    ppermute x1, waiting for transfers between devices, from_behind(): return lax.ppermute(block, axis, route)  16.5 us
    pallas_call x1, Pallas kernels, pair_shards(): call(steps_kernel, [(FIELDS, slab, rows, LANES), (count * mid, LANES)], [...  14.5 us
    ppermute x6, waiting for transfers between devices, send(): return lax.ppermute(block, ('grow', 'cy', 'cz'), pairs)  10.9 us
    ppermute x6, starting transfers between devices, send(): return lax.ppermute(block, ('grow', 'cy', 'cz'), pairs)  10.3 us
    pallas_call x1, Pallas kernels, pair_shards(): call(prepare_kernel, [(FIELDS,) + labels.shape, (count * mid, LANES)] + [...  2.73 us
    unnamed x2, local copies, waits for them, and re-layouts  1.32 us
    ppermute x1, starting transfers between devices, from_behind(): return lax.ppermute(block, axis, route)  1.29 us
    pallas_call x1, Pallas kernels, pair_shards(): call(rims_kernel, [(count * TILE + extra, LANES), (extra, LANES), (extra,...  1.22 us
  transfers between devices with their start and end apart: 7, of which 5 were waited for; matrix products, arithmetic and copies ran while one was open for 0% of the time, Pallas kernels for 2%

profile of v5, /device:TPU:0, one launch (start us, length us, event | category | flops | bytes accessed | tf_op | source)
XLA Modules:
  0.0 60.7 jit_solution(13585463316487615989)
XLA Ops:
  0.6 2.7 %shard_map.67 = (f32[5,4,128,128]{3,2,1,0:T(8,128)}, f32[1280,128]{1,0:T(8,128)}, f32[160,128]{1,0:T(8,128)}, f32[160,128]{1,0:T(8,128)}) custom-call(s32[4,128,128]{2,1,0:T(8,128)} %labels.1, f32[4,128,128]{2,1,0:T(8,128)} %roughness.1, f32[4,128,128]{2,1,0:T(8,128)} %potential.1, f32[3,4,128,128]{3,2,1,0:T(8,128)} %displacement.1), custom_call_target="tpu_custom_call" | custom-call | tf_op jit(solution)/shard_map/pallas_call | solution.py:639
  3.4 3.0 %collective-permute-start.2 = (f32[1280,128]{1,0:T(8,128)}, f32[1280,128]{1,0:T(8,128)S(1)}, u32[]{:S(2)}, u32[]{:S(2)}) collective-permute-start(f32[1280,128]{1,0:T(8,128)} %get-tuple-element.15), channel_id=1, source_target_pairs={{0,16},{1,17},{2,18},{3,19},{4,20},{5,21},{6,22},{7,23},{8,24},{9,... | collective-permute-start | bytes 1966088 | tf_op jit(solution)/shard_map/ppermute | solution.py:637
  6.4 0.0 collective-permute-start
  6.4 1.7 %collective-permute-start.1 = (f32[160,128]{1,0:T(8,128)}, f32[160,128]{1,0:T(8,128)S(1)}, u32[]{:S(2)}, u32[]{:S(2)}) collective-permute-start(f32[160,128]{1,0:T(8,128)} %get-tuple-element.14), channel_id=1, source_target_pairs={{0,12},{1,13},{2,14},{3,15},{4,0},{5,1},{6,2},{7,3},{8,4},{9,5},{1... | collective-permute-start | bytes 245768 | tf_op jit(solution)/shard_map/ppermute | solution.py:637
  8.1 2.3 %collective-permute-done.above = f32[160,128]{1,0:T(8,128)S(1)} collective-permute-done((f32[160,128]{1,0:T(8,128)}, f32[160,128]{1,0:T(8,128)S(1)}, u32[]{:S(2)}, u32[]{:S(2)}) %collective-permute-start) | collective-permute-done | bytes 81952 | tf_op jit(solution)/shard_map/ppermute | solution.py:637
  10.4 0.0 collective-permute-done.1.below
  10.5 0.0 copy-start
  10.5 1.3 %copy-done = f32[5,4,128,128]{3,2,1,0:T(8,128)S(1)} copy-done((f32[5,4,128,128]{3,2,1,0:T(8,128)S(1)}, f32[5,4,128,128]{3,2,1,0:T(8,128)}, u32[]{:S(2)}) %copy-start) | copy-done | bytes 1310744
  11.8 1.2 %shard_map.68 = (f32[344,128]{1,0:T(8,128)S(1)}, f32[184,128]{1,0:T(8,128)S(1)}, f32[184,128]{1,0:T(8,128)S(1)}) custom-call(f32[5,4,128,128]{3,2,1,0:T(8,128)S(1)} %copy-done, f32[160,128]{1,0:T(8,128)S(1)} %collective-permute-done.above, f32[160,128]{1,0:T(8,128)S(1)} %collective-permute-done.1.below), custom_call_target="tpu_custom_call" | custom-call | tf_op jit(solution)/shard_map/pallas_call | solution.py:650
  13.0 0.6 collective-permute-start.3
  13.6 1.6 %collective-permute-start.4 = (f32[184,128]{1,0:T(8,128)S(1)}, f32[184,128]{1,0:T(8,128)S(1)}, u32[]{:S(2)}, u32[]{:S(2)}) collective-permute-start(f32[184,128]{1,0:T(8,128)S(1)} %get-tuple-element.17), channel_id=1, source_target_pairs={{0,1},{1,2},{2,3},{3,0},{4,5},{5,6},{6,7},{7,4},{8,9},{9,10},{10,1... | collective-permute-start | bytes 282632 | tf_op jit(solution)/shard_map/ppermute | solution.py:637
  15.2 3.4 %collective-permute-start.5 = (f32[184,128]{1,0:T(8,128)S(1)}, f32[184,128]{1,0:T(8,128)S(1)}, u32[]{:S(2)}, u32[]{:S(2)}) collective-permute-start(f32[184,128]{1,0:T(8,128)S(1)} %get-tuple-element.18), channel_id=1, source_target_pairs={{0,19},{1,16},{2,17},{3,18},{4,23},{5,20},{6,21},{7,22},{8,27},{9,... | collective-permute-start | bytes 282632 | tf_op jit(solution)/shard_map/ppermute | solution.py:637
  18.6 1.8 %collective-permute-done.4.same = f32[184,128]{1,0:T(8,128)S(1)} collective-permute-done((f32[184,128]{1,0:T(8,128)S(1)}, f32[184,128]{1,0:T(8,128)S(1)}, u32[]{:S(2)}, u32[]{:S(2)}) %collective-permute-start.4) | collective-permute-done | bytes 94240 | tf_op jit(solution)/shard_map/ppermute | solution.py:637
  20.4 3.3 %collective-permute-done.5.other = f32[184,128]{1,0:T(8,128)S(1)} collective-permute-done((f32[184,128]{1,0:T(8,128)S(1)}, f32[184,128]{1,0:T(8,128)S(1)}, u32[]{:S(2)}, u32[]{:S(2)}) %collective-permute-start.5) | collective-permute-done | bytes 94240 | tf_op jit(solution)/shard_map/ppermute | solution.py:637
  23.7 3.4 %collective-permute-done.3.across = f32[344,128]{1,0:T(8,128)S(1)} collective-permute-done((f32[344,128]{1,0:T(8,128)S(1)}, f32[344,128]{1,0:T(8,128)S(1)}, u32[]{:S(2)}, u32[]{:S(2)}) %collective-permute-start.3) | collective-permute-done | bytes 176160 | tf_op jit(solution)/shard_map/ppermute | solution.py:637
  27.1 0.0 collective-permute-done.2.halves
  27.1 14.5 %shard_map.69 = (f32[5,4,128,128]{3,2,1,0:T(8,128)S(1)}, f32[1280,128]{1,0:T(8,128)S(1)}) custom-call(f32[5,4,128,128]{3,2,1,0:T(8,128)S(1)} %copy-done, f32[160,128]{1,0:T(8,128)S(1)} %collective-permute-done.above, f32[160,128]{1,0:T(8,128)S(1)} %collective-permute-done.1.below, f32[1280,128]{1,0:T(8,128)S(1)} %collective-permute-done.2.halves, ...), custom_call_target="tpu_custom_call" | custom-call | tf_op jit(solution)/shard_map/pallas_call | solution.py:658
  41.6 1.3 %collective-permute-start.6 = (f32[1280,128]{1,0:T(8,128)S(1)}, f32[1280,128]{1,0:T(8,128)S(1)}, u32[]{:S(2)}, u32[]{:S(2)}) collective-permute-start(f32[1280,128]{1,0:T(8,128)S(1)} %get-tuple-element.20), channel_id=1, source_target_pairs={{16,0},{17,1},{18,2},{19,3},{20,4},{21,5},{22,6},{23,7},{24,8},{25... | collective-permute-start | bytes 1966088 | tf_op jit(solution)/shard_map/ppermute | solution.py:47
  42.9 16.5 %collective-permute-done.6.message = f32[1280,128]{1,0:T(8,128)S(1)} collective-permute-done((f32[1280,128]{1,0:T(8,128)S(1)}, f32[1280,128]{1,0:T(8,128)S(1)}, u32[]{:S(2)}, u32[]{:S(2)}) %collective-permute-start.6) | collective-permute-done | bytes 655392 | tf_op jit(solution)/shard_map/ppermute | solution.py:47
  59.4 1.2 %shard_map.70 = (f32[4,128,128]{2,1,0:T(8,128)}, f32[4,128,128]{2,1,0:T(8,128)}, f32[3,4,128,128]{3,2,1,0:T(8,128)}) custom-call(f32[5,4,128,128]{3,2,1,0:T(8,128)S(1)} %get-tuple-element.19.result, f32[1280,128]{1,0:T(8,128)S(1)} %collective-permute-done.6.message), custom_call_target="tpu_custom_call" | custom-call | tf_op jit(solution)/shard_map/pallas_call | solution.py:667
Async XLA Ops:
  3.4 23.7 %collective-permute-start.2 = (f32[1280,128]{1,0:T(8,128)}, f32[1280,128]{1,0:T(8,128)S(1)}, u32[]{:S(2)}, u32[]{:S(2)}) collective-permute-start(f32[1280,128]{1,0:T(8,128)} %get-tuple-element.15), channel_id=1, source_target_pairs={{0,16},{1,17},{2,18},{3,19},{4,20},{5,21},{6,22},{7,23},{8,24},{9,... | collective-permute-start | bytes 1966088 | tf_op jit(solution)/shard_map/ppermute | solution.py:637
  6.4 4.1 %collective-permute-start = (f32[160,128]{1,0:T(8,128)}, f32[160,128]{1,0:T(8,128)S(1)}, u32[]{:S(2)}, u32[]{:S(2)}) collective-permute-start(f32[160,128]{1,0:T(8,128)} %get-tuple-element.13), channel_id=1, source_target_pairs={{0,4},{1,5},{2,6},{3,7},{4,8},{5,9},{6,10},{7,11},{8,12},{9,13},{1... | collective-permute-start | bytes 245768 | tf_op jit(solution)/shard_map/ppermute | solution.py:637
  6.4 4.1 %collective-permute-start.1 = (f32[160,128]{1,0:T(8,128)}, f32[160,128]{1,0:T(8,128)S(1)}, u32[]{:S(2)}, u32[]{:S(2)}) collective-permute-start(f32[160,128]{1,0:T(8,128)} %get-tuple-element.14), channel_id=1, source_target_pairs={{0,12},{1,13},{2,14},{3,15},{4,0},{5,1},{6,2},{7,3},{8,4},{9,5},{1... | collective-permute-start | bytes 245768 | tf_op jit(solution)/shard_map/ppermute | solution.py:637
  10.5 1.3 %copy-start = (f32[5,4,128,128]{3,2,1,0:T(8,128)S(1)}, f32[5,4,128,128]{3,2,1,0:T(8,128)}, u32[]{:S(2)}) copy-start(f32[5,4,128,128]{3,2,1,0:T(8,128)} %get-tuple-element.12.fields) | copy-start | bytes 3932164
  13.0 14.1 %collective-permute-start.3 = (f32[344,128]{1,0:T(8,128)S(1)}, f32[344,128]{1,0:T(8,128)S(1)}, u32[]{:S(2)}, u32[]{:S(2)}) collective-permute-start(f32[344,128]{1,0:T(8,128)S(1)} %get-tuple-element.16), channel_id=1, source_target_pairs={{0,16},{1,17},{2,18},{3,19},{4,20},{5,21},{6,22},{7,23},{8,24},{9,... | collective-permute-start | bytes 528392 | tf_op jit(solution)/shard_map/ppermute | solution.py:637
  13.6 6.8 %collective-permute-start.4 = (f32[184,128]{1,0:T(8,128)S(1)}, f32[184,128]{1,0:T(8,128)S(1)}, u32[]{:S(2)}, u32[]{:S(2)}) collective-permute-start(f32[184,128]{1,0:T(8,128)S(1)} %get-tuple-element.17), channel_id=1, source_target_pairs={{0,1},{1,2},{2,3},{3,0},{4,5},{5,6},{6,7},{7,4},{8,9},{9,10},{10,1... | collective-permute-start | bytes 282632 | tf_op jit(solution)/shard_map/ppermute | solution.py:637
  15.2 8.5 %collective-permute-start.5 = (f32[184,128]{1,0:T(8,128)S(1)}, f32[184,128]{1,0:T(8,128)S(1)}, u32[]{:S(2)}, u32[]{:S(2)}) collective-permute-start(f32[184,128]{1,0:T(8,128)S(1)} %get-tuple-element.18), channel_id=1, source_target_pairs={{0,19},{1,16},{2,17},{3,18},{4,23},{5,20},{6,21},{7,22},{8,27},{9,... | collective-permute-start | bytes 282632 | tf_op jit(solution)/shard_map/ppermute | solution.py:637
  41.6 17.8 %collective-permute-start.6 = (f32[1280,128]{1,0:T(8,128)S(1)}, f32[1280,128]{1,0:T(8,128)S(1)}, u32[]{:S(2)}, u32[]{:S(2)}) collective-permute-start(f32[1280,128]{1,0:T(8,128)S(1)} %get-tuple-element.20), channel_id=1, source_target_pairs={{16,0},{17,1},{18,2},{19,3},{20,4},{21,5},{22,6},{23,7},{24,8},{25... | collective-permute-start | bytes 1966088 | tf_op jit(solution)/shard_map/ppermute | solution.py:47

commit v6 on v5

--- a/solution.py
+++ b/solution.py
@@ -1,3 +1,5 @@
+import functools
+
 import jax
 import jax.numpy as jnp
 from jax import lax
@@ -215,7 +217,7 @@
 TILE = 8
 FIELDS = 5
 LAG = 2
-TOGETHER = 6
+TOGETHER = 10
 
 
 def lanes(shape):
@@ -237,6 +239,18 @@
 def half_of(side):
     low = lanes((TILE, LANES)) < LANES // 2
     return jnp.logical_xor(low, side == 1)
+
+
+def pack_halves(fields, start, theirs, out):
+    _, slab, _, _ = fields.shape
+    mid = out.shape[0] // (FIELDS * slab)
+    for field in range(FIELDS):
+        for plane in range(slab):
+            for row in range(0, mid, TILE):
+                upper = fields[field, plane, pl.ds(start + row, TILE), :]
+                lower = fields[field, plane, pl.ds(start + mid + row, TILE), :]
+                to = pl.ds((field * slab + plane) * mid + row, TILE)
+                out[to, :] = jnp.where(theirs, upper, turned(lower, LANES // 2))
 
 
 def prepare_kernel(
@@ -244,7 +258,6 @@
 ):
     _, slab, rows, _ = fields.shape
     theirs = jnp.logical_not(half_of(lax.axis_index("grow")))
-    mid = rows // 2
     copies = [
         pltpu.make_async_copy(source, target, arrived.at[which])
         for which, (source, target) in enumerate(
@@ -268,13 +281,10 @@
             fields[(0,) + spot] = mark * (1.0 - part) + (1.0 - mark) * part
     for copy in copies[2:]:
         copy.wait()
+    pack_halves(fields, 0, theirs, halves)
     for field in range(FIELDS):
         for plane in range(slab):
             which = field * slab + plane
-            for row in range(0, mid, TILE):
-                upper = fields[field, plane, pl.ds(row, TILE), :]
-                lower = turned(fields[field, plane, pl.ds(row + mid, TILE), :], LANES // 2)
-                halves[pl.ds(which * mid + row, TILE), :] = jnp.where(theirs, upper, lower)
             first[pl.ds(which * TILE, TILE), :] = fields[field, plane, pl.ds(0, TILE), :]
             last[pl.ds(which * TILE, TILE), :] = fields[field, plane, pl.ds(rows - TILE, TILE), :]
 
@@ -329,59 +339,102 @@
     strips(fields, above, below, outer * side, other, 0)
 
 
+def rest_kernel(fields, across, other, early, near_a, near_b, rest):
+    pack_halves(
+        fields,
+        fields.shape[2] - 2 * (rest.shape[0] // (FIELDS * fields.shape[1])),
+        jnp.logical_not(half_of(lax.axis_index("grow"))),
+        rest,
+    )
+
+
+def own_kernel(fields, above, below, same, part_a, part_b, natural):
+    _, slab, rows, _ = fields.shape
+    side = lax.axis_index("grow")
+    count = FIELDS * slab
+    per = LANES // REACH
+    outer = (LANES - REACH) * (1 - side)
+    in_outer = from_lane(outer)
+    segment = part_a.shape[2] - 2
+    for field in range(FIELDS):
+        for plane in range(slab):
+            which = field * slab + plane
+            spot = pl.ds(which * TILE, TILE)
+            for at in range(0, rows + 2 * REACH, TILE):
+                row = at - REACH
+                if 0 <= row < rows:
+                    near = fields[field, plane, pl.ds(row, TILE), :]
+                    piece, group = same[spot, :], row // TILE
+                else:
+                    end = int(row > 0)
+                    near = (below if end else above)[spot, :]
+                    extra, group = divmod(2 * which + end, per)
+                    piece = same[pl.ds((count + extra) * TILE, TILE), :]
+                piece = turned(piece, outer - group * REACH)
+                natural[which, pl.ds(at, TILE), :] = jnp.where(in_outer, piece, near)
+            for start, part in ((0, part_a), (rows // 2, part_b)):
+                blocks = [
+                    natural[which, pl.ds(start + row, TILE, stride=segment), :]
+                    for row in range(segment)
+                ]
+                blocks = [
+                    pltpu.roll(blocks[-1], 1, 0),
+                    *blocks,
+                    pltpu.roll(blocks[0], TILE - 1, 0),
+                ]
+                for row, block in enumerate(blocks):
+                    part[field, plane, row] = block
+
+
 def conduct_of(step):
     return COND_EL + COND_LI * step
 
 
-def steps_kernel(
-    fields, above, below, halves, across, same, other, result, message,
-    natural, phase, phase_new, pot, pot_new, disp, disp_new,
-    slopes, slopes_y, cond_x, cond_y, cond_y_back, cond_z,
-):
-    _, slab, rows, _ = fields.shape
+def steps_kernel(part, near, across, other, *refs):
+    halves, refs = refs[: 1 + part], refs[1 + 2 * part :]
+    result, message, natural, phase, phase_new, pot, pot_new, disp, disp_new = refs[:9]
+    slopes, slopes_y, cond_x, cond_y, cond_y_back, cond_z = refs[9:]
+    _, slab, rows, _ = result.shape
+    all_rows = 2 * rows
     planes = 2 * slab
     side = lax.axis_index("grow")
     mine = half_of(side)
     mid = rows // 2
     count = FIELDS * slab
-    groups = rows // TILE
     per = LANES // REACH
     inner = LANES // 2 - REACH * side
     outer = (LANES - REACH) * (1 - side)
     in_inner, in_outer = from_lane(inner), from_lane(outer)
     segment = phase.shape[1] - 2
 
+    def arrived_half(which, row):
+        for ref in halves:
+            half = ref.shape[0] // count
+            if row < 2 * half:
+                block = ref[pl.ds(which * half + row % half, TILE), :]
+                return turned(block, LANES // 2) if row >= half else block
+            row -= 2 * half
+
     for field in range(FIELDS):
         for plane in range(slab):
             which = field * slab + plane
-            own, far = side * slab + plane, (1 - side) * slab + plane
-            spot = pl.ds(which * TILE, TILE)
-            from_same, from_other = same[spot, :], other[spot, :]
-            strip = across[pl.ds((count + which) * TILE, TILE), :]
-            for group in range(groups):
-                row = group * TILE
-                to = pl.ds(REACH + row, TILE)
-                near = fields[field, plane, pl.ds(row, TILE), :]
+            for at in range(0, rows + 2 * REACH, TILE):
+                row = part * rows + at - REACH
+                if 0 <= row < all_rows:
+                    spot, group = pl.ds(which * TILE, TILE), row // TILE
+                    strip = across[pl.ds((count + which) * TILE, TILE), :]
+                    block = arrived_half(which, row)
+                else:
+                    end = int(row > 0)
+                    extra, group = divmod(2 * which + end, per)
+                    spot = pl.ds((count + extra) * TILE, TILE)
+                    strip = across[pl.ds((2 * count + extra) * TILE, TILE), :]
+                    block = across[pl.ds(which * TILE, TILE), :]
+                    block = turned(block, LANES // 2) if end else block
+                block = jnp.where(in_inner, turned(strip, inner - group * REACH), block)
                 back = outer - group * REACH
-                natural[field, own, to, :] = jnp.where(in_outer, turned(from_same, back), near)
-                block = halves[pl.ds(which * mid + row % mid, TILE), :]
-                if row >= mid:
-                    block = turned(block, LANES // 2)
-                block = jnp.where(in_inner, turned(strip, inner - group * REACH), block)
-                natural[field, far, to, :] = jnp.where(in_outer, turned(from_other, back), block)
-            rim = across[spot, :]
-            for end, to in ((0, pl.ds(0, TILE)), (1, pl.ds(REACH + rows, TILE))):
-                at, group = divmod(2 * which + end, per)
-                extra = pl.ds((count + at) * TILE, TILE)
-                back = outer - group * REACH
-                near = (below if end else above)[spot, :]
-                block = jnp.where(in_outer, turned(same[extra, :], back), near)
-                natural[field, own, to, :] = block
-                block = turned(rim, LANES // 2) if end else rim
-                strip = across[pl.ds((2 * count + at) * TILE, TILE), :]
-                block = jnp.where(in_inner, turned(strip, inner - group * REACH), block)
-                block = jnp.where(in_outer, turned(other[extra, :], back), block)
-                natural[field, far, to, :] = block
+                block = jnp.where(in_outer, turned(other[spot, :], back), block)
+                natural[field, plane, pl.ds(at, TILE), :] = block
 
     def parts_of(phase, pot, disp):
         return (phase, pot, disp.at[0], disp.at[1], disp.at[2])
@@ -392,10 +445,14 @@
             ref[plane, segment + 1] = pltpu.roll(ref[plane, 1], TILE - 1, 0)
 
     for field, ref in enumerate(parts_of(phase, pot, disp)):
-        for plane in range(planes):
+        for plane in range(slab):
+            own, far = side * slab + plane, (1 - side) * slab + plane
+            for row in range(segment + 2):
+                ref[own, row] = near[field, plane, row]
             for row in range(segment):
-                ref[plane, 1 + row] = natural[field, plane, pl.ds(row, TILE, stride=segment), :]
-        close(ref)
+                ref[far, 1 + row] = natural[field, plane, pl.ds(row, TILE, stride=segment), :]
+            ref[far, 0] = pltpu.roll(ref[far, segment], 1, 0)
+            ref[far, segment + 1] = pltpu.roll(ref[far, 1], TILE - 1, 0)
 
     def one_row(row, bodies):
         waiting = []
@@ -419,7 +476,10 @@
                 one_row(1 + turn * together + more, bodies)
             return carry
 
-        lax.fori_loop(0, segment // together, some, 0)
+        if together == segment:
+            some(0, 0)
+        else:
+            lax.fori_loop(0, segment // together, some, 0)
 
     def up(block):
         return pltpu.roll(block, LANES - 1, 1)
@@ -585,22 +645,24 @@
                 message[to, :] = jnp.where(mine, upper, turned(lower, LANES // 2))
 
 
-def finish_kernel(result, message, phase, potential, displacement):
-    _, slab, rows, _ = result.shape
+def finish_kernel(result_a, result_b, message_a, message_b, phase, potential, displacement):
+    slab, rows = result_a.shape[1:3]
     side = lax.axis_index("grow")
     mine = half_of(side)
     fresh = side == lax.axis_size("grow") - 1
     mid = rows // 2
-    for field in range(FIELDS):
-        out = (phase, potential, displacement, displacement, displacement)[field]
-        for plane in range(slab):
-            for row in range(0, mid, TILE):
-                block = message[pl.ds((field * slab + plane) * mid + row, TILE), :]
-                for place, piece in ((row, block), (row + mid, turned(block, LANES // 2))):
-                    spot = (plane, pl.ds(place, TILE), slice(None))
-                    whole = jnp.where(mine, result[(field,) + spot], piece)
-                    whole = jnp.where(fresh, V_HIGH if field == 1 else 0.0, whole)
-                    out[spot if field < 2 else (field - 2,) + spot] = whole
+    for part, (result, message) in enumerate(((result_a, message_a), (result_b, message_b))):
+        for field in range(FIELDS):
+            out = (phase, potential, displacement, displacement, displacement)[field]
+            for plane in range(slab):
+                for row in range(0, mid, TILE):
+                    block = message[pl.ds((field * slab + plane) * mid + row, TILE), :]
+                    for place, piece in ((row, block), (row + mid, turned(block, LANES // 2))):
+                        own = result[field, plane, pl.ds(place, TILE), :]
+                        whole = jnp.where(mine, own, piece)
+                        whole = jnp.where(fresh, V_HIGH if field == 1 else 0.0, whole)
+                        spot = (plane, pl.ds(part * rows + place, TILE), slice(None))
+                        out[spot if field < 2 else (field - 2,) + spot] = whole
 
 
 def call(kernel, outs, scratch=(), limit=48, **how):
@@ -610,7 +672,7 @@
         scratch_shapes=[
             pltpu.VMEM(one, jnp.float32) if isinstance(one, tuple) else one for one in scratch
         ],
-        **how,
+        **{"cost_estimate": pl.CostEstimate(flops=1, bytes_accessed=1, transcendentals=0), **how},
         compiler_params=pltpu.CompilerParams(vmem_limit_bytes=limit * 1024 * 1024),
     )
 
@@ -618,7 +680,8 @@
 def pair_shards(labels, roughness, potential, displacement):
     slab, rows, _ = labels.shape
     count = FIELDS * slab
-    mid = rows // 2
+    early = (rows // TILE // 2 + 2) // 2 * TILE
+    late = rows // 2 - early
     sizes = {name: lax.axis_size(name) for name in ("grow", "cy", "cz")}
 
     def index(grow, cy, cz):
@@ -638,38 +701,58 @@
 
     fields, halves, first, last = call(
         prepare_kernel,
-        [(FIELDS,) + labels.shape, (count * mid, LANES)] + [(count * TILE, LANES)] * 2,
+        [(FIELDS,) + labels.shape, (count * early, LANES)] + [(count * TILE, LANES)] * 2,
         [pltpu.VMEM(labels.shape, labels.dtype), labels.shape, pltpu.SemaphoreType.DMA((4,))],
         limit=54,
         in_specs=[pl.BlockSpec(memory_space=pltpu.HBM)] * 4,
     )(labels, roughness, potential, displacement)
-    halves = send(halves, lambda grow, cy, cz: (1 - grow, cy, cz))
+    halves = [send(halves, lambda grow, cy, cz: (1 - grow, cy, cz))]
     above = send(last, lambda grow, cy, cz: (grow, cy + 1, cz))
     below = send(first, lambda grow, cy, cz: (grow, cy - 1, cz))
     extra = rim_rows(slab)
     across, same, other = call(
-        rims_kernel, [(count * TILE + extra, LANES), (extra, LANES), (extra, LANES)]
+        rims_kernel, [(count * TILE + extra, LANES)] + [(extra, LANES)] * 2
     )(fields, above, below)
     across = send(across, lambda grow, cy, cz: (1 - grow, cy, cz))
     same = send(same, lambda grow, cy, cz: (grow, cy, cz - 1 if grow else cz + 1))
     other = send(other, lambda grow, cy, cz: (1 - grow, cy, cz + 1 if grow else cz - 1))
-    span = rows + 2 * REACH
+    span = rows // 2 + 2 * REACH
+    near = (FIELDS, slab, span // TILE + 2, TILE, LANES)
+    near = call(own_kernel, [near, near], [(count, rows + 2 * REACH, LANES)])(
+        fields, above, below, same
+    )
     deep = (2 * slab, span // TILE + 2, TILE, LANES)
-    result, message = call(
-        steps_kernel,
-        [(FIELDS, slab, rows, LANES), (count * mid, LANES)],
-        [(FIELDS, 2 * slab, span, LANES)]
-        + [deep] * 4
-        + [(3,) + deep] * 2
-        + [deep, deep, (2 * slab + 1,) + deep[1:], deep, deep, deep],
-    )(fields, above, below, halves, across, same, other)
-    message = from_behind(message, "grow", -1)
-    return call(finish_kernel, [labels.shape, labels.shape, displacement.shape])(result, message)
+    results, messages = [], []
+    in_vmem, anywhere = (pl.BlockSpec(memory_space=space) for space in (pltpu.VMEM, pl.ANY))
+    (rest,) = call(rest_kernel, [(count * late, LANES)], in_specs=[in_vmem] + [anywhere] * 5)(
+        fields, across, other, *halves, *near
+    )
+    halves.append(send(rest, lambda grow, cy, cz: (1 - grow, cy, cz)))
+    for part in range(2):
+        result, message = call(
+            functools.partial(steps_kernel, part),
+            [(FIELDS, slab, rows // 2, LANES), (count * rows // 4, LANES)],
+            [(FIELDS, slab, span, LANES)]
+            + [deep] * 4
+            + [(3,) + deep] * 2
+            + [deep, deep, (2 * slab + 1,) + deep[1:], deep, deep, deep],
+            in_specs=[in_vmem] * (4 + part) + [anywhere] * part,
+            cost_estimate=pl.CostEstimate(
+                flops=STEPS * SWEEPS * 160 * span * 2 * slab * LANES,
+                bytes_accessed=STEPS * SWEEPS * 40 * span * 2 * slab * LANES,
+                transcendentals=STEPS * 2 * span * 2 * slab * LANES,
+            ),
+        )(near[part], across, other, *halves[: 1 + part], *results)
+        results.append(result)
+        messages.append(from_behind(message, "grow", -1))
+    return call(finish_kernel, [labels.shape, labels.shape, displacement.shape])(
+        *results, *messages
+    )
 
 
 def fits_pair(labels):
     rows, columns = labels.shape[1:]
-    blocks = rows % (2 * TILE) == 0 and rows // TILE * REACH <= LANES
+    blocks = rows % (4 * TILE) == 0 and rows >= 8 * TILE and rows // TILE * REACH <= LANES
     return lax.axis_size("grow") == 2 and columns == LANES and REACH == TILE and blocks
 
 

time: 60.9 us -> 53 us (0.87)
  waiting for transfers between devices: 27.4 us -> 16.9 us
  starting transfers between devices: 11.6 us -> 14.5 us
    ppermute x1 -> x2, waiting for transfers between devices: 16.5 us -> 10.1 us  [from_behind(): return lax.ppermute(block, axis, route)]
    ppermute x6 -> x7, waiting for transfers between devices: 10.9 us -> 6.85 us  [send(): return lax.ppermute(block, ('grow', 'cy', 'cz'), pairs)]
    ppermute x1 -> x2, starting transfers between devices: 1.29 us -> 2.76 us  [from_behind(): return lax.ppermute(block, axis, route)]
    ppermute x6 -> x7, starting transfers between devices: 10.3 us -> 11.7 us  [send(): return lax.ppermute(block, ('grow', 'cy', 'cz'), pairs)]
    pallas_call x3 -> x6, Pallas kernels: 18.5 us -> 18.1 us  [the longest x2 13.6 us: pair_shards(): call(functools.partial(steps_kernel, part), [(FIELDS, slab, rows // 2, LA...]
  transfers between devices with their start and end apart: 7 -> 9, of which waited for: 5 -> 5; matrix products, arithmetic and copies ran while one was open for 0% -> 0% of each run, Pallas kernels for 2% -> 29%
where the time goes in v6:
time: 53 us; the launch traced here: 52.8 us
  Pallas kernels  19.3 us (36%)
  waiting for transfers between devices  16.9 us (32%)
  starting transfers between devices  14.5 us (27%)
  local copies, waits for them, and re-layouts  1.32 us (2%)
  between operations  0.7 us (1%)
    pallas_call x2, Pallas kernels, pair_shards(): call(functools.partial(steps_kernel, part), [(FIELDS, slab, rows // 2, LA...  13.6 us
    ppermute x7, starting transfers between devices, send(): return lax.ppermute(block, ('grow', 'cy', 'cz'), pairs)  11.7 us
    ppermute x2, waiting for transfers between devices, from_behind(): return lax.ppermute(block, axis, route)  10.1 us
    ppermute x7, waiting for transfers between devices, send(): return lax.ppermute(block, ('grow', 'cy', 'cz'), pairs)  6.85 us
    ppermute x2, starting transfers between devices, from_behind(): return lax.ppermute(block, axis, route)  2.76 us
    pallas_call x1, Pallas kernels, pair_shards(): call(prepare_kernel, [(FIELDS,) + labels.shape, (count * early, LANES)] +...  2.64 us
    unnamed x2, local copies, waits for them, and re-layouts  1.32 us
    pallas_call x1, Pallas kernels, pair_shards(): call(finish_kernel, [labels.shape, labels.shape, displacement.shape])  1.23 us
  transfers between devices with their start and end apart: 9, of which 5 were waited for; matrix products, arithmetic and copies ran while one was open for 0% of the time, Pallas kernels for 29%

profile of v6, /device:TPU:0, one launch (start us, length us, event | category | flops | bytes accessed | tf_op | source)
XLA Modules:
  0.0 52.8 jit_solution(14797708111959096431)
XLA Ops:
  0.6 2.6 %shard_map.67 = (f32[5,4,128,128]{3,2,1,0:T(8,128)}, f32[800,128]{1,0:T(8,128)}, f32[160,128]{1,0:T(8,128)}, f32[160,128]{1,0:T(8,128)}) custom-call(s32[4,128,128]{2,1,0:T(8,128)} %labels.1, f32[4,128,128]{2,1,0:T(8,128)} %roughness.1, f32[4,128,128]{2,1,0:T(8,128)} %potential.1, f32[3,4,128,128]{3,2,1,0:T(8,128)} %displacement.1), custom_call_target="tpu_custom_call" | custom-call | flops 1 | bytes 1 | tf_op jit(solution)/shard_map/pallas_call | solution.py:702
  3.3 3.0 %collective-permute-start.5 = (f32[800,128]{1,0:T(8,128)}, f32[800,128]{1,0:T(8,128)S(1)}, u32[]{:S(2)}, u32[]{:S(2)}) collective-permute-start(f32[800,128]{1,0:T(8,128)} %get-tuple-element.23), channel_id=1, source_target_pairs={{0,16},{1,17},{2,18},{3,19},{4,20},{5,21},{6,22},{7,23},{8,24},{9,... | collective-permute-start | bytes 1228808 | tf_op jit(solution)/shard_map/ppermute | solution.py:700
  6.3 0.0 collective-permute-start
  6.3 1.7 %collective-permute-start.1 = (f32[160,128]{1,0:T(8,128)}, f32[160,128]{1,0:T(8,128)S(1)}, u32[]{:S(2)}, u32[]{:S(2)}) collective-permute-start(f32[160,128]{1,0:T(8,128)} %get-tuple-element.18), channel_id=1, source_target_pairs={{0,12},{1,13},{2,14},{3,15},{4,0},{5,1},{6,2},{7,3},{8,4},{9,5},{1... | collective-permute-start | bytes 245768 | tf_op jit(solution)/shard_map/ppermute | solution.py:700
  8.0 2.3 %collective-permute-done.above = f32[160,128]{1,0:T(8,128)S(1)} collective-permute-done((f32[160,128]{1,0:T(8,128)}, f32[160,128]{1,0:T(8,128)S(1)}, u32[]{:S(2)}, u32[]{:S(2)}) %collective-permute-start) | collective-permute-done | bytes 81952 | tf_op jit(solution)/shard_map/ppermute | solution.py:700
  10.4 0.0 collective-permute-done.1.below
  10.4 1.3 %copy-done = f32[5,4,128,128]{3,2,1,0:T(8,128)S(1)} copy-done((f32[5,4,128,128]{3,2,1,0:T(8,128)S(1)}, f32[5,4,128,128]{3,2,1,0:T(8,128)}, u32[]{:S(2)}) %copy-start) | copy-done | bytes 1310744
  11.7 1.2 %shard_map.68 = (f32[344,128]{1,0:T(8,128)S(1)}, f32[184,128]{1,0:T(8,128)S(1)}, f32[184,128]{1,0:T(8,128)S(1)}) custom-call(f32[5,4,128,128]{3,2,1,0:T(8,128)S(1)} %copy-done, f32[160,128]{1,0:T(8,128)S(1)} %collective-permute-done.above, f32[160,128]{1,0:T(8,128)S(1)} %collective-permute-done.1.below), custom_call_target="tpu_custom_call" | custom-call | flops 1 | bytes 1 | tf_op jit(solution)/shard_map/pallas_call | solution.py:713
  12.9 0.6 %collective-permute-start.3 = (f32[344,128]{1,0:T(8,128)S(1)}, f32[344,128]{1,0:T(8,128)S(1)}, u32[]{:S(2)}, u32[]{:S(2)}) collective-permute-start(f32[344,128]{1,0:T(8,128)S(1)} %get-tuple-element.21), channel_id=1, source_target_pairs={{0,16},{1,17},{2,18},{3,19},{4,20},{5,21},{6,22},{7,23},{8,24},{9,... | collective-permute-start | bytes 528392 | tf_op jit(solution)/shard_map/ppermute | solution.py:700
  13.5 1.6 %collective-permute-start.2 = (f32[184,128]{1,0:T(8,128)S(1)}, f32[184,128]{1,0:T(8,128)S(1)}, u32[]{:S(2)}, u32[]{:S(2)}) collective-permute-start(f32[184,128]{1,0:T(8,128)S(1)} %get-tuple-element.19), channel_id=1, source_target_pairs={{0,1},{1,2},{2,3},{3,0},{4,5},{5,6},{6,7},{7,4},{8,9},{9,10},{10,1... | collective-permute-start | bytes 282632 | tf_op jit(solution)/shard_map/ppermute | solution.py:700
  15.1 3.4 %collective-permute-start.4 = (f32[184,128]{1,0:T(8,128)S(1)}, f32[184,128]{1,0:T(8,128)S(1)}, u32[]{:S(2)}, u32[]{:S(2)}) collective-permute-start(f32[184,128]{1,0:T(8,128)S(1)} %get-tuple-element.22), channel_id=1, source_target_pairs={{0,19},{1,16},{2,17},{3,18},{4,23},{5,20},{6,21},{7,22},{8,27},{9,... | collective-permute-start | bytes 282632 | tf_op jit(solution)/shard_map/ppermute | solution.py:700
  18.5 1.8 %collective-permute-done.2.same = f32[184,128]{1,0:T(8,128)S(1)} collective-permute-done((f32[184,128]{1,0:T(8,128)S(1)}, f32[184,128]{1,0:T(8,128)S(1)}, u32[]{:S(2)}, u32[]{:S(2)}) %collective-permute-start.2) | collective-permute-done | bytes 94240 | tf_op jit(solution)/shard_map/ppermute | solution.py:700
  20.3 0.5 shard_map.69
  20.8 2.7 %collective-permute-done.4.other = f32[184,128]{1,0:T(8,128)S(1)} collective-permute-done((f32[184,128]{1,0:T(8,128)S(1)}, f32[184,128]{1,0:T(8,128)S(1)}, u32[]{:S(2)}, u32[]{:S(2)}) %collective-permute-start.4) | collective-permute-done | bytes 94240 | tf_op jit(solution)/shard_map/ppermute | solution.py:700
  23.5 0.1 shard_map.71
  23.7 1.4 %collective-permute-start.6 = (f32[480,128]{1,0:T(8,128)S(1)}, f32[480,128]{1,0:T(8,128)S(1)}, u32[]{:S(2)}, u32[]{:S(2)}) collective-permute-start(f32[480,128]{1,0:T(8,128)S(1)} %shard_map.71), channel_id=1, source_target_pairs={{0,16},{1,17},{2,18},{3,19},{4,20},{5,21},{6,22},{7,23},{8,24},{9,... | collective-permute-start | bytes 737288 | tf_op jit(solution)/shard_map/ppermute | solution.py:700
  25.1 6.7 %shard_map.70 = (f32[5,4,64,128]{3,2,1,0:T(8,128)S(1)}, f32[640,128]{1,0:T(8,128)S(1)}) custom-call(f32[5,4,12,8,128]{4,3,2,1,0:T(8,128)S(1)} %get-tuple-element.20.near.near_a, f32[344,128]{1,0:T(8,128)S(1)} %collective-permute-done.3.across, f32[184,128]{1,0:T(8,128)S(1)} %collective-permute-done.4.other, f32[800,128]{1,0:T(8,128)S(1)} %collective-permute-done.5.refs_0_.early), custom_call_target="tpu_custom_call" | custom-call | flops 78643200 | bytes 19660800 | tf_op jit(solution)/shard_map/pallas_call | solution.py:732
  31.8 1.5 %collective-permute-start.7 = (f32[640,128]{1,0:T(8,128)S(1)}, f32[640,128]{1,0:T(8,128)S(1)}, u32[]{:S(2)}, u32[]{:S(2)}) collective-permute-start(f32[640,128]{1,0:T(8,128)S(1)} %get-tuple-element.27), channel_id=1, source_target_pairs={{16,0},{17,1},{18,2},{19,3},{20,4},{21,5},{22,6},{23,7},{24,8},{25... | collective-permute-start | bytes 983048 | tf_op jit(solution)/shard_map/ppermute | solution.py:49
  33.3 0.0 collective-permute-done.6.refs_1_
  33.3 6.9 %shard_map.72 = (f32[5,4,64,128]{3,2,1,0:T(8,128)S(1)}, f32[640,128]{1,0:T(8,128)S(1)}) custom-call(f32[5,4,12,8,128]{4,3,2,1,0:T(8,128)S(1)} %get-tuple-element.25.near_b.near, f32[344,128]{1,0:T(8,128)S(1)} %collective-permute-done.3.across, f32[184,128]{1,0:T(8,128)S(1)} %collective-permute-done.4.other, ...), custom_call_target="tpu_custom_call" | custom-call | flops 78643200 | bytes 19660800 | tf_op jit(solution)/shard_map/pallas_call | solution.py:732
  40.2 1.3 %collective-permute-start.8 = (f32[640,128]{1,0:T(8,128)S(1)}, f32[640,128]{1,0:T(8,128)S(1)}, u32[]{:S(2)}, u32[]{:S(2)}) collective-permute-start(f32[640,128]{1,0:T(8,128)S(1)} %get-tuple-element.28), channel_id=1, source_target_pairs={{16,0},{17,1},{18,2},{19,3},{20,4},{21,5},{22,6},{23,7},{24,8},{25... | collective-permute-start | bytes 983048 | tf_op jit(solution)/shard_map/ppermute | solution.py:49
  41.5 1.7 %collective-permute-done.7.message_a = f32[640,128]{1,0:T(8,128)S(1)} collective-permute-done((f32[640,128]{1,0:T(8,128)S(1)}, f32[640,128]{1,0:T(8,128)S(1)}, u32[]{:S(2)}, u32[]{:S(2)}) %collective-permute-start.7) | collective-permute-done | bytes 327712 | tf_op jit(solution)/shard_map/ppermute | solution.py:49
  43.2 8.4 %collective-permute-done.8.message_b = f32[640,128]{1,0:T(8,128)S(1)} collective-permute-done((f32[640,128]{1,0:T(8,128)S(1)}, f32[640,128]{1,0:T(8,128)S(1)}, u32[]{:S(2)}, u32[]{:S(2)}) %collective-permute-start.8) | collective-permute-done | bytes 327712 | tf_op jit(solution)/shard_map/ppermute | solution.py:49
  51.5 1.2 %shard_map.73 = (f32[4,128,128]{2,1,0:T(8,128)}, f32[4,128,128]{2,1,0:T(8,128)}, f32[3,4,128,128]{3,2,1,0:T(8,128)}) custom-call(f32[5,4,64,128]{3,2,1,0:T(8,128)S(1)} %get-tuple-element.24.refs_2_.result_a, f32[5,4,64,128]{3,2,1,0:T(8,128)S(1)} %get-tuple-element.26.result_b, f32[640,128]{1,0:T(8,128)S(1)} %collective-permute-done.7.message_a, ...), custom_call_target="tpu_custom_call" | custom-call | flops 1 | bytes 1 | tf_op jit(solution)/shard_map/pallas_call | solution.py:748
  (3 shorter events, 0.0 us)
Async XLA Ops:
  3.3 20.2 %collective-permute-start.5 = (f32[800,128]{1,0:T(8,128)}, f32[800,128]{1,0:T(8,128)S(1)}, u32[]{:S(2)}, u32[]{:S(2)}) collective-permute-start(f32[800,128]{1,0:T(8,128)} %get-tuple-element.23), channel_id=1, source_target_pairs={{0,16},{1,17},{2,18},{3,19},{4,20},{5,21},{6,22},{7,23},{8,24},{9,... | collective-permute-start | bytes 1228808 | tf_op jit(solution)/shard_map/ppermute | solution.py:700
  6.3 4.1 %collective-permute-start = (f32[160,128]{1,0:T(8,128)}, f32[160,128]{1,0:T(8,128)S(1)}, u32[]{:S(2)}, u32[]{:S(2)}) collective-permute-start(f32[160,128]{1,0:T(8,128)} %get-tuple-element.17), channel_id=1, source_target_pairs={{0,4},{1,5},{2,6},{3,7},{4,8},{5,9},{6,10},{7,11},{8,12},{9,13},{1... | collective-permute-start | bytes 245768 | tf_op jit(solution)/shard_map/ppermute | solution.py:700
  6.3 4.1 %collective-permute-start.1 = (f32[160,128]{1,0:T(8,128)}, f32[160,128]{1,0:T(8,128)S(1)}, u32[]{:S(2)}, u32[]{:S(2)}) collective-permute-start(f32[160,128]{1,0:T(8,128)} %get-tuple-element.18), channel_id=1, source_target_pairs={{0,12},{1,13},{2,14},{3,15},{4,0},{5,1},{6,2},{7,3},{8,4},{9,5},{1... | collective-permute-start | bytes 245768 | tf_op jit(solution)/shard_map/ppermute | solution.py:700
  10.4 1.3 %copy-start = (f32[5,4,128,128]{3,2,1,0:T(8,128)S(1)}, f32[5,4,128,128]{3,2,1,0:T(8,128)}, u32[]{:S(2)}) copy-start(f32[5,4,128,128]{3,2,1,0:T(8,128)} %get-tuple-element.16.fields) | copy-start | bytes 3932164
  12.9 10.6 %collective-permute-start.3 = (f32[344,128]{1,0:T(8,128)S(1)}, f32[344,128]{1,0:T(8,128)S(1)}, u32[]{:S(2)}, u32[]{:S(2)}) collective-permute-start(f32[344,128]{1,0:T(8,128)S(1)} %get-tuple-element.21), channel_id=1, source_target_pairs={{0,16},{1,17},{2,18},{3,19},{4,20},{5,21},{6,22},{7,23},{8,24},{9,... | collective-permute-start | bytes 528392 | tf_op jit(solution)/shard_map/ppermute | solution.py:700
  13.5 6.8 %collective-permute-start.2 = (f32[184,128]{1,0:T(8,128)S(1)}, f32[184,128]{1,0:T(8,128)S(1)}, u32[]{:S(2)}, u32[]{:S(2)}) collective-permute-start(f32[184,128]{1,0:T(8,128)S(1)} %get-tuple-element.19), channel_id=1, source_target_pairs={{0,1},{1,2},{2,3},{3,0},{4,5},{5,6},{6,7},{7,4},{8,9},{9,10},{10,1... | collective-permute-start | bytes 282632 | tf_op jit(solution)/shard_map/ppermute | solution.py:700
  15.1 8.4 %collective-permute-start.4 = (f32[184,128]{1,0:T(8,128)S(1)}, f32[184,128]{1,0:T(8,128)S(1)}, u32[]{:S(2)}, u32[]{:S(2)}) collective-permute-start(f32[184,128]{1,0:T(8,128)S(1)} %get-tuple-element.22), channel_id=1, source_target_pairs={{0,19},{1,16},{2,17},{3,18},{4,23},{5,20},{6,21},{7,22},{8,27},{9,... | collective-permute-start | bytes 282632 | tf_op jit(solution)/shard_map/ppermute | solution.py:700
  23.7 9.6 %collective-permute-start.6 = (f32[480,128]{1,0:T(8,128)S(1)}, f32[480,128]{1,0:T(8,128)S(1)}, u32[]{:S(2)}, u32[]{:S(2)}) collective-permute-start(f32[480,128]{1,0:T(8,128)S(1)} %shard_map.71), channel_id=1, source_target_pairs={{0,16},{1,17},{2,18},{3,19},{4,20},{5,21},{6,22},{7,23},{8,24},{9,... | collective-permute-start | bytes 737288 | tf_op jit(solution)/shard_map/ppermute | solution.py:700
  31.8 11.3 %collective-permute-start.7 = (f32[640,128]{1,0:T(8,128)S(1)}, f32[640,128]{1,0:T(8,128)S(1)}, u32[]{:S(2)}, u32[]{:S(2)}) collective-permute-start(f32[640,128]{1,0:T(8,128)S(1)} %get-tuple-element.27), channel_id=1, source_target_pairs={{16,0},{17,1},{18,2},{19,3},{20,4},{21,5},{22,6},{23,7},{24,8},{25... | collective-permute-start | bytes 983048 | tf_op jit(solution)/shard_map/ppermute | solution.py:49
  40.2 11.4 %collective-permute-start.8 = (f32[640,128]{1,0:T(8,128)S(1)}, f32[640,128]{1,0:T(8,128)S(1)}, u32[]{:S(2)}, u32[]{:S(2)}) collective-permute-start(f32[640,128]{1,0:T(8,128)S(1)} %get-tuple-element.28), channel_id=1, source_target_pairs={{16,0},{17,1},{18,2},{19,3},{20,4},{21,5},{22,6},{23,7},{24,8},{25... | collective-permute-start | bytes 983048 | tf_op jit(solution)/shard_map/ppermute | solution.py:49

commit v7 on v5

--- a/solution.py
+++ b/solution.py
@@ -1,3 +1,5 @@
+import functools
+
 import jax
 import jax.numpy as jnp
 from jax import lax
@@ -215,7 +217,7 @@
 TILE = 8
 FIELDS = 5
 LAG = 2
-TOGETHER = 6
+TOGETHER = 12
 
 
 def lanes(shape):
@@ -239,12 +241,57 @@
     return jnp.logical_xor(low, side == 1)
 
 
+def pack_halves(fields, upper, lower, mid, theirs, out):
+    _, slab, _, _ = fields.shape
+    for field in range(FIELDS):
+        for plane in range(slab):
+            for row in range(0, mid, TILE):
+                one = fields[field, plane, pl.ds(upper + row, TILE), :]
+                two = fields[field, plane, pl.ds(lower + row, TILE), :]
+                to = pl.ds((field * slab + plane) * mid + row, TILE)
+                out[to, :] = jnp.where(theirs, one, turned(two, LANES // 2))
+
+
+def pack_strips(fields, base, out, start):
+    _, slab, rows, _ = fields.shape
+    for field in range(FIELDS):
+        for plane in range(slab):
+            packed = jnp.zeros((TILE, LANES), jnp.float32)
+            for group in range(rows // TILE):
+                block = fields[field, plane, pl.ds(group * TILE, TILE), :]
+                block = turned(block, group * REACH - base)
+                packed = jnp.where(from_lane(group * REACH), block, packed)
+            out[pl.ds(start + (field * slab + plane) * TILE, TILE), :] = packed
+
+
+def pack_rim_strips(above, below, base, out, start):
+    per = LANES // REACH
+    blocks = 2 * above.shape[0] // TILE
+    for first in range(0, blocks, per):
+        packed = jnp.zeros((TILE, LANES), jnp.float32)
+        for which in range(first, min(first + per, blocks)):
+            block = (above, below)[which % 2][pl.ds(which // 2 * TILE, TILE), :]
+            to = which % per * REACH
+            packed = jnp.where(from_lane(to), turned(block, to - base), packed)
+        out[pl.ds(start + first // per * TILE, TILE), :] = packed
+
+
+def strip_bases(side):
+    outer = LANES - REACH
+    return LANES // 2 - REACH + REACH * side, outer * (1 - side), outer * side
+
+
+def split(rows):
+    return rows // 4 - REACH, 3 * rows // 4 + REACH
+
+
 def prepare_kernel(
-    labels, roughness, potential, displacement, fields, halves, first, last, marks, rough, arrived
+    labels, roughness, potential, displacement,
+    fields, halves, same, other, first, last, marks, rough, arrived,
 ):
     _, slab, rows, _ = fields.shape
-    theirs = jnp.logical_not(half_of(lax.axis_index("grow")))
-    mid = rows // 2
+    side = lax.axis_index("grow")
+    count = FIELDS * slab
     copies = [
         pltpu.make_async_copy(source, target, arrived.at[which])
         for which, (source, target) in enumerate(
@@ -268,120 +315,123 @@
             fields[(0,) + spot] = mark * (1.0 - part) + (1.0 - mark) * part
     for copy in copies[2:]:
         copy.wait()
+    start, stop = split(rows)
+    mid = (stop - start) // 2
+    pack_halves(fields, start, start + mid, mid, jnp.logical_not(half_of(side)), halves)
+    for out, at, base in zip((halves, same, other), (count * mid, 0, 0), strip_bases(side)):
+        pack_strips(fields, base, out, at)
+    for field in range(FIELDS):
+        for plane in range(slab):
+            spot = pl.ds((field * slab + plane) * TILE, TILE)
+            first[spot, :] = fields[field, plane, pl.ds(0, TILE), :]
+            last[spot, :] = fields[field, plane, pl.ds(rows - TILE, TILE), :]
+
+
+def rims_kernel(fields, above, below, same_first, other_first, halves, same, other):
+    _, slab, rows, _ = fields.shape
+    side = lax.axis_index("grow")
+    theirs = jnp.logical_not(half_of(side))
+    count = FIELDS * slab
+    start, stop = split(rows)
+    pack_halves(fields, 0, stop, start, theirs, halves)
+    for which in range(count):
+        spot = pl.ds(which * TILE, TILE)
+        rims = jnp.where(theirs, above[spot, :], turned(below[spot, :], LANES // 2))
+        halves[pl.ds(count * start + which * TILE, TILE), :] = rims
+    starts = (count * (start + TILE), 0, 0)
+    for out, at, base in zip((halves, same, other), starts, strip_bases(side)):
+        pack_rim_strips(above, below, base, out, at)
+
+
+def blocks_of(part, rows):
+    start, stop = split(rows)
+    if part == 0:
+        return list(range(start, stop, TILE))
+    inner = start + 2 * REACH
+    return list(range(-REACH, inner, TILE)) + list(range(rows - inner, rows + REACH, TILE))
+
+
+def packed_at(which, row, rows, count):
+    if 0 <= row < rows:
+        return False, which * TILE, row // TILE * REACH
+    at, group = divmod(2 * which + int(row > 0), LANES // REACH)
+    return True, at * TILE, group * REACH
+
+
+def own_kernel(part, fields, *refs):
+    out, natural = refs[-2:]
+    same, *more = refs[:-2]
+    same_rims, above, below = more or (None, None, None)
+    _, slab, rows, _ = fields.shape
+    count = FIELDS * slab
+    outer = (LANES - REACH) * (1 - lax.axis_index("grow"))
+    in_outer = from_lane(outer)
+    segment = out.shape[2] - 2
     for field in range(FIELDS):
         for plane in range(slab):
             which = field * slab + plane
-            for row in range(0, mid, TILE):
-                upper = fields[field, plane, pl.ds(row, TILE), :]
-                lower = turned(fields[field, plane, pl.ds(row + mid, TILE), :], LANES // 2)
-                halves[pl.ds(which * mid + row, TILE), :] = jnp.where(theirs, upper, lower)
-            first[pl.ds(which * TILE, TILE), :] = fields[field, plane, pl.ds(0, TILE), :]
-            last[pl.ds(which * TILE, TILE), :] = fields[field, plane, pl.ds(rows - TILE, TILE), :]
-
-
-def strips(fields, above, below, base, out, start):
-    _, slab, rows, _ = fields.shape
-    count = FIELDS * slab
-    spare = []
-    for field in range(FIELDS):
-        for plane in range(slab):
-            which = field * slab + plane
-            packed = jnp.zeros((TILE, LANES), jnp.float32)
-            for group in range(rows // TILE):
-                block = fields[field, plane, pl.ds(group * TILE, TILE), :]
-                block = turned(block, group * REACH - base)
-                packed = jnp.where(from_lane(group * REACH), block, packed)
-            out[pl.ds(start + which * TILE, TILE), :] = packed
-            spot = pl.ds(which * TILE, TILE)
-            spare.append(above[spot, :])
-            spare.append(below[spot, :])
-    strips_of_rims(spare, base, out, start + count * TILE)
-
-
-def strips_of_rims(blocks, base, out, start):
-    per = LANES // REACH
-    for at in range(0, len(blocks), per):
-        packed = jnp.zeros((TILE, LANES), jnp.float32)
-        for group, block in enumerate(blocks[at : at + per]):
-            packed = jnp.where(
-                from_lane(group * REACH), turned(block, group * REACH - base), packed
-            )
-        out[pl.ds(start + at // per * TILE, TILE), :] = packed
-
-
-def rim_rows(slab):
-    count = FIELDS * slab
-    return (count + -(-2 * count * REACH // LANES)) * TILE
-
-
-def rims_kernel(fields, above, below, across, same, other):
-    slab = fields.shape[1]
-    side = lax.axis_index("grow")
-    theirs = jnp.logical_not(half_of(side))
-    count = FIELDS * slab
-    for which in range(count):
-        spot = pl.ds(which * TILE, TILE)
-        across[spot, :] = jnp.where(theirs, above[spot, :], turned(below[spot, :], LANES // 2))
-    inner = LANES // 2 - REACH + REACH * side
-    outer = LANES - REACH
-    strips(fields, above, below, inner, across, count * TILE)
-    strips(fields, above, below, outer * (1 - side), same, 0)
-    strips(fields, above, below, outer * side, other, 0)
+            for at, row in enumerate(blocks_of(part, rows)):
+                of_rim, spot, lane = packed_at(which, row, rows, count)
+                piece = (same_rims if of_rim else same)[pl.ds(spot, TILE), :]
+                if of_rim:
+                    near = (below if row > 0 else above)[pl.ds(which * TILE, TILE), :]
+                else:
+                    near = fields[field, plane, pl.ds(row, TILE), :]
+                near = jnp.where(in_outer, turned(piece, outer - lane), near)
+                natural[which, pl.ds(at * TILE, TILE), :] = near
+            blocks = [natural[which, pl.ds(row, TILE, stride=segment), :] for row in range(segment)]
+            blocks = [pltpu.roll(blocks[-1], 1, 0), *blocks, pltpu.roll(blocks[0], TILE - 1, 0)]
+            for row, block in enumerate(blocks):
+                out[field, plane, row] = block
 
 
 def conduct_of(step):
     return COND_EL + COND_LI * step
 
 
-def steps_kernel(
-    fields, above, below, halves, across, same, other, result, message,
-    natural, phase, phase_new, pot, pot_new, disp, disp_new,
-    slopes, slopes_y, cond_x, cond_y, cond_y_back, cond_z,
-):
-    _, slab, rows, _ = fields.shape
+def steps_kernel(part, near, other, halves, *refs):
+    if part:
+        other_rims, rest, _, *refs = refs
+    result, message, natural, phase, phase_new, pot, pot_new, disp, disp_new = refs[:9]
+    slopes, slopes_y, cond_x, cond_y, cond_y_back, cond_z = refs[9:]
+    _, slab, rows, _ = result.shape
+    all_rows = 2 * rows
     planes = 2 * slab
     side = lax.axis_index("grow")
     mine = half_of(side)
-    mid = rows // 2
     count = FIELDS * slab
-    groups = rows // TILE
-    per = LANES // REACH
     inner = LANES // 2 - REACH * side
     outer = (LANES - REACH) * (1 - side)
     in_inner, in_outer = from_lane(inner), from_lane(outer)
     segment = phase.shape[1] - 2
+    start, stop = split(all_rows)
+    half = (stop - start) // 2
+    blocks = blocks_of(part, all_rows)
+
+    def arrived_half(which, row):
+        if start <= row < stop:
+            block = halves[pl.ds(which * half + (row - start) % half, TILE), :]
+            return turned(block, LANES // 2) if row - start >= half else block
+        if 0 <= row < all_rows:
+            block = rest[pl.ds(which * start + row % stop, TILE), :]
+        else:
+            block = rest[pl.ds(count * start + which * TILE, TILE), :]
+        return turned(block, LANES // 2) if row > 0 and row >= stop else block
 
     for field in range(FIELDS):
         for plane in range(slab):
             which = field * slab + plane
-            own, far = side * slab + plane, (1 - side) * slab + plane
-            spot = pl.ds(which * TILE, TILE)
-            from_same, from_other = same[spot, :], other[spot, :]
-            strip = across[pl.ds((count + which) * TILE, TILE), :]
-            for group in range(groups):
-                row = group * TILE
-                to = pl.ds(REACH + row, TILE)
-                near = fields[field, plane, pl.ds(row, TILE), :]
-                back = outer - group * REACH
-                natural[field, own, to, :] = jnp.where(in_outer, turned(from_same, back), near)
-                block = halves[pl.ds(which * mid + row % mid, TILE), :]
-                if row >= mid:
-                    block = turned(block, LANES // 2)
-                block = jnp.where(in_inner, turned(strip, inner - group * REACH), block)
-                natural[field, far, to, :] = jnp.where(in_outer, turned(from_other, back), block)
-            rim = across[spot, :]
-            for end, to in ((0, pl.ds(0, TILE)), (1, pl.ds(REACH + rows, TILE))):
-                at, group = divmod(2 * which + end, per)
-                extra = pl.ds((count + at) * TILE, TILE)
-                back = outer - group * REACH
-                near = (below if end else above)[spot, :]
-                block = jnp.where(in_outer, turned(same[extra, :], back), near)
-                natural[field, own, to, :] = block
-                block = turned(rim, LANES // 2) if end else rim
-                strip = across[pl.ds((2 * count + at) * TILE, TILE), :]
-                block = jnp.where(in_inner, turned(strip, inner - group * REACH), block)
-                block = jnp.where(in_outer, turned(other[extra, :], back), block)
-                natural[field, far, to, :] = block
+            for at, row in enumerate(blocks):
+                of_rim, spot, lane = packed_at(which, row, all_rows, count)
+                if of_rim:
+                    strip = rest[pl.ds(count * (start + TILE) + spot, TILE), :]
+                    beside = other_rims[pl.ds(spot, TILE), :]
+                else:
+                    strip = halves[pl.ds(count * half + spot, TILE), :]
+                    beside = other[pl.ds(spot, TILE), :]
+                block = jnp.where(in_inner, turned(strip, inner - lane), arrived_half(which, row))
+                block = jnp.where(in_outer, turned(beside, outer - lane), block)
+                natural[field, plane, pl.ds(at * TILE, TILE), :] = block
 
     def parts_of(phase, pot, disp):
         return (phase, pot, disp.at[0], disp.at[1], disp.at[2])
@@ -392,10 +442,14 @@
             ref[plane, segment + 1] = pltpu.roll(ref[plane, 1], TILE - 1, 0)
 
     for field, ref in enumerate(parts_of(phase, pot, disp)):
-        for plane in range(planes):
+        for plane in range(slab):
+            own, far = side * slab + plane, (1 - side) * slab + plane
+            for row in range(segment + 2):
+                ref[own, row] = near[field, plane, row]
             for row in range(segment):
-                ref[plane, 1 + row] = natural[field, plane, pl.ds(row, TILE, stride=segment), :]
-        close(ref)
+                ref[far, 1 + row] = natural[field, plane, pl.ds(row, TILE, stride=segment), :]
+            ref[far, 0] = pltpu.roll(ref[far, segment], 1, 0)
+            ref[far, segment + 1] = pltpu.roll(ref[far, 1], TILE - 1, 0)
 
     def one_row(row, bodies):
         waiting = []
@@ -419,7 +473,10 @@
                 one_row(1 + turn * together + more, bodies)
             return carry
 
-        lax.fori_loop(0, segment // together, some, 0)
+        if together == segment:
+            some(0, 0)
+        else:
+            lax.fori_loop(0, segment // together, some, 0)
 
     def up(block):
         return pltpu.roll(block, LANES - 1, 1)
@@ -571,36 +628,57 @@
         phase, phase_new = phase_new, phase
         if not last:
             close(phase)
+    outs = results_of(part, all_rows)
     for field, ref in enumerate(parts_of(phase, pot, disp)):
         for plane in range(slab):
             for row in range(segment):
                 to = pl.ds(row, TILE, stride=segment)
                 natural[field, plane, to, :] = ref[slab + plane, 1 + row]
-            for row in range(0, mid, TILE):
-                upper = natural[field, plane, pl.ds(REACH + row, TILE), :]
-                lower = natural[field, plane, pl.ds(REACH + row + mid, TILE), :]
-                result[field, plane, pl.ds(row, TILE), :] = upper
-                result[field, plane, pl.ds(row + mid, TILE), :] = lower
-                to = pl.ds((field * slab + plane) * mid + row, TILE)
-                message[to, :] = jnp.where(mine, upper, turned(lower, LANES // 2))
-
-
-def finish_kernel(result, message, phase, potential, displacement):
+            for at in range(len(outs) // 2):
+                pair = []
+                for place in (at, at + len(outs) // 2):
+                    spot = pl.ds(blocks.index(outs[place]) * TILE, TILE)
+                    pair.append(natural[field, plane, spot, :])
+                    result[field, plane, pl.ds(place * TILE, TILE), :] = pair[-1]
+                to = pl.ds(((field * slab + plane) * len(outs) // 2 + at) * TILE, TILE)
+                message[to, :] = jnp.where(mine, pair[0], turned(pair[1], LANES // 2))
+
+
+def results_of(part, rows):
+    quarter = rows // 4
+    if part == 0:
+        return list(range(quarter, 3 * quarter, TILE))
+    return list(range(0, quarter, TILE)) + list(range(3 * quarter, rows, TILE))
+
+
+def finish_kernel(part, result, message, *refs):
+    phase, potential, displacement, whole, arrived = refs[3 * part :]
     _, slab, rows, _ = result.shape
     side = lax.axis_index("grow")
     mine = half_of(side)
     fresh = side == lax.axis_size("grow") - 1
-    mid = rows // 2
+    half = rows // 2
+    copies = []
     for field in range(FIELDS):
-        out = (phase, potential, displacement, displacement, displacement)[field]
         for plane in range(slab):
-            for row in range(0, mid, TILE):
-                block = message[pl.ds((field * slab + plane) * mid + row, TILE), :]
-                for place, piece in ((row, block), (row + mid, turned(block, LANES // 2))):
-                    spot = (plane, pl.ds(place, TILE), slice(None))
-                    whole = jnp.where(mine, result[(field,) + spot], piece)
-                    whole = jnp.where(fresh, V_HIGH if field == 1 else 0.0, whole)
-                    out[spot if field < 2 else (field - 2,) + spot] = whole
+            for row in range(0, rows, TILE):
+                spot = pl.ds((field * slab + plane) * half + row % half, TILE)
+                block = message[spot, :]
+                block = turned(block, LANES // 2) if row >= half else block
+                block = jnp.where(mine, result[field, plane, pl.ds(row, TILE), :], block)
+                block = jnp.where(fresh, V_HIGH if field == 1 else 0.0, block)
+                whole[field, plane, pl.ds(row, TILE), :] = block
+        out = (phase, potential, displacement.at[0], displacement.at[1], displacement.at[2])[field]
+        for source, target in (((0, 0), (half, 3 * half)) if part else ((0, half), (half, rows))):
+            copy = pltpu.make_async_copy(
+                whole.at[field, :, pl.ds(source, half), :],
+                out.at[:, pl.ds(target, half), :],
+                arrived.at[len(copies)],
+            )
+            copy.start()
+            copies.append(copy)
+    for copy in copies:
+        copy.wait()
 
 
 def call(kernel, outs, scratch=(), limit=48, **how):
@@ -610,7 +688,7 @@
         scratch_shapes=[
             pltpu.VMEM(one, jnp.float32) if isinstance(one, tuple) else one for one in scratch
         ],
-        **how,
+        **{"cost_estimate": pl.CostEstimate(flops=1, bytes_accessed=1, transcendentals=0), **how},
         compiler_params=pltpu.CompilerParams(vmem_limit_bytes=limit * 1024 * 1024),
     )
 
@@ -618,7 +696,9 @@
 def pair_shards(labels, roughness, potential, displacement):
     slab, rows, _ = labels.shape
     count = FIELDS * slab
-    mid = rows // 2
+    start, stop = split(rows)
+    half = (stop - start) // 2
+    spare = -(-2 * count * REACH // LANES) * TILE
     sizes = {name: lax.axis_size(name) for name in ("grow", "cy", "cz")}
 
     def index(grow, cy, cz):
@@ -636,40 +716,79 @@
         pairs = [(index(*at), index(*route(*at))) for at in everyone]
         return lax.ppermute(block, ("grow", "cy", "cz"), pairs)
 
-    fields, halves, first, last = call(
+    def to_partner(block):
+        return send(block, lambda grow, cy, cz: (1 - grow, cy, cz))
+
+    def beside_same(block):
+        return send(block, lambda grow, cy, cz: (grow, cy, cz - 1 if grow else cz + 1))
+
+    def beside_other(block):
+        return send(block, lambda grow, cy, cz: (1 - grow, cy, cz + 1 if grow else cz - 1))
+
+    in_vmem, anywhere, hbm = (
+        pl.BlockSpec(memory_space=space) for space in (pltpu.VMEM, pl.ANY, pltpu.HBM)
+    )
+    thin = (count * TILE, LANES)
+    fields, halves, same, other, first, last = call(
         prepare_kernel,
-        [(FIELDS,) + labels.shape, (count * mid, LANES)] + [(count * TILE, LANES)] * 2,
+        [(FIELDS,) + labels.shape, (count * (half + TILE), LANES)] + [thin] * 4,
         [pltpu.VMEM(labels.shape, labels.dtype), labels.shape, pltpu.SemaphoreType.DMA((4,))],
         limit=54,
-        in_specs=[pl.BlockSpec(memory_space=pltpu.HBM)] * 4,
+        in_specs=[hbm] * 4,
     )(labels, roughness, potential, displacement)
-    halves = send(halves, lambda grow, cy, cz: (1 - grow, cy, cz))
+    halves = to_partner(halves)
+    other = beside_other(other)
     above = send(last, lambda grow, cy, cz: (grow, cy + 1, cz))
     below = send(first, lambda grow, cy, cz: (grow, cy - 1, cz))
-    extra = rim_rows(slab)
-    across, same, other = call(
-        rims_kernel, [(count * TILE + extra, LANES), (extra, LANES), (extra, LANES)]
-    )(fields, above, below)
-    across = send(across, lambda grow, cy, cz: (1 - grow, cy, cz))
-    same = send(same, lambda grow, cy, cz: (grow, cy, cz - 1 if grow else cz + 1))
-    other = send(other, lambda grow, cy, cz: (1 - grow, cy, cz + 1 if grow else cz - 1))
-    span = rows + 2 * REACH
-    deep = (2 * slab, span // TILE + 2, TILE, LANES)
-    result, message = call(
-        steps_kernel,
-        [(FIELDS, slab, rows, LANES), (count * mid, LANES)],
-        [(FIELDS, 2 * slab, span, LANES)]
-        + [deep] * 4
-        + [(3,) + deep] * 2
-        + [deep, deep, (2 * slab + 1,) + deep[1:], deep, deep, deep],
-    )(fields, above, below, halves, across, same, other)
-    message = from_behind(message, "grow", -1)
-    return call(finish_kernel, [labels.shape, labels.shape, displacement.shape])(result, message)
+    same = beside_same(same)
+    rest, same_rims, other_rims = call(
+        rims_kernel,
+        [(count * (start + TILE) + spare, LANES)] + [(spare, LANES)] * 2,
+        in_specs=[in_vmem] * 3 + [anywhere] * 2,
+    )(fields, above, below, same, other)
+    rest = to_partner(rest)
+    other_rims = beside_other(other_rims)
+    same_rims = beside_same(same_rims)
+    results, messages, outs = [], [], []
+    for part in range(2):
+        span = len(blocks_of(part, rows)) * TILE
+        deep = (2 * slab, span // TILE + 2, TILE, LANES)
+        (near,) = call(
+            functools.partial(own_kernel, part),
+            [(FIELDS, slab) + deep[1:]],
+            [(count, span, LANES)],
+        )(fields, same, *([same_rims, above, below] if part else []))
+        result, message = call(
+            functools.partial(steps_kernel, part),
+            [(FIELDS, slab, rows // 2, LANES), (count * rows // 4, LANES)],
+            [(FIELDS, slab, span, LANES)]
+            + [deep] * 4
+            + [(3,) + deep] * 2
+            + [deep, deep, (2 * slab + 1,) + deep[1:], deep, deep, deep],
+            in_specs=[in_vmem] * (3 + 2 * part) + [anywhere] * part,
+            cost_estimate=pl.CostEstimate(
+                flops=STEPS * SWEEPS * 160 * span * 2 * slab * LANES,
+                bytes_accessed=STEPS * SWEEPS * 40 * span * 2 * slab * LANES,
+                transcendentals=STEPS * 2 * span * 2 * slab * LANES,
+            ),
+        )(near, other, halves, *([other_rims, rest, *results] if part else []))
+        results.append(result)
+        messages.append(from_behind(message, "grow", -1))
+    for part in range(2):
+        outs = call(
+            functools.partial(finish_kernel, part),
+            [labels.shape, labels.shape, displacement.shape],
+            [(FIELDS, slab, rows // 2, LANES), pltpu.SemaphoreType.DMA((2 * FIELDS,))],
+            in_specs=[in_vmem] * 2 + [hbm] * (3 * part),
+            out_specs=[hbm] * 3,
+            input_output_aliases={2 + which: which for which in range(3 * part)},
+        )(results[part], messages[part], *outs)
+    return outs
 
 
 def fits_pair(labels):
     rows, columns = labels.shape[1:]
-    blocks = rows % (2 * TILE) == 0 and rows // TILE * REACH <= LANES
+    blocks = rows % (8 * TILE) == 0 and rows // TILE * REACH <= LANES
     return lax.axis_size("grow") == 2 and columns == LANES and REACH == TILE and blocks
 
 

time: 60.9 us -> 53.1 us (0.87)
  waiting for transfers between devices: 27.4 us -> 13.9 us
  starting transfers between devices: 11.6 us -> 15.3 us
  Pallas kernels: 19.7 us -> 21.5 us
    ppermute x1 -> x2, waiting for transfers between devices: 16.5 us -> 6.67 us  [from_behind(): return lax.ppermute(block, axis, route)]
    ppermute x6 -> x8, waiting for transfers between devices: 10.9 us -> 7.19 us  [send(): return lax.ppermute(block, ('grow', 'cy', 'cz'), pairs)]
    ppermute x6 -> x8, starting transfers between devices: 10.3 us -> 12.6 us  [send(): return lax.ppermute(block, ('grow', 'cy', 'cz'), pairs)]
    pallas_call x4 -> x8, Pallas kernels: 19.7 us -> 21.5 us  [the longest x2 14.8 us: pair_shards(): call(functools.partial(steps_kernel, part), [(FIELDS, slab, rows // 2, LA...]
    ppermute x1 -> x2, starting transfers between devices: 1.29 us -> 2.76 us  [from_behind(): return lax.ppermute(block, axis, route)]
  transfers between devices with their start and end apart: 7 -> 10, of which waited for: 5 -> 4; matrix products, arithmetic and copies ran while one was open for 0% -> 0% of each run, Pallas kernels for 2% -> 32%
where the time goes in v7:
time: 53.1 us; the launch traced here: 52.9 us
  Pallas kernels  21.5 us (40%)
  starting transfers between devices  15.3 us (29%)
  waiting for transfers between devices  13.9 us (26%)
  local copies, waits for them, and re-layouts  1.32 us (2%)
  between operations  0.88 us (2%)
    pallas_call x2, Pallas kernels, pair_shards(): call(functools.partial(steps_kernel, part), [(FIELDS, slab, rows // 2, LA...  14.8 us
    ppermute x8, starting transfers between devices, send(): return lax.ppermute(block, ('grow', 'cy', 'cz'), pairs)  12.6 us
    ppermute x8, waiting for transfers between devices, send(): return lax.ppermute(block, ('grow', 'cy', 'cz'), pairs)  7.19 us
    ppermute x2, waiting for transfers between devices, from_behind(): return lax.ppermute(block, axis, route)  6.67 us
    pallas_call x1, Pallas kernels, pair_shards(): call(prepare_kernel, [(FIELDS,) + labels.shape, (count * (half + TILE), L...  3.81 us
    ppermute x2, starting transfers between devices, from_behind(): return lax.ppermute(block, axis, route)  2.76 us
    pallas_call x2, Pallas kernels, pair_shards(): call(functools.partial(finish_kernel, part), [labels.shape, labels.shape,...  1.99 us
    unnamed x2, local copies, waits for them, and re-layouts  1.32 us
  transfers between devices with their start and end apart: 10, of which 4 were waited for; matrix products, arithmetic and copies ran while one was open for 0% of the time, Pallas kernels for 32%

profile of v7, /device:TPU:0, one launch (start us, length us, event | category | flops | bytes accessed | tf_op | source)
XLA Modules:
  0.0 52.9 jit_solution(9561501199396808529)
XLA Ops:
  0.6 3.8 %shard_map.67 = (f32[5,4,128,128]{3,2,1,0:T(8,128)}, f32[960,128]{1,0:T(8,128)}, f32[160,128]{1,0:T(8,128)}, f32[160,128]{1,0:T(8,128)}, f32[160,128]{1,0:T(8,128)}, /*index=5*/f32[160,128]{1,0:T(8,128)}) custom-call(s32[4,128,128]{2,1,0:T(8,128)} %labels.1, f32[4,128,128]{2,1,0:T(8,128)} %roughness.1, f32[4,128,128]{2,1,0:T(8,128)} %potential.1, ...), custom_call_target="tpu_custom_call" | custom-call | flops 1 | bytes 1 | tf_op jit(solution)/shard_map/pallas_call | solution.py:732
  4.4 3.0 %collective-permute-start.5 = (f32[960,128]{1,0:T(8,128)}, f32[960,128]{1,0:T(8,128)S(1)}, u32[]{:S(2)}, u32[]{:S(2)}) collective-permute-start(f32[960,128]{1,0:T(8,128)} %get-tuple-element.25), channel_id=1, source_target_pairs={{0,16},{1,17},{2,18},{3,19},{4,20},{5,21},{6,22},{7,23},{8,24},{9,... | collective-permute-start | bytes 1474568 | tf_op jit(solution)/shard_map/ppermute | solution.py:717
  7.5 1.6 %collective-permute-start = (f32[160,128]{1,0:T(8,128)}, f32[160,128]{1,0:T(8,128)S(1)}, u32[]{:S(2)}, u32[]{:S(2)}) collective-permute-start(f32[160,128]{1,0:T(8,128)} %get-tuple-element.20), channel_id=1, source_target_pairs={{0,1},{1,2},{2,3},{3,0},{4,5},{5,6},{6,7},{7,4},{8,9},{9,10},{10,1... | collective-permute-start | bytes 245768 | tf_op jit(solution)/shard_map/ppermute | solution.py:717
  9.0 1.7 %collective-permute-start.2 = (f32[160,128]{1,0:T(8,128)}, f32[160,128]{1,0:T(8,128)S(1)}, u32[]{:S(2)}, u32[]{:S(2)}) collective-permute-start(f32[160,128]{1,0:T(8,128)} %get-tuple-element.22), channel_id=1, source_target_pairs={{0,12},{1,13},{2,14},{3,15},{4,0},{5,1},{6,2},{7,3},{8,4},{9,5},{1... | collective-permute-start | bytes 245768 | tf_op jit(solution)/shard_map/ppermute | solution.py:717
  10.8 2.4 %collective-permute-start.3 = (f32[160,128]{1,0:T(8,128)}, f32[160,128]{1,0:T(8,128)S(1)}, u32[]{:S(2)}, u32[]{:S(2)}) collective-permute-start(f32[160,128]{1,0:T(8,128)} %get-tuple-element.23), channel_id=1, source_target_pairs={{0,19},{1,16},{2,17},{3,18},{4,23},{5,20},{6,21},{7,22},{8,27},{9,... | collective-permute-start | bytes 245768 | tf_op jit(solution)/shard_map/ppermute | solution.py:717
  13.2 0.7 %collective-permute-done.same_first.refs_0_ = f32[160,128]{1,0:T(8,128)S(1)} collective-permute-done((f32[160,128]{1,0:T(8,128)}, f32[160,128]{1,0:T(8,128)S(1)}, u32[]{:S(2)}, u32[]{:S(2)}) %collective-permute-start) | collective-permute-done | bytes 81952 | tf_op jit(solution)/shard_map/ppermute | solution.py:717
  13.9 0.0 collective-permute-done.2.below.refs_3_
  13.9 4.3 %collective-permute-done.3.other_first.other = f32[160,128]{1,0:T(8,128)S(1)} collective-permute-done((f32[160,128]{1,0:T(8,128)}, f32[160,128]{1,0:T(8,128)S(1)}, u32[]{:S(2)}, u32[]{:S(2)}) %collective-permute-start.3) | collective-permute-done | bytes 81952 | tf_op jit(solution)/shard_map/ppermute | solution.py:717
  18.2 1.3 %copy-done = f32[5,4,128,128]{3,2,1,0:T(8,128)S(1)} copy-done((f32[5,4,128,128]{3,2,1,0:T(8,128)S(1)}, f32[5,4,128,128]{3,2,1,0:T(8,128)}, u32[]{:S(2)}) %copy-start) | copy-done | bytes 1310744
  19.5 0.3 shard_map.68
  19.8 0.8 %collective-permute-start.7 = (f32[664,128]{1,0:T(8,128)S(1)}, f32[664,128]{1,0:T(8,128)S(1)}, u32[]{:S(2)}, u32[]{:S(2)}) collective-permute-start(f32[664,128]{1,0:T(8,128)S(1)} %get-tuple-element.27), channel_id=1, source_target_pairs={{0,16},{1,17},{2,18},{3,19},{4,20},{5,21},{6,22},{7,23},{8,24},{9,... | collective-permute-start | bytes 1019912 | tf_op jit(solution)/shard_map/ppermute | solution.py:717
  20.6 2.9 %collective-permute-start.6 = (f32[24,128]{1,0:T(8,128)S(1)}, f32[24,128]{1,0:T(8,128)S(1)}, u32[]{:S(2)}, u32[]{:S(2)}) collective-permute-start(f32[24,128]{1,0:T(8,128)S(1)} %get-tuple-element.26), channel_id=1, source_target_pairs={{0,19},{1,16},{2,17},{3,18},{4,23},{5,20},{6,21},{7,22},{8,27},{9,... | collective-permute-start | bytes 36872 | tf_op jit(solution)/shard_map/ppermute | solution.py:717
  23.6 0.3 shard_map.70.near
  23.9 2.2 %collective-permute-done.4.refs_1_ = f32[24,128]{1,0:T(8,128)S(1)} collective-permute-done((f32[24,128]{1,0:T(8,128)S(1)}, f32[24,128]{1,0:T(8,128)S(1)}, u32[]{:S(2)}, u32[]{:S(2)}) %collective-permute-start.4) | collective-permute-done | bytes 12320 | tf_op jit(solution)/shard_map/ppermute | solution.py:717
  26.1 0.4 shard_map.69.near
  26.5 6.8 %shard_map.71 = (f32[5,4,64,128]{3,2,1,0:T(8,128)S(1)}, f32[640,128]{1,0:T(8,128)S(1)}) custom-call(f32[5,4,12,8,128]{4,3,2,1,0:T(8,128)S(1)} %shard_map.70.near, f32[160,128]{1,0:T(8,128)S(1)} %collective-permute-done.3.other_first.other, f32[960,128]{1,0:T(8,128)S(1)} %collective-permute-done.5.halves), custom_call_target="tpu_custom_call" | custom-call | flops 78643200 | bytes 19660800 | tf_op jit(solution)/shard_map/pallas_call | solution.py:761
  33.3 1.5 %collective-permute-start.9 = (f32[640,128]{1,0:T(8,128)S(1)}, f32[640,128]{1,0:T(8,128)S(1)}, u32[]{:S(2)}, u32[]{:S(2)}) collective-permute-start(f32[640,128]{1,0:T(8,128)S(1)} %get-tuple-element.31), channel_id=1, source_target_pairs={{16,0},{17,1},{18,2},{19,3},{20,4},{21,5},{22,6},{23,7},{24,8},{25... | collective-permute-start | bytes 983048 | tf_op jit(solution)/shard_map/ppermute | solution.py:49
  34.8 0.0 collective-permute-done.6.refs_0_
  34.8 8.0 %shard_map.72 = (f32[5,4,64,128]{3,2,1,0:T(8,128)S(1)}, f32[640,128]{1,0:T(8,128)S(1)}) custom-call(f32[5,4,14,8,128]{4,3,2,1,0:T(8,128)S(1)} %shard_map.69.near, f32[160,128]{1,0:T(8,128)S(1)} %collective-permute-done.3.other_first.other, f32[960,128]{1,0:T(8,128)S(1)} %collective-permute-done.5.halves, f32[24,128]{1,0:T(8,128)S(1)} %collective-permute-done.6.refs_0_, ...), custom_call_target="tpu_custom_call" | custom-call | flops 94371840 | bytes 23592960 | tf_op jit(solution)/shard_map/pallas_call | solution.py:761
  42.8 1.3 %collective-permute-start.8 = (f32[640,128]{1,0:T(8,128)S(1)}, f32[640,128]{1,0:T(8,128)S(1)}, u32[]{:S(2)}, u32[]{:S(2)}) collective-permute-start(f32[640,128]{1,0:T(8,128)S(1)} %get-tuple-element.30), channel_id=1, source_target_pairs={{16,0},{17,1},{18,2},{19,3},{20,4},{21,5},{22,6},{23,7},{24,8},{25... | collective-permute-start | bytes 983048 | tf_op jit(solution)/shard_map/ppermute | solution.py:49
  44.1 0.0 collective-permute-done.9.message
  44.1 1.0 %shard_map.73 = (f32[4,128,128]{2,1,0:T(8,128)}, f32[4,128,128]{2,1,0:T(8,128)}, f32[3,4,128,128]{3,2,1,0:T(8,128)}) custom-call(f32[5,4,64,128]{3,2,1,0:T(8,128)S(1)} %get-tuple-element.28.refs_2_.result, f32[640,128]{1,0:T(8,128)S(1)} %collective-permute-done.9.message), custom_call_target="tpu_custom_call" | custom-call | flops 1 | bytes 1 | tf_op jit(solution)/shard_map/pallas_call | solution.py:778
  45.1 6.7 %collective-permute-done.8.message = f32[640,128]{1,0:T(8,128)S(1)} collective-permute-done((f32[640,128]{1,0:T(8,128)S(1)}, f32[640,128]{1,0:T(8,128)S(1)}, u32[]{:S(2)}, u32[]{:S(2)}) %collective-permute-start.8) | collective-permute-done | bytes 327712 | tf_op jit(solution)/shard_map/ppermute | solution.py:49
  51.7 1.0 %shard_map.74 = (f32[4,128,128]{2,1,0:T(8,128)}, f32[4,128,128]{2,1,0:T(8,128)}, f32[3,4,128,128]{3,2,1,0:T(8,128)}) custom-call(f32[5,4,64,128]{3,2,1,0:T(8,128)S(1)} %get-tuple-element.29.result, f32[640,128]{1,0:T(8,128)S(1)} %collective-permute-done.8.message, ...), custom_call_target="tpu_custom_call", output_to_operand_aliasing={{0}: (2, {}), {1}: (3, {}), {2}: (4, {})} | custom-call | flops 1 | bytes 1 | tf_op jit(solution)/shard_map/pallas_call | solution.py:778
  (6 shorter events, 0.0 us)
Async XLA Ops:
  4.4 22.0 %collective-permute-start.5 = (f32[960,128]{1,0:T(8,128)}, f32[960,128]{1,0:T(8,128)S(1)}, u32[]{:S(2)}, u32[]{:S(2)}) collective-permute-start(f32[960,128]{1,0:T(8,128)} %get-tuple-element.25), channel_id=1, source_target_pairs={{0,16},{1,17},{2,18},{3,19},{4,20},{5,21},{6,22},{7,23},{8,24},{9,... | collective-permute-start | bytes 1474568 | tf_op jit(solution)/shard_map/ppermute | solution.py:717
  7.5 6.4 %collective-permute-start = (f32[160,128]{1,0:T(8,128)}, f32[160,128]{1,0:T(8,128)S(1)}, u32[]{:S(2)}, u32[]{:S(2)}) collective-permute-start(f32[160,128]{1,0:T(8,128)} %get-tuple-element.20), channel_id=1, source_target_pairs={{0,1},{1,2},{2,3},{3,0},{4,5},{5,6},{6,7},{7,4},{8,9},{9,10},{10,1... | collective-permute-start | bytes 245768 | tf_op jit(solution)/shard_map/ppermute | solution.py:717
  9.0 4.9 %collective-permute-start.1 = (f32[160,128]{1,0:T(8,128)}, f32[160,128]{1,0:T(8,128)S(1)}, u32[]{:S(2)}, u32[]{:S(2)}) collective-permute-start(f32[160,128]{1,0:T(8,128)} %get-tuple-element.21), channel_id=1, source_target_pairs={{0,4},{1,5},{2,6},{3,7},{4,8},{5,9},{6,10},{7,11},{8,12},{9,13},{1... | collective-permute-start | bytes 245768 | tf_op jit(solution)/shard_map/ppermute | solution.py:717
  9.0 4.9 %collective-permute-start.2 = (f32[160,128]{1,0:T(8,128)}, f32[160,128]{1,0:T(8,128)S(1)}, u32[]{:S(2)}, u32[]{:S(2)}) collective-permute-start(f32[160,128]{1,0:T(8,128)} %get-tuple-element.22), channel_id=1, source_target_pairs={{0,12},{1,13},{2,14},{3,15},{4,0},{5,1},{6,2},{7,3},{8,4},{9,5},{1... | collective-permute-start | bytes 245768 | tf_op jit(solution)/shard_map/ppermute | solution.py:717
  10.8 7.4 %collective-permute-start.3 = (f32[160,128]{1,0:T(8,128)}, f32[160,128]{1,0:T(8,128)S(1)}, u32[]{:S(2)}, u32[]{:S(2)}) collective-permute-start(f32[160,128]{1,0:T(8,128)} %get-tuple-element.23), channel_id=1, source_target_pairs={{0,19},{1,16},{2,17},{3,18},{4,23},{5,20},{6,21},{7,22},{8,27},{9,... | collective-permute-start | bytes 245768 | tf_op jit(solution)/shard_map/ppermute | solution.py:717
  18.2 1.3 %copy-start = (f32[5,4,128,128]{3,2,1,0:T(8,128)S(1)}, f32[5,4,128,128]{3,2,1,0:T(8,128)}, u32[]{:S(2)}) copy-start(f32[5,4,128,128]{3,2,1,0:T(8,128)} %get-tuple-element.19.fields) | copy-start | bytes 3932164
  19.8 15.0 %collective-permute-start.7 = (f32[664,128]{1,0:T(8,128)S(1)}, f32[664,128]{1,0:T(8,128)S(1)}, u32[]{:S(2)}, u32[]{:S(2)}) collective-permute-start(f32[664,128]{1,0:T(8,128)S(1)} %get-tuple-element.27), channel_id=1, source_target_pairs={{0,16},{1,17},{2,18},{3,19},{4,20},{5,21},{6,22},{7,23},{8,24},{9,... | collective-permute-start | bytes 1019912 | tf_op jit(solution)/shard_map/ppermute | solution.py:717
  20.6 5.5 %collective-permute-start.4 = (f32[24,128]{1,0:T(8,128)S(1)}, f32[24,128]{1,0:T(8,128)S(1)}, u32[]{:S(2)}, u32[]{:S(2)}) collective-permute-start(f32[24,128]{1,0:T(8,128)S(1)} %get-tuple-element.24), channel_id=1, source_target_pairs={{0,1},{1,2},{2,3},{3,0},{4,5},{5,6},{6,7},{7,4},{8,9},{9,10},{10,1... | collective-permute-start | bytes 36872 | tf_op jit(solution)/shard_map/ppermute | solution.py:717
  20.6 14.2 %collective-permute-start.6 = (f32[24,128]{1,0:T(8,128)S(1)}, f32[24,128]{1,0:T(8,128)S(1)}, u32[]{:S(2)}, u32[]{:S(2)}) collective-permute-start(f32[24,128]{1,0:T(8,128)S(1)} %get-tuple-element.26), channel_id=1, source_target_pairs={{0,19},{1,16},{2,17},{3,18},{4,23},{5,20},{6,21},{7,22},{8,27},{9,... | collective-permute-start | bytes 36872 | tf_op jit(solution)/shard_map/ppermute | solution.py:717
  33.3 10.8 %collective-permute-start.9 = (f32[640,128]{1,0:T(8,128)S(1)}, f32[640,128]{1,0:T(8,128)S(1)}, u32[]{:S(2)}, u32[]{:S(2)}) collective-permute-start(f32[640,128]{1,0:T(8,128)S(1)} %get-tuple-element.31), channel_id=1, source_target_pairs={{16,0},{17,1},{18,2},{19,3},{20,4},{21,5},{22,6},{23,7},{24,8},{25... | collective-permute-start | bytes 983048 | tf_op jit(solution)/shard_map/ppermute | solution.py:49
  42.8 9.0 %collective-permute-start.8 = (f32[640,128]{1,0:T(8,128)S(1)}, f32[640,128]{1,0:T(8,128)S(1)}, u32[]{:S(2)}, u32[]{:S(2)}) collective-permute-start(f32[640,128]{1,0:T(8,128)S(1)} %get-tuple-element.30), channel_id=1, source_target_pairs={{16,0},{17,1},{18,2},{19,3},{20,4},{21,5},{22,6},{23,7},{24,8},{25... | collective-permute-start | bytes 983048 | tf_op jit(solution)/shard_map/ppermute | solution.py:49

commit v8 on v7

--- a/solution.py
+++ b/solution.py
@@ -327,7 +327,7 @@
             last[spot, :] = fields[field, plane, pl.ds(rows - TILE, TILE), :]
 
 
-def rims_kernel(fields, above, below, same_first, other_first, halves, same, other):
+def rims_kernel(fields, other_first, same_first, above, below, halves, same, other):
     _, slab, rows, _ = fields.shape
     side = lax.axis_index("grow")
     theirs = jnp.logical_not(half_of(side))
@@ -361,7 +361,7 @@
 def own_kernel(part, fields, *refs):
     out, natural = refs[-2:]
     same, *more = refs[:-2]
-    same_rims, above, below = more or (None, None, None)
+    same_rims, above, below, _ = more or (None,) * 4
     _, slab, rows, _ = fields.shape
     count = FIELDS * slab
     outer = (LANES - REACH) * (1 - lax.axis_index("grow"))
@@ -684,7 +684,9 @@
 def call(kernel, outs, scratch=(), limit=48, **how):
     return pl.pallas_call(
         kernel,
-        out_shape=[jax.ShapeDtypeStruct(shape, jnp.float32) for shape in outs],
+        out_shape=[
+            jax.ShapeDtypeStruct(one, jnp.float32) if isinstance(one, tuple) else one for one in outs
+        ],
         scratch_shapes=[
             pltpu.VMEM(one, jnp.float32) if isinstance(one, tuple) else one for one in scratch
         ],
@@ -731,7 +733,10 @@
     thin = (count * TILE, LANES)
     fields, halves, same, other, first, last = call(
         prepare_kernel,
-        [(FIELDS,) + labels.shape, (count * (half + TILE), LANES)] + [thin] * 4,
+        [
+            pltpu.VMEM(shape, jnp.float32)
+            for shape in ((FIELDS,) + labels.shape, (count * (half + TILE), LANES), *[thin] * 4)
+        ],
         [pltpu.VMEM(labels.shape, labels.dtype), labels.shape, pltpu.SemaphoreType.DMA((4,))],
         limit=54,
         in_specs=[hbm] * 4,
@@ -744,8 +749,8 @@
     rest, same_rims, other_rims = call(
         rims_kernel,
         [(count * (start + TILE) + spare, LANES)] + [(spare, LANES)] * 2,
-        in_specs=[in_vmem] * 3 + [anywhere] * 2,
-    )(fields, above, below, same, other)
+        in_specs=[in_vmem] + [anywhere] * 2 + [in_vmem] * 2,
+    )(fields, other, same, above, below)
     rest = to_partner(rest)
     other_rims = beside_other(other_rims)
     same_rims = beside_same(same_rims)
@@ -757,7 +762,8 @@
             functools.partial(own_kernel, part),
             [(FIELDS, slab) + deep[1:]],
             [(count, span, LANES)],
-        )(fields, same, *([same_rims, above, below] if part else []))
+            in_specs=[in_vmem] * (2 + 3 * part) + [anywhere] * part,
+        )(fields, same, *([same_rims, above, below, *results] if part else []))
         result, message = call(
             functools.partial(steps_kernel, part),
             [(FIELDS, slab, rows // 2, LANES), (count * rows // 4, LANES)],

time: 53.1 us -> 48.5 us (0.913)
  waiting for transfers between devices: 13.9 us -> 11.2 us
  local copies, waits for them, and re-layouts: 1.32 us -> 0 us
  Pallas kernels: 21.5 us -> 20.3 us
  starting transfers between devices: 15.3 us -> 15.9 us
    ppermute x8, waiting for transfers between devices: 7.19 us -> 3.07 us  [send(): return lax.ppermute(block, ('grow', 'cy', 'cz'), pairs)]
    ppermute x2, waiting for transfers between devices: 6.67 us -> 8.14 us  [from_behind(): return lax.ppermute(block, axis, route)]
    unnamed x2 -> x0, local copies, waits for them, and re-layouts: 1.32 us -> none
    pallas_call x1, Pallas kernels: 3.81 us -> 2.61 us  [pair_shards(): call(prepare_kernel, [pltpu.VMEM(shape, jnp.float32) for shape in ((FIELD...]
    ppermute x8, starting transfers between devices: 12.6 us -> 13.1 us  [send(): return lax.ppermute(block, ('grow', 'cy', 'cz'), pairs)]
  transfers between devices with their start and end apart: 10 -> 10, of which waited for: 4 -> 3; matrix products, arithmetic and copies ran while one was open for 0% -> 0% of each run, Pallas kernels for 32% -> 35%
where the time goes in v8:
time: 48.5 us; the launch traced here: 48.3 us
  Pallas kernels  20.3 us (42%)
  starting transfers between devices  15.9 us (33%)
  waiting for transfers between devices  11.2 us (23%)
  between operations  0.89 us (2%)
    pallas_call x2, Pallas kernels, pair_shards(): call(functools.partial(steps_kernel, part), [(FIELDS, slab, rows // 2, LA...  14.8 us
    ppermute x8, starting transfers between devices, send(): return lax.ppermute(block, ('grow', 'cy', 'cz'), pairs)  13.1 us
    ppermute x2, waiting for transfers between devices, from_behind(): return lax.ppermute(block, axis, route)  8.14 us
    ppermute x8, waiting for transfers between devices, send(): return lax.ppermute(block, ('grow', 'cy', 'cz'), pairs)  3.07 us
    ppermute x2, starting transfers between devices, from_behind(): return lax.ppermute(block, axis, route)  2.76 us
    pallas_call x1, Pallas kernels, pair_shards(): call(prepare_kernel, [pltpu.VMEM(shape, jnp.float32) for shape in ((FIELD...  2.61 us
    pallas_call x2, Pallas kernels, pair_shards(): call(functools.partial(finish_kernel, part), [labels.shape, labels.shape,...  1.99 us
  transfers between devices with their start and end apart: 10, of which 3 were waited for; matrix products, arithmetic and copies ran while one was open for 0% of the time, Pallas kernels for 35%

profile of v8, /device:TPU:0, one launch (start us, length us, event | category | flops | bytes accessed | tf_op | source)
XLA Modules:
  0.0 48.3 jit_solution(8451595567996688522)
XLA Ops:
  0.6 2.6 %shard_map.67 = (f32[5,4,128,128]{3,2,1,0:T(8,128)S(1)}, f32[960,128]{1,0:T(8,128)S(1)}, f32[160,128]{1,0:T(8,128)S(1)}, f32[160,128]{1,0:T(8,128)S(1)}, f32[160,128]{1,0:T(8,128)S(1)}, /*index=5*/f32[160,128]{1,0:T(8,128)S(1)}) custom-call(s32[4,128,128]{2,1,0:T(8,128)} %labels.1, f32[4,128,128]{2,1,0:T(8,128)} %roughness.1, f32[4,128,128]{2,1,0:T(8,128)} %potential.1, ...), custom_call_target="tpu_custom_call" | custom-call | flops 1 | bytes 1 | tf_op jit(solution)/shard_map/pallas_call | solution.py:734
  3.2 3.0 %collective-permute-start.5 = (f32[960,128]{1,0:T(8,128)S(1)}, f32[960,128]{1,0:T(8,128)S(1)}, u32[]{:S(2)}, u32[]{:S(2)}) collective-permute-start(f32[960,128]{1,0:T(8,128)S(1)} %get-tuple-element.25), channel_id=1, source_target_pairs={{0,16},{1,17},{2,18},{3,19},{4,20},{5,21},{6,22},{7,23},{8,24},{9,... | collective-permute-start | bytes 1474568 | tf_op jit(solution)/shard_map/ppermute | solution.py:719
  6.3 1.6 %collective-permute-start = (f32[160,128]{1,0:T(8,128)S(1)}, f32[160,128]{1,0:T(8,128)S(1)}, u32[]{:S(2)}, u32[]{:S(2)}) collective-permute-start(f32[160,128]{1,0:T(8,128)S(1)} %get-tuple-element.20), channel_id=1, source_target_pairs={{0,1},{1,2},{2,3},{3,0},{4,5},{5,6},{6,7},{7,4},{8,9},{9,10},{10,1... | collective-permute-start | bytes 245768 | tf_op jit(solution)/shard_map/ppermute | solution.py:719
  7.8 2.4 %collective-permute-start.1 = (f32[160,128]{1,0:T(8,128)S(1)}, f32[160,128]{1,0:T(8,128)S(1)}, u32[]{:S(2)}, u32[]{:S(2)}) collective-permute-start(f32[160,128]{1,0:T(8,128)S(1)} %get-tuple-element.21), channel_id=1, source_target_pairs={{0,19},{1,16},{2,17},{3,18},{4,23},{5,20},{6,21},{7,22},{8,27},{9,... | collective-permute-start | bytes 245768 | tf_op jit(solution)/shard_map/ppermute | solution.py:719
  10.3 1.7 %collective-permute-start.3 = (f32[160,128]{1,0:T(8,128)S(1)}, f32[160,128]{1,0:T(8,128)S(1)}, u32[]{:S(2)}, u32[]{:S(2)}) collective-permute-start(f32[160,128]{1,0:T(8,128)S(1)} %get-tuple-element.23), channel_id=1, source_target_pairs={{0,12},{1,13},{2,14},{3,15},{4,0},{5,1},{6,2},{7,3},{8,4},{9,5},{1... | collective-permute-start | bytes 245768 | tf_op jit(solution)/shard_map/ppermute | solution.py:719
  12.0 1.0 %collective-permute-done.same_first.refs_0_ = f32[160,128]{1,0:T(8,128)S(1)} collective-permute-done((f32[160,128]{1,0:T(8,128)S(1)}, f32[160,128]{1,0:T(8,128)S(1)}, u32[]{:S(2)}, u32[]{:S(2)}) %collective-permute-start) | collective-permute-done | bytes 81952 | tf_op jit(solution)/shard_map/ppermute | solution.py:719
  13.0 2.1 %collective-permute-done.1.other_first.other = f32[160,128]{1,0:T(8,128)S(1)} collective-permute-done((f32[160,128]{1,0:T(8,128)S(1)}, f32[160,128]{1,0:T(8,128)S(1)}, u32[]{:S(2)}, u32[]{:S(2)}) %collective-permute-start.1) | collective-permute-done | bytes 81952 | tf_op jit(solution)/shard_map/ppermute | solution.py:719
  15.1 0.0 collective-permute-done.2.above.refs_2_
  15.1 0.0 collective-permute-done.3.below.refs_3_
  15.1 0.3 shard_map.68
  15.4 0.8 %collective-permute-start.7 = (f32[664,128]{1,0:T(8,128)S(1)}, f32[664,128]{1,0:T(8,128)S(1)}, u32[]{:S(2)}, u32[]{:S(2)}) collective-permute-start(f32[664,128]{1,0:T(8,128)S(1)} %get-tuple-element.28), channel_id=1, source_target_pairs={{0,16},{1,17},{2,18},{3,19},{4,20},{5,21},{6,22},{7,23},{8,24},{9,... | collective-permute-start | bytes 1019912 | tf_op jit(solution)/shard_map/ppermute | solution.py:719
  16.2 0.5 collective-permute-start.4
  16.7 3.1 %collective-permute-start.6 = (f32[24,128]{1,0:T(8,128)S(1)}, f32[24,128]{1,0:T(8,128)S(1)}, u32[]{:S(2)}, u32[]{:S(2)}) collective-permute-start(f32[24,128]{1,0:T(8,128)S(1)} %get-tuple-element.27), channel_id=1, source_target_pairs={{0,19},{1,16},{2,17},{3,18},{4,23},{5,20},{6,21},{7,22},{8,27},{9,... | collective-permute-start | bytes 36872 | tf_op jit(solution)/shard_map/ppermute | solution.py:719
  19.7 0.3 shard_map.69.near
  20.0 0.0 collective-permute-done.5.halves
  20.1 6.8 %shard_map.70 = (f32[5,4,64,128]{3,2,1,0:T(8,128)S(1)}, f32[640,128]{1,0:T(8,128)S(1)}) custom-call(f32[5,4,12,8,128]{4,3,2,1,0:T(8,128)S(1)} %shard_map.69.near, f32[160,128]{1,0:T(8,128)S(1)} %collective-permute-done.1.other_first.other, f32[960,128]{1,0:T(8,128)S(1)} %collective-permute-done.5.halves), custom_call_target="tpu_custom_call" | custom-call | flops 78643200 | bytes 19660800 | tf_op jit(solution)/shard_map/pallas_call | solution.py:767
  26.9 1.5 %collective-permute-start.9 = (f32[640,128]{1,0:T(8,128)S(1)}, f32[640,128]{1,0:T(8,128)S(1)}, u32[]{:S(2)}, u32[]{:S(2)}) collective-permute-start(f32[640,128]{1,0:T(8,128)S(1)} %get-tuple-element.31), channel_id=1, source_target_pairs={{16,0},{17,1},{18,2},{19,3},{20,4},{21,5},{22,6},{23,7},{24,8},{25... | collective-permute-start | bytes 983048 | tf_op jit(solution)/shard_map/ppermute | solution.py:49
  28.3 0.0 collective-permute-done.4.refs_1_
  28.4 0.4 shard_map.71.near
  28.8 8.0 %shard_map.72 = (f32[5,4,64,128]{3,2,1,0:T(8,128)S(1)}, f32[640,128]{1,0:T(8,128)S(1)}) custom-call(f32[5,4,14,8,128]{4,3,2,1,0:T(8,128)S(1)} %shard_map.71.near, f32[160,128]{1,0:T(8,128)S(1)} %collective-permute-done.1.other_first.other, f32[960,128]{1,0:T(8,128)S(1)} %collective-permute-done.5.halves, f32[24,128]{1,0:T(8,128)S(1)} %collective-permute-done.6.refs_0_, ...), custom_call_target="tpu_custom_call" | custom-call | flops 94371840 | bytes 23592960 | tf_op jit(solution)/shard_map/pallas_call | solution.py:767
  36.7 1.3 %collective-permute-start.8 = (f32[640,128]{1,0:T(8,128)S(1)}, f32[640,128]{1,0:T(8,128)S(1)}, u32[]{:S(2)}, u32[]{:S(2)}) collective-permute-start(f32[640,128]{1,0:T(8,128)S(1)} %get-tuple-element.30), channel_id=1, source_target_pairs={{16,0},{17,1},{18,2},{19,3},{20,4},{21,5},{22,6},{23,7},{24,8},{25... | collective-permute-start | bytes 983048 | tf_op jit(solution)/shard_map/ppermute | solution.py:49
  38.0 1.0 %shard_map.73 = (f32[4,128,128]{2,1,0:T(8,128)}, f32[4,128,128]{2,1,0:T(8,128)}, f32[3,4,128,128]{3,2,1,0:T(8,128)}) custom-call(f32[5,4,64,128]{3,2,1,0:T(8,128)S(1)} %get-tuple-element.26.refs_4_.refs_2_.result, f32[640,128]{1,0:T(8,128)S(1)} %collective-permute-done.9.message), custom_call_target="tpu_custom_call" | custom-call | flops 1 | bytes 1 | tf_op jit(solution)/shard_map/pallas_call | solution.py:784
  39.0 8.1 %collective-permute-done.8.message = f32[640,128]{1,0:T(8,128)S(1)} collective-permute-done((f32[640,128]{1,0:T(8,128)S(1)}, f32[640,128]{1,0:T(8,128)S(1)}, u32[]{:S(2)}, u32[]{:S(2)}) %collective-permute-start.8) | collective-permute-done | bytes 327712 | tf_op jit(solution)/shard_map/ppermute | solution.py:49
  47.2 1.0 %shard_map.74 = (f32[4,128,128]{2,1,0:T(8,128)}, f32[4,128,128]{2,1,0:T(8,128)}, f32[3,4,128,128]{3,2,1,0:T(8,128)}) custom-call(f32[5,4,64,128]{3,2,1,0:T(8,128)S(1)} %get-tuple-element.29.result, f32[640,128]{1,0:T(8,128)S(1)} %collective-permute-done.8.message, ...), custom_call_target="tpu_custom_call", output_to_operand_aliasing={{0}: (2, {}), {1}: (3, {}), {2}: (4, {})} | custom-call | flops 1 | bytes 1 | tf_op jit(solution)/shard_map/pallas_call | solution.py:784
  (4 shorter events, 0.0 us)
Async XLA Ops:
  3.2 16.8 %collective-permute-start.5 = (f32[960,128]{1,0:T(8,128)S(1)}, f32[960,128]{1,0:T(8,128)S(1)}, u32[]{:S(2)}, u32[]{:S(2)}) collective-permute-start(f32[960,128]{1,0:T(8,128)S(1)} %get-tuple-element.25), channel_id=1, source_target_pairs={{0,16},{1,17},{2,18},{3,19},{4,20},{5,21},{6,22},{7,23},{8,24},{9,... | collective-permute-start | bytes 1474568 | tf_op jit(solution)/shard_map/ppermute | solution.py:719
  6.3 6.7 %collective-permute-start = (f32[160,128]{1,0:T(8,128)S(1)}, f32[160,128]{1,0:T(8,128)S(1)}, u32[]{:S(2)}, u32[]{:S(2)}) collective-permute-start(f32[160,128]{1,0:T(8,128)S(1)} %get-tuple-element.20), channel_id=1, source_target_pairs={{0,1},{1,2},{2,3},{3,0},{4,5},{5,6},{6,7},{7,4},{8,9},{9,10},{10,1... | collective-permute-start | bytes 245768 | tf_op jit(solution)/shard_map/ppermute | solution.py:719
  7.8 7.2 %collective-permute-start.1 = (f32[160,128]{1,0:T(8,128)S(1)}, f32[160,128]{1,0:T(8,128)S(1)}, u32[]{:S(2)}, u32[]{:S(2)}) collective-permute-start(f32[160,128]{1,0:T(8,128)S(1)} %get-tuple-element.21), channel_id=1, source_target_pairs={{0,19},{1,16},{2,17},{3,18},{4,23},{5,20},{6,21},{7,22},{8,27},{9,... | collective-permute-start | bytes 245768 | tf_op jit(solution)/shard_map/ppermute | solution.py:719
  10.3 4.8 %collective-permute-start.2 = (f32[160,128]{1,0:T(8,128)S(1)}, f32[160,128]{1,0:T(8,128)S(1)}, u32[]{:S(2)}, u32[]{:S(2)}) collective-permute-start(f32[160,128]{1,0:T(8,128)S(1)} %get-tuple-element.22), channel_id=1, source_target_pairs={{0,4},{1,5},{2,6},{3,7},{4,8},{5,9},{6,10},{7,11},{8,12},{9,13},{1... | collective-permute-start | bytes 245768 | tf_op jit(solution)/shard_map/ppermute | solution.py:719
  10.3 4.8 %collective-permute-start.3 = (f32[160,128]{1,0:T(8,128)S(1)}, f32[160,128]{1,0:T(8,128)S(1)}, u32[]{:S(2)}, u32[]{:S(2)}) collective-permute-start(f32[160,128]{1,0:T(8,128)S(1)} %get-tuple-element.23), channel_id=1, source_target_pairs={{0,12},{1,13},{2,14},{3,15},{4,0},{5,1},{6,2},{7,3},{8,4},{9,5},{1... | collective-permute-start | bytes 245768 | tf_op jit(solution)/shard_map/ppermute | solution.py:719
  15.4 13.4 %collective-permute-start.7 = (f32[664,128]{1,0:T(8,128)S(1)}, f32[664,128]{1,0:T(8,128)S(1)}, u32[]{:S(2)}, u32[]{:S(2)}) collective-permute-start(f32[664,128]{1,0:T(8,128)S(1)} %get-tuple-element.28), channel_id=1, source_target_pairs={{0,16},{1,17},{2,18},{3,19},{4,20},{5,21},{6,22},{7,23},{8,24},{9,... | collective-permute-start | bytes 1019912 | tf_op jit(solution)/shard_map/ppermute | solution.py:719
  16.2 12.2 %collective-permute-start.4 = (f32[24,128]{1,0:T(8,128)S(1)}, f32[24,128]{1,0:T(8,128)S(1)}, u32[]{:S(2)}, u32[]{:S(2)}) collective-permute-start(f32[24,128]{1,0:T(8,128)S(1)} %get-tuple-element.24), channel_id=1, source_target_pairs={{0,1},{1,2},{2,3},{3,0},{4,5},{5,6},{6,7},{7,4},{8,9},{9,10},{10,1... | collective-permute-start | bytes 36872 | tf_op jit(solution)/shard_map/ppermute | solution.py:719
  16.7 12.1 %collective-permute-start.6 = (f32[24,128]{1,0:T(8,128)S(1)}, f32[24,128]{1,0:T(8,128)S(1)}, u32[]{:S(2)}, u32[]{:S(2)}) collective-permute-start(f32[24,128]{1,0:T(8,128)S(1)} %get-tuple-element.27), channel_id=1, source_target_pairs={{0,19},{1,16},{2,17},{3,18},{4,23},{5,20},{6,21},{7,22},{8,27},{9,... | collective-permute-start | bytes 36872 | tf_op jit(solution)/shard_map/ppermute | solution.py:719
  26.9 11.1 %collective-permute-start.9 = (f32[640,128]{1,0:T(8,128)S(1)}, f32[640,128]{1,0:T(8,128)S(1)}, u32[]{:S(2)}, u32[]{:S(2)}) collective-permute-start(f32[640,128]{1,0:T(8,128)S(1)} %get-tuple-element.31), channel_id=1, source_target_pairs={{16,0},{17,1},{18,2},{19,3},{20,4},{21,5},{22,6},{23,7},{24,8},{25... | collective-permute-start | bytes 983048 | tf_op jit(solution)/shard_map/ppermute | solution.py:49
  36.7 10.5 %collective-permute-start.8 = (f32[640,128]{1,0:T(8,128)S(1)}, f32[640,128]{1,0:T(8,128)S(1)}, u32[]{:S(2)}, u32[]{:S(2)}) collective-permute-start(f32[640,128]{1,0:T(8,128)S(1)} %get-tuple-element.30), channel_id=1, source_target_pairs={{16,0},{17,1},{18,2},{19,3},{20,4},{21,5},{22,6},{23,7},{24,8},{25... | collective-permute-start | bytes 983048 | tf_op jit(solution)/shard_map/ppermute | solution.py:49

commit v9 on v8

--- a/solution.py
+++ b/solution.py
@@ -216,6 +216,7 @@
 REACH = STEPS * (SWEEPS + 1)
 TILE = 8
 FIELDS = 5
+PER_TILE = 1
 LAG = 2
 TOGETHER = 12
 
@@ -264,8 +265,7 @@
             out[pl.ds(start + (field * slab + plane) * TILE, TILE), :] = packed
 
 
-def pack_rim_strips(above, below, base, out, start):
-    per = LANES // REACH
+def pack_rim_strips(above, below, base, out, start, per):
     blocks = 2 * above.shape[0] // TILE
     for first in range(0, blocks, per):
         packed = jnp.zeros((TILE, LANES), jnp.float32)
@@ -282,7 +282,8 @@
 
 
 def split(rows):
-    return rows // 4 - REACH, 3 * rows // 4 + REACH
+    edge = rows // TILE * 3 // 16 * TILE
+    return edge - REACH, rows - edge + REACH
 
 
 def prepare_kernel(
@@ -338,9 +339,10 @@
         spot = pl.ds(which * TILE, TILE)
         rims = jnp.where(theirs, above[spot, :], turned(below[spot, :], LANES // 2))
         halves[pl.ds(count * start + which * TILE, TILE), :] = rims
-    starts = (count * (start + TILE), 0, 0)
-    for out, at, base in zip((halves, same, other), starts, strip_bases(side)):
-        pack_rim_strips(above, below, base, out, at)
+    inner, *outer = strip_bases(side)
+    pack_rim_strips(above, below, inner, halves, count * (start + TILE), LANES // REACH)
+    for out, base in zip((same, other), outer):
+        pack_rim_strips(above, below, base, out, 0, PER_TILE)
 
 
 def blocks_of(part, rows):
@@ -351,10 +353,10 @@
     return list(range(-REACH, inner, TILE)) + list(range(rows - inner, rows + REACH, TILE))
 
 
-def packed_at(which, row, rows, count):
+def packed_at(which, row, rows, per):
     if 0 <= row < rows:
         return False, which * TILE, row // TILE * REACH
-    at, group = divmod(2 * which + int(row > 0), LANES // REACH)
+    at, group = divmod(2 * which + int(row > 0), per)
     return True, at * TILE, group * REACH
 
 
@@ -371,7 +373,7 @@
         for plane in range(slab):
             which = field * slab + plane
             for at, row in enumerate(blocks_of(part, rows)):
-                of_rim, spot, lane = packed_at(which, row, rows, count)
+                of_rim, spot, lane = packed_at(which, row, rows, PER_TILE)
                 piece = (same_rims if of_rim else same)[pl.ds(spot, TILE), :]
                 if of_rim:
                     near = (below if row > 0 else above)[pl.ds(which * TILE, TILE), :]
@@ -389,13 +391,12 @@
     return COND_EL + COND_LI * step
 
 
-def steps_kernel(part, near, other, halves, *refs):
+def steps_kernel(part, all_rows, near, other, halves, *refs):
     if part:
         other_rims, rest, _, *refs = refs
     result, message, natural, phase, phase_new, pot, pot_new, disp, disp_new = refs[:9]
     slopes, slopes_y, cond_x, cond_y, cond_y_back, cond_z = refs[9:]
-    _, slab, rows, _ = result.shape
-    all_rows = 2 * rows
+    slab = result.shape[1]
     planes = 2 * slab
     side = lax.axis_index("grow")
     mine = half_of(side)
@@ -422,15 +423,17 @@
         for plane in range(slab):
             which = field * slab + plane
             for at, row in enumerate(blocks):
-                of_rim, spot, lane = packed_at(which, row, all_rows, count)
+                of_rim, spot, lane = packed_at(which, row, all_rows, LANES // REACH)
+                back = outer - lane
                 if of_rim:
                     strip = rest[pl.ds(count * (start + TILE) + spot, TILE), :]
-                    beside = other_rims[pl.ds(spot, TILE), :]
+                    _, spot, beside_lane = packed_at(which, row, all_rows, PER_TILE)
+                    beside, back = other_rims[pl.ds(spot, TILE), :], outer - beside_lane
                 else:
                     strip = halves[pl.ds(count * half + spot, TILE), :]
                     beside = other[pl.ds(spot, TILE), :]
                 block = jnp.where(in_inner, turned(strip, inner - lane), arrived_half(which, row))
-                block = jnp.where(in_outer, turned(beside, outer - lane), block)
+                block = jnp.where(in_outer, turned(beside, back), block)
                 natural[field, plane, pl.ds(at * TILE, TILE), :] = block
 
     def parts_of(phase, pot, disp):
@@ -645,10 +648,11 @@
 
 
 def results_of(part, rows):
-    quarter = rows // 4
+    start, stop = split(rows)
+    edge = start + REACH
     if part == 0:
-        return list(range(quarter, 3 * quarter, TILE))
-    return list(range(0, quarter, TILE)) + list(range(3 * quarter, rows, TILE))
+        return list(range(edge, rows - edge, TILE))
+    return list(range(0, edge, TILE)) + list(range(rows - edge, rows, TILE))
 
 
 def finish_kernel(part, result, message, *refs):
@@ -658,6 +662,8 @@
     mine = half_of(side)
     fresh = side == lax.axis_size("grow") - 1
     half = rows // 2
+    edge = (phase.shape[1] - rows) // 2
+    targets = (0, phase.shape[1] - half) if part else (edge, edge + half)
     copies = []
     for field in range(FIELDS):
         for plane in range(slab):
@@ -669,7 +675,7 @@
                 block = jnp.where(fresh, V_HIGH if field == 1 else 0.0, block)
                 whole[field, plane, pl.ds(row, TILE), :] = block
         out = (phase, potential, displacement.at[0], displacement.at[1], displacement.at[2])[field]
-        for source, target in (((0, 0), (half, 3 * half)) if part else ((0, half), (half, rows))):
+        for source, target in zip((0, half), targets):
             copy = pltpu.make_async_copy(
                 whole.at[field, :, pl.ds(source, half), :],
                 out.at[:, pl.ds(target, half), :],
@@ -748,7 +754,7 @@
     same = beside_same(same)
     rest, same_rims, other_rims = call(
         rims_kernel,
-        [(count * (start + TILE) + spare, LANES)] + [(spare, LANES)] * 2,
+        [(count * (start + TILE) + spare, LANES)] + [(2 * count // PER_TILE * TILE, LANES)] * 2,
         in_specs=[in_vmem] + [anywhere] * 2 + [in_vmem] * 2,
     )(fields, other, same, above, below)
     rest = to_partner(rest)
@@ -756,7 +762,7 @@
     same_rims = beside_same(same_rims)
     results, messages, outs = [], [], []
     for part in range(2):
-        span = len(blocks_of(part, rows)) * TILE
+        span, done = (len(of(part, rows)) * TILE for of in (blocks_of, results_of))
         deep = (2 * slab, span // TILE + 2, TILE, LANES)
         (near,) = call(
             functools.partial(own_kernel, part),
@@ -765,8 +771,8 @@
             in_specs=[in_vmem] * (2 + 3 * part) + [anywhere] * part,
         )(fields, same, *([same_rims, above, below, *results] if part else []))
         result, message = call(
-            functools.partial(steps_kernel, part),
-            [(FIELDS, slab, rows // 2, LANES), (count * rows // 4, LANES)],
+            functools.partial(steps_kernel, part, rows),
+            [(FIELDS, slab, done, LANES), (count * done // 2, LANES)],
             [(FIELDS, slab, span, LANES)]
             + [deep] * 4
             + [(3,) + deep] * 2
@@ -784,7 +790,7 @@
         outs = call(
             functools.partial(finish_kernel, part),
             [labels.shape, labels.shape, displacement.shape],
-            [(FIELDS, slab, rows // 2, LANES), pltpu.SemaphoreType.DMA((2 * FIELDS,))],
+            [results[part].shape, pltpu.SemaphoreType.DMA((2 * FIELDS,))],
             in_specs=[in_vmem] * 2 + [hbm] * (3 * part),
             out_specs=[hbm] * 3,
             input_output_aliases={2 + which: which for which in range(3 * part)},
@@ -794,7 +800,8 @@
 
 def fits_pair(labels):
     rows, columns = labels.shape[1:]
-    blocks = rows % (8 * TILE) == 0 and rows // TILE * REACH <= LANES
+    start, stop = split(rows)
+    blocks = rows % (2 * TILE) == 0 and rows // TILE * REACH <= LANES and start >= TILE
     return lax.axis_size("grow") == 2 and columns == LANES and REACH == TILE and blocks
 
 

time: 48.5 us -> 50.4 us (1.039)
  the two profiles are of different devices: /device:TPU:0 before, /device:TPU:20 now
where the time goes in v9:
time: 50.4 us; the launch traced here: 50.2 us
  Pallas kernels  20.3 us (40%)
  waiting for transfers between devices  17.8 us (35%)
  starting transfers between devices  11.3 us (22%)
  between operations  0.9 us (2%)
    pallas_call x2, Pallas kernels, pair_shards(): call(functools.partial(steps_kernel, part, rows), [(FIELDS, slab, done, L...  14.7 us
    ppermute x8, waiting for transfers between devices, send(): return lax.ppermute(block, ('grow', 'cy', 'cz'), pairs)  12 us
    ppermute x8, starting transfers between devices, send(): return lax.ppermute(block, ('grow', 'cy', 'cz'), pairs)  8.52 us
    ppermute x2, waiting for transfers between devices, from_behind(): return lax.ppermute(block, axis, route)  5.75 us
    ppermute x2, starting transfers between devices, from_behind(): return lax.ppermute(block, axis, route)  2.76 us
    pallas_call x1, Pallas kernels, pair_shards(): call(prepare_kernel, [pltpu.VMEM(shape, jnp.float32) for shape in ((FIELD...  2.63 us
    pallas_call x2, Pallas kernels, pair_shards(): call(functools.partial(finish_kernel, part), [labels.shape, labels.shape,...  1.98 us
  transfers between devices with their start and end apart: 10, of which 5 were waited for; matrix products, arithmetic and copies ran while one was open for 0% of the time, Pallas kernels for 33%

profile of v9, /device:TPU:20, one launch (start us, length us, event | category | flops | bytes accessed | tf_op | source)
XLA Modules:
  0.0 50.2 jit_solution(10128919639516359671)
XLA Ops:
  0.6 2.6 %shard_map.67 = (f32[5,4,128,128]{3,2,1,0:T(8,128)S(1)}, f32[1120,128]{1,0:T(8,128)S(1)}, f32[160,128]{1,0:T(8,128)S(1)}, f32[160,128]{1,0:T(8,128)S(1)}, f32[16...) custom-call(s32[4,128,128]{2,1,0:T(8,128)} %labels.1, f32[4,128,128]{2,1,0:T(8,128)} %roughness.1, f32[4,128,128]{2,1,0:T(8,128)} %potential.1, ...), custom_call_target="tpu_custom_call" | custom-call | flops 1 | bytes 1 | tf_op jit(solution)/shard_map/pallas_call | solution.py:740
  3.3 1.6 %collective-permute-start.5 = (f32[1120,128]{1,0:T(8,128)S(1)}, f32[1120,128]{1,0:T(8,128)S(1)}, u32[]{:S(2)}, u32[]{:S(2)}) collective-permute-start(f32[1120,128]{1,0:T(8,128)S(1)} %get-tuple-element.25), channel_id=1, source_target_pairs={{0,16},{1,17},{2,18},{3,19},{4,20},{5,21},{6,22},{7,23},{8,24},{9,... | collective-permute-start | bytes 1720328 | tf_op jit(solution)/shard_map/ppermute | solution.py:725
  4.8 1.6 %collective-permute-start = (f32[160,128]{1,0:T(8,128)S(1)}, f32[160,128]{1,0:T(8,128)S(1)}, u32[]{:S(2)}, u32[]{:S(2)}) collective-permute-start(f32[160,128]{1,0:T(8,128)S(1)} %get-tuple-element.20), channel_id=1, source_target_pairs={{0,1},{1,2},{2,3},{3,0},{4,5},{5,6},{6,7},{7,4},{8,9},{9,10},{10,1... | collective-permute-start | bytes 245768 | tf_op jit(solution)/shard_map/ppermute | solution.py:725
  6.4 0.0 collective-permute-start.1
  6.4 0.0 collective-permute-start.2
  6.4 1.7 %collective-permute-start.3 = (f32[160,128]{1,0:T(8,128)S(1)}, f32[160,128]{1,0:T(8,128)S(1)}, u32[]{:S(2)}, u32[]{:S(2)}) collective-permute-start(f32[160,128]{1,0:T(8,128)S(1)} %get-tuple-element.23), channel_id=1, source_target_pairs={{0,12},{1,13},{2,14},{3,15},{4,0},{5,1},{6,2},{7,3},{8,4},{9,5},{1... | collective-permute-start | bytes 245768 | tf_op jit(solution)/shard_map/ppermute | solution.py:725
  8.2 2.0 %collective-permute-done.same_first.refs_0_ = f32[160,128]{1,0:T(8,128)S(1)} collective-permute-done((f32[160,128]{1,0:T(8,128)S(1)}, f32[160,128]{1,0:T(8,128)S(1)}, u32[]{:S(2)}, u32[]{:S(2)}) %collective-permute-start) | collective-permute-done | bytes 81952 | tf_op jit(solution)/shard_map/ppermute | solution.py:725
  10.1 2.3 %collective-permute-done.1.other_first.other = f32[160,128]{1,0:T(8,128)S(1)} collective-permute-done((f32[160,128]{1,0:T(8,128)S(1)}, f32[160,128]{1,0:T(8,128)S(1)}, u32[]{:S(2)}, u32[]{:S(2)}) %collective-permute-start.1) | collective-permute-done | bytes 81952 | tf_op jit(solution)/shard_map/ppermute | solution.py:725
  12.4 0.3 shard_map.68
  12.7 0.1 collective-permute-start.7
  12.8 2.2 %collective-permute-start.4 = (f32[320,128]{1,0:T(8,128)S(1)}, f32[320,128]{1,0:T(8,128)S(1)}, u32[]{:S(2)}, u32[]{:S(2)}) collective-permute-start(f32[320,128]{1,0:T(8,128)S(1)} %get-tuple-element.24), channel_id=1, source_target_pairs={{0,1},{1,2},{2,3},{3,0},{4,5},{5,6},{6,7},{7,4},{8,9},{9,10},{10,1... | collective-permute-start | bytes 491528 | tf_op jit(solution)/shard_map/ppermute | solution.py:725
  15.0 1.4 %collective-permute-start.6 = (f32[320,128]{1,0:T(8,128)S(1)}, f32[320,128]{1,0:T(8,128)S(1)}, u32[]{:S(2)}, u32[]{:S(2)}) collective-permute-start(f32[320,128]{1,0:T(8,128)S(1)} %get-tuple-element.27), channel_id=1, source_target_pairs={{0,19},{1,16},{2,17},{3,18},{4,23},{5,20},{6,21},{7,22},{8,27},{9,... | collective-permute-start | bytes 491528 | tf_op jit(solution)/shard_map/ppermute | solution.py:725
  16.3 0.4 shard_map.69.near
  16.7 7.8 %collective-permute-done.5.halves = f32[1120,128]{1,0:T(8,128)S(1)} collective-permute-done((f32[1120,128]{1,0:T(8,128)S(1)}, f32[1120,128]{1,0:T(8,128)S(1)}, u32[]{:S(2)}, u32[]{:S(2)}) %collective-permute-start.5) | collective-permute-done | bytes 573472 | tf_op jit(solution)/shard_map/ppermute | solution.py:725
  24.5 8.0 %shard_map.70 = (f32[5,4,80,128]{3,2,1,0:T(8,128)S(1)}, f32[800,128]{1,0:T(8,128)S(1)}) custom-call(f32[5,4,14,8,128]{4,3,2,1,0:T(8,128)S(1)} %shard_map.69.near, f32[160,128]{1,0:T(8,128)S(1)} %collective-permute-done.1.other_first.other, f32[1120,128]{1,0:T(8,128)S(1)} %collective-permute-done.5.halves), custom_call_target="tpu_custom_call" | custom-call | flops 94371840 | bytes 23592960 | tf_op jit(solution)/shard_map/pallas_call | solution.py:773
  32.5 1.5 %collective-permute-start.9 = (f32[800,128]{1,0:T(8,128)S(1)}, f32[800,128]{1,0:T(8,128)S(1)}, u32[]{:S(2)}, u32[]{:S(2)}) collective-permute-start(f32[800,128]{1,0:T(8,128)S(1)} %get-tuple-element.31), channel_id=1, source_target_pairs={{16,0},{17,1},{18,2},{19,3},{20,4},{21,5},{22,6},{23,7},{24,8},{25... | collective-permute-start | bytes 1228808 | tf_op jit(solution)/shard_map/ppermute | solution.py:49
  33.9 0.3 shard_map.71.near
  34.3 0.0 collective-permute-done.6.refs_0_
  34.3 6.7 %shard_map.72 = (f32[5,4,48,128]{3,2,1,0:T(8,128)S(1)}, f32[480,128]{1,0:T(8,128)S(1)}) custom-call(f32[5,4,12,8,128]{4,3,2,1,0:T(8,128)S(1)} %shard_map.71.near, f32[160,128]{1,0:T(8,128)S(1)} %collective-permute-done.1.other_first.other, f32[1120,128]{1,0:T(8,128)S(1)} %collective-permute-done.5.halves, f32[320,128]{1,0:T(8,128)S(1)} %collective-permute-done.6.refs_0_, ...), custom_call_target="tpu_custom_call" | custom-call | flops 78643200 | bytes 19660800 | tf_op jit(solution)/shard_map/pallas_call | solution.py:773
  41.0 1.3 %collective-permute-start.8 = (f32[480,128]{1,0:T(8,128)S(1)}, f32[480,128]{1,0:T(8,128)S(1)}, u32[]{:S(2)}, u32[]{:S(2)}) collective-permute-start(f32[480,128]{1,0:T(8,128)S(1)} %get-tuple-element.30), channel_id=1, source_target_pairs={{16,0},{17,1},{18,2},{19,3},{20,4},{21,5},{22,6},{23,7},{24,8},{25... | collective-permute-start | bytes 737288 | tf_op jit(solution)/shard_map/ppermute | solution.py:49
  42.3 2.3 %collective-permute-done.9.message = f32[800,128]{1,0:T(8,128)S(1)} collective-permute-done((f32[800,128]{1,0:T(8,128)S(1)}, f32[800,128]{1,0:T(8,128)S(1)}, u32[]{:S(2)}, u32[]{:S(2)}) %collective-permute-start.9) | collective-permute-done | bytes 409632 | tf_op jit(solution)/shard_map/ppermute | solution.py:49
  44.6 1.1 %shard_map.73 = (f32[4,128,128]{2,1,0:T(8,128)}, f32[4,128,128]{2,1,0:T(8,128)}, f32[3,4,128,128]{3,2,1,0:T(8,128)}) custom-call(f32[5,4,80,128]{3,2,1,0:T(8,128)S(1)} %get-tuple-element.26.refs_4_.refs_2_.result, f32[800,128]{1,0:T(8,128)S(1)} %collective-permute-done.9.message), custom_call_target="tpu_custom_call" | custom-call | flops 1 | bytes 1 | tf_op jit(solution)/shard_map/pallas_call | solution.py:790
  45.6 3.5 %collective-permute-done.8.message = f32[480,128]{1,0:T(8,128)S(1)} collective-permute-done((f32[480,128]{1,0:T(8,128)S(1)}, f32[480,128]{1,0:T(8,128)S(1)}, u32[]{:S(2)}, u32[]{:S(2)}) %collective-permute-start.8) | collective-permute-done | bytes 245792 | tf_op jit(solution)/shard_map/ppermute | solution.py:49
  49.2 0.9 %shard_map.74 = (f32[4,128,128]{2,1,0:T(8,128)}, f32[4,128,128]{2,1,0:T(8,128)}, f32[3,4,128,128]{3,2,1,0:T(8,128)}) custom-call(f32[5,4,48,128]{3,2,1,0:T(8,128)S(1)} %get-tuple-element.29.result, f32[480,128]{1,0:T(8,128)S(1)} %collective-permute-done.8.message, ...), custom_call_target="tpu_custom_call", output_to_operand_aliasing={{0}: (2, {}), {1}: (3, {}), {2}: (4, {})} | custom-call | flops 1 | bytes 1 | tf_op jit(solution)/shard_map/pallas_call | solution.py:790
  (4 shorter events, 0.0 us)
Async XLA Ops:
  3.3 21.2 %collective-permute-start.5 = (f32[1120,128]{1,0:T(8,128)S(1)}, f32[1120,128]{1,0:T(8,128)S(1)}, u32[]{:S(2)}, u32[]{:S(2)}) collective-permute-start(f32[1120,128]{1,0:T(8,128)S(1)} %get-tuple-element.25), channel_id=1, source_target_pairs={{0,16},{1,17},{2,18},{3,19},{4,20},{5,21},{6,22},{7,23},{8,24},{9,... | collective-permute-start | bytes 1720328 | tf_op jit(solution)/shard_map/ppermute | solution.py:725
  4.8 5.3 %collective-permute-start = (f32[160,128]{1,0:T(8,128)S(1)}, f32[160,128]{1,0:T(8,128)S(1)}, u32[]{:S(2)}, u32[]{:S(2)}) collective-permute-start(f32[160,128]{1,0:T(8,128)S(1)} %get-tuple-element.20), channel_id=1, source_target_pairs={{0,1},{1,2},{2,3},{3,0},{4,5},{5,6},{6,7},{7,4},{8,9},{9,10},{10,1... | collective-permute-start | bytes 245768 | tf_op jit(solution)/shard_map/ppermute | solution.py:725
  6.4 6.0 %collective-permute-start.1 = (f32[160,128]{1,0:T(8,128)S(1)}, f32[160,128]{1,0:T(8,128)S(1)}, u32[]{:S(2)}, u32[]{:S(2)}) collective-permute-start(f32[160,128]{1,0:T(8,128)S(1)} %get-tuple-element.21), channel_id=1, source_target_pairs={{0,19},{1,16},{2,17},{3,18},{4,23},{5,20},{6,21},{7,22},{8,27},{9,... | collective-permute-start | bytes 245768 | tf_op jit(solution)/shard_map/ppermute | solution.py:725
  6.4 6.0 %collective-permute-start.2 = (f32[160,128]{1,0:T(8,128)S(1)}, f32[160,128]{1,0:T(8,128)S(1)}, u32[]{:S(2)}, u32[]{:S(2)}) collective-permute-start(f32[160,128]{1,0:T(8,128)S(1)} %get-tuple-element.22), channel_id=1, source_target_pairs={{0,4},{1,5},{2,6},{3,7},{4,8},{5,9},{6,10},{7,11},{8,12},{9,13},{1... | collective-permute-start | bytes 245768 | tf_op jit(solution)/shard_map/ppermute | solution.py:725
  6.4 6.0 %collective-permute-start.3 = (f32[160,128]{1,0:T(8,128)S(1)}, f32[160,128]{1,0:T(8,128)S(1)}, u32[]{:S(2)}, u32[]{:S(2)}) collective-permute-start(f32[160,128]{1,0:T(8,128)S(1)} %get-tuple-element.23), channel_id=1, source_target_pairs={{0,12},{1,13},{2,14},{3,15},{4,0},{5,1},{6,2},{7,3},{8,4},{9,5},{1... | collective-permute-start | bytes 245768 | tf_op jit(solution)/shard_map/ppermute | solution.py:725
  12.7 21.6 %collective-permute-start.7 = (f32[504,128]{1,0:T(8,128)S(1)}, f32[504,128]{1,0:T(8,128)S(1)}, u32[]{:S(2)}, u32[]{:S(2)}) collective-permute-start(f32[504,128]{1,0:T(8,128)S(1)} %get-tuple-element.28), channel_id=1, source_target_pairs={{0,16},{1,17},{2,18},{3,19},{4,20},{5,21},{6,22},{7,23},{8,24},{9,... | collective-permute-start | bytes 774152 | tf_op jit(solution)/shard_map/ppermute | solution.py:725
  12.8 21.2 %collective-permute-start.4 = (f32[320,128]{1,0:T(8,128)S(1)}, f32[320,128]{1,0:T(8,128)S(1)}, u32[]{:S(2)}, u32[]{:S(2)}) collective-permute-start(f32[320,128]{1,0:T(8,128)S(1)} %get-tuple-element.24), channel_id=1, source_target_pairs={{0,1},{1,2},{2,3},{3,0},{4,5},{5,6},{6,7},{7,4},{8,9},{9,10},{10,1... | collective-permute-start | bytes 491528 | tf_op jit(solution)/shard_map/ppermute | solution.py:725
  15.0 19.3 %collective-permute-start.6 = (f32[320,128]{1,0:T(8,128)S(1)}, f32[320,128]{1,0:T(8,128)S(1)}, u32[]{:S(2)}, u32[]{:S(2)}) collective-permute-start(f32[320,128]{1,0:T(8,128)S(1)} %get-tuple-element.27), channel_id=1, source_target_pairs={{0,19},{1,16},{2,17},{3,18},{4,23},{5,20},{6,21},{7,22},{8,27},{9,... | collective-permute-start | bytes 491528 | tf_op jit(solution)/shard_map/ppermute | solution.py:725
  32.5 12.1 %collective-permute-start.9 = (f32[800,128]{1,0:T(8,128)S(1)}, f32[800,128]{1,0:T(8,128)S(1)}, u32[]{:S(2)}, u32[]{:S(2)}) collective-permute-start(f32[800,128]{1,0:T(8,128)S(1)} %get-tuple-element.31), channel_id=1, source_target_pairs={{16,0},{17,1},{18,2},{19,3},{20,4},{21,5},{22,6},{23,7},{24,8},{25... | collective-permute-start | bytes 1228808 | tf_op jit(solution)/shard_map/ppermute | solution.py:49
  41.0 8.1 %collective-permute-start.8 = (f32[480,128]{1,0:T(8,128)S(1)}, f32[480,128]{1,0:T(8,128)S(1)}, u32[]{:S(2)}, u32[]{:S(2)}) collective-permute-start(f32[480,128]{1,0:T(8,128)S(1)} %get-tuple-element.30), channel_id=1, source_target_pairs={{16,0},{17,1},{18,2},{19,3},{20,4},{21,5},{22,6},{23,7},{24,8},{25... | collective-permute-start | bytes 737288 | tf_op jit(solution)/shard_map/ppermute | solution.py:49

commit v10 on v8

--- a/solution.py
+++ b/solution.py
@@ -385,15 +385,15 @@
                 out[field, plane, row] = block
 
 
-def conduct_of(step):
-    return COND_EL + COND_LI * step
+def face_conduct(step):
+    return 0.5 * TAU_P * COND_EL + 0.5 * TAU_P * COND_LI * step
 
 
 def steps_kernel(part, near, other, halves, *refs):
     if part:
         other_rims, rest, _, *refs = refs
     result, message, natural, phase, phase_new, pot, pot_new, disp, disp_new = refs[:9]
-    slopes, slopes_y, cond_x, cond_y, cond_y_back, cond_z = refs[9:]
+    slopes, slopes_y, cond_x, cond_y, cond_z = refs[9:]
     _, slab, rows, _ = result.shape
     all_rows = 2 * rows
     planes = 2 * slab
@@ -484,26 +484,36 @@
     def down(block):
         return pltpu.roll(block, 1, 1)
 
-    push = 0.5 * TAU_U * STIFF * EIGEN
+    push = 0.5 * STIFF * EIGEN / SHEAR
 
     def conduct_pass(source):
+        known = {}
+
+        def step_at(plane, row):
+            if not isinstance(row, int):
+                return interp(source[plane, row])
+            if (plane, row) not in known:
+                known[plane, row] = interp(source[plane, row])
+            return known[plane, row]
+
         def body(row):
-            face = 0.5 * TAU_P
-            before = conduct_of(1.0)
+            before = face_conduct(1.0)
             for plane in range(planes):
-                step, ahead, back = (interp(source[plane, row + shift]) for shift in (0, 1, -1))
-                here = conduct_of(step)
+                step, ahead, back = (step_at(plane, row + shift) for shift in (0, 1, -1))
+                here = face_conduct(step)
                 yield [
                     (slopes, (plane,), push * step),
                     (slopes_y, (plane,), push * (ahead - back)),
-                    (cond_x, (plane,), face * (before + here)),
-                    (cond_y, (plane,), face * (here + conduct_of(ahead))),
-                    (cond_y_back, (plane,), face * (here + conduct_of(back))),
-                    (cond_z, (plane,), face * (here + up(here))),
+                    (cond_x, (plane,), before + here),
+                    (cond_y, (plane,), here + face_conduct(ahead)),
+                    (cond_z, (plane,), here + up(here)),
                 ]
                 before = here
-            yield [(cond_x, (planes,), face * (before + conduct_of(0.0)))]
-
+            yield [(cond_x, (planes,), before + face_conduct(0.0))]
+
+        for plane in range(planes):
+            first, second = (face_conduct(step_at(plane, row)) for row in (0, 1))
+            cond_y[plane, 0] = first + second
         return body
 
     def potential_pass(old, new, low):
@@ -515,7 +525,7 @@
                 after = old[plane + 1, row] if plane + 1 < planes else V_HIGH
                 leaving = cond_x[plane + 1, row] * (after - here)
                 along_y = cond_y[plane, row] * (old[plane, row + 1] - here)
-                along_y -= cond_y_back[plane, row] * (here - old[plane, row - 1])
+                along_y -= cond_y[plane, row - 1] * (here - old[plane, row - 1])
                 along_z = cond_z[plane, row] * (up(here) - here)
                 along_z -= down(along_z)
                 yield [(new, (plane,), here + ((leaving - entering) + along_y + along_z))]
@@ -524,9 +534,9 @@
         return body
 
     grad = LAME_FIRST + SHEAR
-    cross = 0.25 * TAU_U * grad
-    side_on = TAU_U * SHEAR
-    head_on = TAU_U * (SHEAR + grad)
+    cross = 0.25 * grad / SHEAR
+    head_on = 1.0 + grad / SHEAR
+    scale = TAU_U * SHEAR
     keep = 1.0 - TAU_U * (6.0 * SHEAR + 2.0 * grad)
 
     def elastic_pass(old, new, low):
@@ -547,30 +557,19 @@
                 (a, b, c), sums, diffs, slope = here
                 sum_x = [one + two for one, two in zip(after[0], before[0])]
                 lift = cross * (after[0][2] - before[0][2])
-                mid_a = side_on * a
-                new_a = (
-                    keep * a
-                    + head_on * sum_x[0]
-                    + side_on * sums[0]
-                    + (up(mid_a + lift) + down(mid_a - lift))
-                    + (after[3] - before[3])
-                )
+                force = (head_on * sum_x[0] + sums[0]) + (after[3] - before[3])
+                force += up(a + lift) + down(a - lift)
+                new_a = keep * a + scale * force
                 lift = cross * diffs[2]
-                mid_b = side_on * b
-                new_b = (
-                    keep * b
-                    + head_on * sums[1]
-                    + side_on * sum_x[1]
-                    + (up(mid_b + lift) + down(mid_b - lift))
-                    + (cross * (after[2][0] - before[2][0]) - slopes_y[plane, row])
-                )
+                force = cross * (after[2][0] - before[2][0]) - slopes_y[plane, row]
+                force += head_on * sums[1] + sum_x[1]
+                force += up(b + lift) + down(b - lift)
+                new_b = keep * b + scale * force
                 lift = cross * (after[0][0] - before[0][0]) + slope
                 mid_c = head_on * c
-                new_c = (
-                    keep * c
-                    + side_on * (sum_x[2] + sums[2])
-                    + (up(mid_c + lift) + down(mid_c - lift))
-                )
+                force = sum_x[2] + sums[2]
+                force += up(mid_c + lift) + down(mid_c - lift)
+                new_c = keep * c + scale * force
                 yield [(new, (part, plane), value) for part, value in enumerate((new_a, new_b, new_c))]
                 before, here = here, after
 
@@ -770,7 +769,7 @@
             [(FIELDS, slab, span, LANES)]
             + [deep] * 4
             + [(3,) + deep] * 2
-            + [deep, deep, (2 * slab + 1,) + deep[1:], deep, deep, deep],
+            + [deep, deep, (2 * slab + 1,) + deep[1:], deep, deep],
             in_specs=[in_vmem] * (3 + 2 * part) + [anywhere] * part,
             cost_estimate=pl.CostEstimate(
                 flops=STEPS * SWEEPS * 160 * span * 2 * slab * LANES,

time: 48.5 us -> 48 us (0.990)
  Pallas kernels: 20.3 us -> 19.8 us
    pallas_call x2, Pallas kernels: 14.8 us -> 14.2 us  [pair_shards(): call(functools.partial(steps_kernel, part), [(FIELDS, slab, rows // 2, LA...]
  transfers between devices with their start and end apart: 10 -> 10, of which waited for: 3 -> 3; matrix products, arithmetic and copies ran while one was open for 0% -> 0% of each run, Pallas kernels for 35% -> 34%
where the time goes in v10:
time: 48 us; the launch traced here: 47.8 us
  Pallas kernels  19.8 us (41%)
  starting transfers between devices  15.9 us (33%)
  waiting for transfers between devices  11.2 us (23%)
  between operations  0.89 us (2%)
    pallas_call x2, Pallas kernels, pair_shards(): call(functools.partial(steps_kernel, part), [(FIELDS, slab, rows // 2, LA...  14.2 us
    ppermute x8, starting transfers between devices, send(): return lax.ppermute(block, ('grow', 'cy', 'cz'), pairs)  13.1 us
    ppermute x2, waiting for transfers between devices, from_behind(): return lax.ppermute(block, axis, route)  8.14 us
    ppermute x8, waiting for transfers between devices, send(): return lax.ppermute(block, ('grow', 'cy', 'cz'), pairs)  3.07 us
    ppermute x2, starting transfers between devices, from_behind(): return lax.ppermute(block, axis, route)  2.76 us
    pallas_call x1, Pallas kernels, pair_shards(): call(prepare_kernel, [pltpu.VMEM(shape, jnp.float32) for shape in ((FIELD...  2.61 us
    pallas_call x2, Pallas kernels, pair_shards(): call(functools.partial(finish_kernel, part), [labels.shape, labels.shape,...  1.99 us
  transfers between devices with their start and end apart: 10, of which 3 were waited for; matrix products, arithmetic and copies ran while one was open for 0% of the time, Pallas kernels for 34%

profile of v10, /device:TPU:0, one launch (start us, length us, event | category | flops | bytes accessed | tf_op | source)
XLA Modules:
  0.0 47.8 jit_solution(3073605138135653999)
XLA Ops:
  0.6 2.6 %shard_map.67 = (f32[5,4,128,128]{3,2,1,0:T(8,128)S(1)}, f32[960,128]{1,0:T(8,128)S(1)}, f32[160,128]{1,0:T(8,128)S(1)}, f32[160,128]{1,0:T(8,128)S(1)}, f32[160,128]{1,0:T(8,128)S(1)}, /*index=5*/f32[160,128]{1,0:T(8,128)S(1)}) custom-call(s32[4,128,128]{2,1,0:T(8,128)} %labels.1, f32[4,128,128]{2,1,0:T(8,128)} %roughness.1, f32[4,128,128]{2,1,0:T(8,128)} %potential.1, ...), custom_call_target="tpu_custom_call" | custom-call | flops 1 | bytes 1 | tf_op jit(solution)/shard_map/pallas_call | solution.py:733
  3.2 3.0 %collective-permute-start.5 = (f32[960,128]{1,0:T(8,128)S(1)}, f32[960,128]{1,0:T(8,128)S(1)}, u32[]{:S(2)}, u32[]{:S(2)}) collective-permute-start(f32[960,128]{1,0:T(8,128)S(1)} %get-tuple-element.25), channel_id=1, source_target_pairs={{0,16},{1,17},{2,18},{3,19},{4,20},{5,21},{6,22},{7,23},{8,24},{9,... | collective-permute-start | bytes 1474568 | tf_op jit(solution)/shard_map/ppermute | solution.py:718
  6.3 1.6 %collective-permute-start = (f32[160,128]{1,0:T(8,128)S(1)}, f32[160,128]{1,0:T(8,128)S(1)}, u32[]{:S(2)}, u32[]{:S(2)}) collective-permute-start(f32[160,128]{1,0:T(8,128)S(1)} %get-tuple-element.20), channel_id=1, source_target_pairs={{0,1},{1,2},{2,3},{3,0},{4,5},{5,6},{6,7},{7,4},{8,9},{9,10},{10,1... | collective-permute-start | bytes 245768 | tf_op jit(solution)/shard_map/ppermute | solution.py:718
  7.8 2.4 %collective-permute-start.1 = (f32[160,128]{1,0:T(8,128)S(1)}, f32[160,128]{1,0:T(8,128)S(1)}, u32[]{:S(2)}, u32[]{:S(2)}) collective-permute-start(f32[160,128]{1,0:T(8,128)S(1)} %get-tuple-element.21), channel_id=1, source_target_pairs={{0,19},{1,16},{2,17},{3,18},{4,23},{5,20},{6,21},{7,22},{8,27},{9,... | collective-permute-start | bytes 245768 | tf_op jit(solution)/shard_map/ppermute | solution.py:718
  10.3 1.7 %collective-permute-start.3 = (f32[160,128]{1,0:T(8,128)S(1)}, f32[160,128]{1,0:T(8,128)S(1)}, u32[]{:S(2)}, u32[]{:S(2)}) collective-permute-start(f32[160,128]{1,0:T(8,128)S(1)} %get-tuple-element.23), channel_id=1, source_target_pairs={{0,12},{1,13},{2,14},{3,15},{4,0},{5,1},{6,2},{7,3},{8,4},{9,5},{1... | collective-permute-start | bytes 245768 | tf_op jit(solution)/shard_map/ppermute | solution.py:718
  12.0 1.0 %collective-permute-done.same_first.refs_0_ = f32[160,128]{1,0:T(8,128)S(1)} collective-permute-done((f32[160,128]{1,0:T(8,128)S(1)}, f32[160,128]{1,0:T(8,128)S(1)}, u32[]{:S(2)}, u32[]{:S(2)}) %collective-permute-start) | collective-permute-done | bytes 81952 | tf_op jit(solution)/shard_map/ppermute | solution.py:718
  13.0 2.1 %collective-permute-done.1.other_first.other = f32[160,128]{1,0:T(8,128)S(1)} collective-permute-done((f32[160,128]{1,0:T(8,128)S(1)}, f32[160,128]{1,0:T(8,128)S(1)}, u32[]{:S(2)}, u32[]{:S(2)}) %collective-permute-start.1) | collective-permute-done | bytes 81952 | tf_op jit(solution)/shard_map/ppermute | solution.py:718
  15.1 0.0 collective-permute-done.2.above.refs_2_
  15.1 0.0 collective-permute-done.3.below.refs_3_
  15.1 0.3 shard_map.68
  15.4 0.8 %collective-permute-start.7 = (f32[664,128]{1,0:T(8,128)S(1)}, f32[664,128]{1,0:T(8,128)S(1)}, u32[]{:S(2)}, u32[]{:S(2)}) collective-permute-start(f32[664,128]{1,0:T(8,128)S(1)} %get-tuple-element.28), channel_id=1, source_target_pairs={{0,16},{1,17},{2,18},{3,19},{4,20},{5,21},{6,22},{7,23},{8,24},{9,... | collective-permute-start | bytes 1019912 | tf_op jit(solution)/shard_map/ppermute | solution.py:718
  16.2 0.5 %collective-permute-start.4 = (f32[24,128]{1,0:T(8,128)S(1)}, f32[24,128]{1,0:T(8,128)S(1)}, u32[]{:S(2)}, u32[]{:S(2)}) collective-permute-start(f32[24,128]{1,0:T(8,128)S(1)} %get-tuple-element.24), channel_id=1, source_target_pairs={{0,1},{1,2},{2,3},{3,0},{4,5},{5,6},{6,7},{7,4},{8,9},{9,10},{10,1... | collective-permute-start | bytes 36872 | tf_op jit(solution)/shard_map/ppermute | solution.py:718
  16.7 3.1 %collective-permute-start.6 = (f32[24,128]{1,0:T(8,128)S(1)}, f32[24,128]{1,0:T(8,128)S(1)}, u32[]{:S(2)}, u32[]{:S(2)}) collective-permute-start(f32[24,128]{1,0:T(8,128)S(1)} %get-tuple-element.27), channel_id=1, source_target_pairs={{0,19},{1,16},{2,17},{3,18},{4,23},{5,20},{6,21},{7,22},{8,27},{9,... | collective-permute-start | bytes 36872 | tf_op jit(solution)/shard_map/ppermute | solution.py:718
  19.7 0.3 shard_map.69.near
  20.0 0.0 collective-permute-done.5.halves
  20.1 6.6 %shard_map.70 = (f32[5,4,64,128]{3,2,1,0:T(8,128)S(1)}, f32[640,128]{1,0:T(8,128)S(1)}) custom-call(f32[5,4,12,8,128]{4,3,2,1,0:T(8,128)S(1)} %shard_map.69.near, f32[160,128]{1,0:T(8,128)S(1)} %collective-permute-done.1.other_first.other, f32[960,128]{1,0:T(8,128)S(1)} %collective-permute-done.5.halves), custom_call_target="tpu_custom_call" | custom-call | flops 78643200 | bytes 19660800 | tf_op jit(solution)/shard_map/pallas_call | solution.py:766
  26.6 1.5 %collective-permute-start.9 = (f32[640,128]{1,0:T(8,128)S(1)}, f32[640,128]{1,0:T(8,128)S(1)}, u32[]{:S(2)}, u32[]{:S(2)}) collective-permute-start(f32[640,128]{1,0:T(8,128)S(1)} %get-tuple-element.31), channel_id=1, source_target_pairs={{16,0},{17,1},{18,2},{19,3},{20,4},{21,5},{22,6},{23,7},{24,8},{25... | collective-permute-start | bytes 983048 | tf_op jit(solution)/shard_map/ppermute | solution.py:49
  28.1 0.0 collective-permute-done.4.refs_1_
  28.1 0.4 shard_map.71.near
  28.5 7.6 %shard_map.72 = (f32[5,4,64,128]{3,2,1,0:T(8,128)S(1)}, f32[640,128]{1,0:T(8,128)S(1)}) custom-call(f32[5,4,14,8,128]{4,3,2,1,0:T(8,128)S(1)} %shard_map.71.near, f32[160,128]{1,0:T(8,128)S(1)} %collective-permute-done.1.other_first.other, f32[960,128]{1,0:T(8,128)S(1)} %collective-permute-done.5.halves, f32[24,128]{1,0:T(8,128)S(1)} %collective-permute-done.6.refs_0_, ...), custom_call_target="tpu_custom_call" | custom-call | flops 94371840 | bytes 23592960 | tf_op jit(solution)/shard_map/pallas_call | solution.py:766
  36.2 1.3 %collective-permute-start.8 = (f32[640,128]{1,0:T(8,128)S(1)}, f32[640,128]{1,0:T(8,128)S(1)}, u32[]{:S(2)}, u32[]{:S(2)}) collective-permute-start(f32[640,128]{1,0:T(8,128)S(1)} %get-tuple-element.30), channel_id=1, source_target_pairs={{16,0},{17,1},{18,2},{19,3},{20,4},{21,5},{22,6},{23,7},{24,8},{25... | collective-permute-start | bytes 983048 | tf_op jit(solution)/shard_map/ppermute | solution.py:49
  37.5 1.0 %shard_map.73 = (f32[4,128,128]{2,1,0:T(8,128)}, f32[4,128,128]{2,1,0:T(8,128)}, f32[3,4,128,128]{3,2,1,0:T(8,128)}) custom-call(f32[5,4,64,128]{3,2,1,0:T(8,128)S(1)} %get-tuple-element.26.refs_4_.refs_2_.result, f32[640,128]{1,0:T(8,128)S(1)} %collective-permute-done.9.message), custom_call_target="tpu_custom_call" | custom-call | flops 1 | bytes 1 | tf_op jit(solution)/shard_map/pallas_call | solution.py:783
  38.5 8.1 %collective-permute-done.8.message = f32[640,128]{1,0:T(8,128)S(1)} collective-permute-done((f32[640,128]{1,0:T(8,128)S(1)}, f32[640,128]{1,0:T(8,128)S(1)}, u32[]{:S(2)}, u32[]{:S(2)}) %collective-permute-start.8) | collective-permute-done | bytes 327712 | tf_op jit(solution)/shard_map/ppermute | solution.py:49
  46.6 1.0 %shard_map.74 = (f32[4,128,128]{2,1,0:T(8,128)}, f32[4,128,128]{2,1,0:T(8,128)}, f32[3,4,128,128]{3,2,1,0:T(8,128)}) custom-call(f32[5,4,64,128]{3,2,1,0:T(8,128)S(1)} %get-tuple-element.29.result, f32[640,128]{1,0:T(8,128)S(1)} %collective-permute-done.8.message, ...), custom_call_target="tpu_custom_call", output_to_operand_aliasing={{0}: (2, {}), {1}: (3, {}), {2}: (4, {})} | custom-call | flops 1 | bytes 1 | tf_op jit(solution)/shard_map/pallas_call | solution.py:783
  (4 shorter events, 0.0 us)
Async XLA Ops:
  3.2 16.8 %collective-permute-start.5 = (f32[960,128]{1,0:T(8,128)S(1)}, f32[960,128]{1,0:T(8,128)S(1)}, u32[]{:S(2)}, u32[]{:S(2)}) collective-permute-start(f32[960,128]{1,0:T(8,128)S(1)} %get-tuple-element.25), channel_id=1, source_target_pairs={{0,16},{1,17},{2,18},{3,19},{4,20},{5,21},{6,22},{7,23},{8,24},{9,... | collective-permute-start | bytes 1474568 | tf_op jit(solution)/shard_map/ppermute | solution.py:718
  6.3 6.7 %collective-permute-start = (f32[160,128]{1,0:T(8,128)S(1)}, f32[160,128]{1,0:T(8,128)S(1)}, u32[]{:S(2)}, u32[]{:S(2)}) collective-permute-start(f32[160,128]{1,0:T(8,128)S(1)} %get-tuple-element.20), channel_id=1, source_target_pairs={{0,1},{1,2},{2,3},{3,0},{4,5},{5,6},{6,7},{7,4},{8,9},{9,10},{10,1... | collective-permute-start | bytes 245768 | tf_op jit(solution)/shard_map/ppermute | solution.py:718
  7.8 7.2 %collective-permute-start.1 = (f32[160,128]{1,0:T(8,128)S(1)}, f32[160,128]{1,0:T(8,128)S(1)}, u32[]{:S(2)}, u32[]{:S(2)}) collective-permute-start(f32[160,128]{1,0:T(8,128)S(1)} %get-tuple-element.21), channel_id=1, source_target_pairs={{0,19},{1,16},{2,17},{3,18},{4,23},{5,20},{6,21},{7,22},{8,27},{9,... | collective-permute-start | bytes 245768 | tf_op jit(solution)/shard_map/ppermute | solution.py:718
  10.3 4.8 %collective-permute-start.2 = (f32[160,128]{1,0:T(8,128)S(1)}, f32[160,128]{1,0:T(8,128)S(1)}, u32[]{:S(2)}, u32[]{:S(2)}) collective-permute-start(f32[160,128]{1,0:T(8,128)S(1)} %get-tuple-element.22), channel_id=1, source_target_pairs={{0,4},{1,5},{2,6},{3,7},{4,8},{5,9},{6,10},{7,11},{8,12},{9,13},{1... | collective-permute-start | bytes 245768 | tf_op jit(solution)/shard_map/ppermute | solution.py:718
  10.3 4.8 %collective-permute-start.3 = (f32[160,128]{1,0:T(8,128)S(1)}, f32[160,128]{1,0:T(8,128)S(1)}, u32[]{:S(2)}, u32[]{:S(2)}) collective-permute-start(f32[160,128]{1,0:T(8,128)S(1)} %get-tuple-element.23), channel_id=1, source_target_pairs={{0,12},{1,13},{2,14},{3,15},{4,0},{5,1},{6,2},{7,3},{8,4},{9,5},{1... | collective-permute-start | bytes 245768 | tf_op jit(solution)/shard_map/ppermute | solution.py:718
  15.4 13.2 %collective-permute-start.7 = (f32[664,128]{1,0:T(8,128)S(1)}, f32[664,128]{1,0:T(8,128)S(1)}, u32[]{:S(2)}, u32[]{:S(2)}) collective-permute-start(f32[664,128]{1,0:T(8,128)S(1)} %get-tuple-element.28), channel_id=1, source_target_pairs={{0,16},{1,17},{2,18},{3,19},{4,20},{5,21},{6,22},{7,23},{8,24},{9,... | collective-permute-start | bytes 1019912 | tf_op jit(solution)/shard_map/ppermute | solution.py:718
  16.2 11.9 %collective-permute-start.4 = (f32[24,128]{1,0:T(8,128)S(1)}, f32[24,128]{1,0:T(8,128)S(1)}, u32[]{:S(2)}, u32[]{:S(2)}) collective-permute-start(f32[24,128]{1,0:T(8,128)S(1)} %get-tuple-element.24), channel_id=1, source_target_pairs={{0,1},{1,2},{2,3},{3,0},{4,5},{5,6},{6,7},{7,4},{8,9},{9,10},{10,1... | collective-permute-start | bytes 36872 | tf_op jit(solution)/shard_map/ppermute | solution.py:718
  16.7 11.9 %collective-permute-start.6 = (f32[24,128]{1,0:T(8,128)S(1)}, f32[24,128]{1,0:T(8,128)S(1)}, u32[]{:S(2)}, u32[]{:S(2)}) collective-permute-start(f32[24,128]{1,0:T(8,128)S(1)} %get-tuple-element.27), channel_id=1, source_target_pairs={{0,19},{1,16},{2,17},{3,18},{4,23},{5,20},{6,21},{7,22},{8,27},{9,... | collective-permute-start | bytes 36872 | tf_op jit(solution)/shard_map/ppermute | solution.py:718
  26.6 10.8 %collective-permute-start.9 = (f32[640,128]{1,0:T(8,128)S(1)}, f32[640,128]{1,0:T(8,128)S(1)}, u32[]{:S(2)}, u32[]{:S(2)}) collective-permute-start(f32[640,128]{1,0:T(8,128)S(1)} %get-tuple-element.31), channel_id=1, source_target_pairs={{16,0},{17,1},{18,2},{19,3},{20,4},{21,5},{22,6},{23,7},{24,8},{25... | collective-permute-start | bytes 983048 | tf_op jit(solution)/shard_map/ppermute | solution.py:49
  36.2 10.5 %collective-permute-start.8 = (f32[640,128]{1,0:T(8,128)S(1)}, f32[640,128]{1,0:T(8,128)S(1)}, u32[]{:S(2)}, u32[]{:S(2)}) collective-permute-start(f32[640,128]{1,0:T(8,128)S(1)} %get-tuple-element.30), channel_id=1, source_target_pairs={{16,0},{17,1},{18,2},{19,3},{20,4},{21,5},{22,6},{23,7},{24,8},{25... | collective-permute-start | bytes 983048 | tf_op jit(solution)/shard_map/ppermute | solution.py:49
